TPU v7x, 32 devices: a whole 2x2x4 slice. The times are simulated.
32 devices in a mesh: group: 2 (over x), patch: 8 (over z, y), expert: 2 (over core).
Axes of the slice: x: 2, y: 2, z: 4, core: 2. Of those that a mesh axis runs over, the one named last changes fastest.
Arguments:
- queries: bfloat16 [2048, 1792], P(('group', 'patch'), 'expert'), parts along dimension 0, may hold values from -8 to 8
- fresh_keys: bfloat16 [2048, 1792], P(('group', 'patch'), 'expert'), parts along dimension 0, may hold values from -6 to 6
- fresh_values: bfloat16 [2048, 1792], P(('group', 'patch'), 'expert'), parts along dimension 0, may hold values from -6 to 6
- stale_keys: bfloat16 [2048, 1792], P(('group', 'patch'), 'expert'), parts along dimension 0, may hold values from -8 to 8
- stale_values: bfloat16 [2048, 1792], P(('group', 'patch'), 'expert'), parts along dimension 0, may hold values from -6 to 6
- residual: bfloat16 [2048, 1792], P(('group', 'patch', 'expert')), parts along dimension 0, may hold values from -40 to 40
- out_weight: bfloat16 [1792, 1792], P('expert'), may hold values from -0.125 to 0.125
- modulation: float32 [4, 1792], P('group'), parts along dimension 0, may hold values from -3 to 3
- up_weight: bfloat16 [16, 1792, 3584], P(('patch', 'expert')), may hold values from -0.125 to 0.125
- down_weight: bfloat16 [16, 3584, 1792], P(('patch', 'expert')), may hold values from -0.09375 to 0.09375
- routes: int32 [2048, 2], P(('group', 'patch', 'expert')), parts along dimension 0, may hold values from 0 to 15, all different within a row; in each aligned block of 64 rows (0 to 63, 64 to 127, ...) at most 16 rows name the same one
- gates: float32 [2048, 2], P(('group', 'patch', 'expert')), parts along dimension 0, may hold values from 0.2 to 1
Outputs:
- mixed: bfloat16 [2048, 1792], P(('group', 'patch', 'expert')), parts along dimension 0
There are 2 independent parts, one for each index of `group`. A program takes and returns all parts, laid end to end along the dimension named above; an argument that names none is the same for every part. Nothing has to cross between parts.
Inputs may be any that keep to these rules, and one draw needn't show every extreme that they name: `routes`: each row names 2 different experts; within an aligned block of 64 rows (the rows of one device) no expert is named by more than 16 rows, and in some blocks one is named by exactly 16.
All inputs are finite; a program needn't handle non-finite values.
Results may differ from a plain program's by a relative error of at most 0.0045.
Values may be sent and summed in bfloat16 or wider, within the bound.
No kernel may reach another device: no remote copies, remote signals or barrier semaphores. Data moves between devices by JAX's collectives and lax.ppermute only.
A program may use at most 128 MiB of HBM per device.

v0:
```python
import math

import jax
import jax.numpy as jnp
from jax import lax
from jax.sharding import PartitionSpec as P

HEAD_DIM = 112
EXPERTS = 16
TOPK = 2


def split_heads(block_rows):
    return block_rows.reshape(block_rows.shape[0], block_rows.shape[1] // HEAD_DIM, HEAD_DIM)


def head_scores(query_heads, key_rows):
    products = jnp.einsum(
        "qhd,khd->qhk", query_heads, split_heads(key_rows), preferred_element_type=jnp.float32
    )
    return products * (1.0 / math.sqrt(HEAD_DIM))


def weighted_values(weights, value_rows):
    return jnp.einsum(
        "qhk,khd->qhd",
        weights.astype(jnp.bfloat16),
        split_heads(value_rows),
        preferred_element_type=jnp.float32,
    )


def fresh_partial(query_heads, fresh_keys, fresh_values):
    scores = head_scores(query_heads, fresh_keys)
    row_max = scores.max(-1)
    weights = jnp.exp(scores - row_max[..., None])
    return (row_max, weights.sum(-1), weighted_values(weights, fresh_values))


def attend_keys(queries, fresh_keys, fresh_values, stale_keys, stale_values):
    row_count = queries.shape[0]
    own_start = lax.axis_index("patch") * row_count
    query_heads = split_heads(queries)
    initial = fresh_partial(query_heads, fresh_keys, fresh_values)
    running_max, denominator, numerator = initial
    piece_keys = lax.all_gather(stale_keys, "patch", axis=0, tiled=True)
    piece_values = lax.all_gather(stale_values, "patch", axis=0, tiled=True)
    scores = head_scores(query_heads, piece_keys)
    positions = jnp.arange(piece_keys.shape[0], dtype=jnp.int32)
    own_rows = (positions >= own_start) & (positions < own_start + row_count)
    scores = jnp.where(own_rows[None, None, :], -1e30, scores)
    newest = jnp.maximum(running_max, scores.max(-1))
    rescale = jnp.exp(running_max - newest)
    weights = jnp.where(own_rows[None, None, :], 0.0, jnp.exp(scores - newest[..., None]))
    running_max, denominator, numerator = (
        newest,
        denominator * rescale + weights.sum(-1),
        numerator * rescale[..., None] + weighted_values(weights, piece_values),
    )
    return numerator / denominator[..., None]


def expert_slice(slots, up_weight, down_weight):
    leading = slots.shape[:-1]
    features = slots.shape[-1]
    inputs = slots.reshape(-1, features)
    hidden_units = jax.nn.gelu(
        jnp.dot(inputs, up_weight[0], preferred_element_type=jnp.float32), approximate=True
    ).astype(jnp.bfloat16)
    outputs = jnp.dot(hidden_units, down_weight[0], preferred_element_type=jnp.float32).astype(
        jnp.bfloat16
    )
    return outputs.reshape(leading + (features,))


def body(
    queries,
    fresh_keys,
    fresh_values,
    stale_keys,
    stale_values,
    residual,
    out_weight,
    modulation,
    up_weight,
    down_weight,
    routes,
    gates,
):
    heads_out = attend_keys(queries, fresh_keys, fresh_values, stale_keys, stale_values)
    attended = heads_out.reshape(queries.shape[0], queries.shape[1]).astype(jnp.bfloat16)
    local_rows = residual.shape[0]
    features = residual.shape[1]
    hidden_state = residual.astype(jnp.float32) + lax.psum_scatter(
        jnp.dot(attended, out_weight, preferred_element_type=jnp.float32).astype(jnp.bfloat16),
        "expert",
        scatter_dimension=0,
        tiled=True,
    ).astype(jnp.float32)
    row_mean = hidden_state.mean(-1, keepdims=True)
    centered = hidden_state - row_mean
    variance = (centered * centered).mean(-1, keepdims=True)
    normed = (centered / jnp.sqrt(variance + 1e-06) * (1.0 + modulation[1]) + modulation[0]).astype(
        jnp.bfloat16
    )
    capacity = local_rows // 4
    flat_routes = routes.reshape(-1)
    one_hot = (flat_routes[:, None] == jnp.arange(EXPERTS, dtype=jnp.int32)[None, :]).astype(
        jnp.int32
    )
    position = (jnp.cumsum(one_hot, axis=0) * one_hot).sum(-1) - 1
    slot_index = flat_routes * capacity + position
    assign = (
        slot_index[None, :] == jnp.arange(EXPERTS * capacity, dtype=jnp.int32)[:, None]
    ).astype(jnp.bfloat16)
    pair_rows = jnp.repeat(normed, TOPK, axis=0)
    buffer = jnp.dot(assign, pair_rows, preferred_element_type=jnp.float32).astype(jnp.bfloat16)
    patch_count = lax.axis_size("patch")
    core_count = lax.axis_size("expert")
    device_count = patch_count * core_count
    slice_count = device_count // EXPERTS
    outgoing = jnp.broadcast_to(
        buffer.reshape(EXPERTS, 1, capacity, features), (EXPERTS, slice_count, capacity, features)
    ).reshape(device_count, capacity, features)
    returned = lax.all_to_all(
        expert_slice(
            lax.all_to_all(outgoing, ("patch", "expert"), split_axis=0, concat_axis=0, tiled=True),
            up_weight,
            down_weight,
        ),
        ("patch", "expert"),
        split_axis=0,
        concat_axis=0,
        tiled=True,
    )
    expert_out = (
        returned.reshape(EXPERTS, slice_count, capacity, features)
        .astype(jnp.float32)
        .sum(1)
        .reshape(EXPERTS * capacity, features)
    )
    picked = jnp.take(expert_out, slot_index, axis=0).reshape(local_rows, TOPK, features)
    mixed = hidden_state + (picked * gates[..., None]).sum(1)
    return mixed.astype(jnp.bfloat16)


def solution(mesh):
    placed = (
        P(("group", "patch"), "expert"),
        P(("group", "patch"), "expert"),
        P(("group", "patch"), "expert"),
        P(("group", "patch"), "expert"),
        P(("group", "patch"), "expert"),
        P(("group", "patch", "expert"), None),
        P("expert", None),
        P("group", None),
        P(("patch", "expert"), None, None),
        P(("patch", "expert"), None, None),
        P(("group", "patch", "expert"), None),
        P(("group", "patch", "expert"), None),
    )
    return jax.shard_map(
        body,
        mesh=mesh,
        in_specs=placed,
        out_specs=P(("group", "patch", "expert"), None),
        check_vma=False,
    )
```

profile of v0, /device:TPU:1, one launch (start us, length us, event | category | flops | bytes accessed | tf_op | source)
XLA Modules:
  0.0 221.1 jit_solution(5357750498133696452)
XLA Ops:
  6.5 0.0 copy-start
  6.5 0.0 all-gather.3.cloned.1.call-start
  6.5 0.7 all-gather.3.cloned.1.call-update
  7.3 0.0 all-gather.5.cloned.1.call-start
  7.3 0.7 all-gather.5.cloned.1.call-update
  8.0 0.0 reduce-scatter.2.cloned.1.call-start
  8.1 1.1 copy.35
  9.2 1.8 copy.34
  10.9 1.8 copy.36
  12.7 1.2 fusion.53
  13.9 0.0 copy-start.3
  14.0 0.8 copy-done.3
  14.8 0.1 fusion.37
  14.8 42.0 %all-gather.3.cloned.1.call-done = bf16[1024,896]{1,0:T(8,128)(2,1)} async-done(((bf16[128,896]{1,0:T(8,128)(2,1)}), bf16[1024,896]{1,0:T(8,128)(2,1)}) %all-gather.3.cloned.1.call-update) | async-done | bytes 1835024 | tf_op jit(solution)/shard_map/all_gather | solution.py:46
  56.9 3.8 %copy.38 = bf16[1024,896]{0,1:T(8,128)(2,1)} copy(bf16[1024,896]{1,0:T(8,128)(2,1)} %all-gather.3.cloned.1.call-done) | data formatting | bytes 3670016 | tf_op jit(solution)/shard_map/all_gather | solution.py:46
  60.7 2.8 %bitcast_reduce_fusion = (f32[128,8]{0,1:T(8,128)S(1)}, f32[8,1024,128]{2,1,0:T(8,128)S(1)}) fusion(pred[1024]{0:T(1024)(128)(4,1)S(1)} %fusion.44, bf16[1024,8,112]{0,2,1:T(8,128)(2,1)} %bitcast.70, bf16[128,8,112]{0,2,1:T(8,128)(2,1)S(1)} %bitcast.73), kind=kOutput, calls=%fused_computation.7 | convolution fusion | flops 238025728 | bytes 6263808 | tf_op jit(solution)/shard_map/qhd,khd->qhk/dot_general | solution.py:18
  63.5 0.0 copy-start.1
  63.5 1.9 copy-done.1
  65.4 1.4 fusion.18
  66.8 37.5 %all-gather.5.cloned.1.call-done = bf16[1024,896]{1,0:T(8,128)(2,1)} async-done(((bf16[128,896]{1,0:T(8,128)(2,1)}), bf16[1024,896]{1,0:T(8,128)(2,1)}) %all-gather.5.cloned.1.call-update) | async-done | bytes 1835024 | tf_op jit(solution)/shard_map/all_gather | solution.py:47
  104.4 3.8 %copy.39 = bf16[1024,896]{0,1:T(8,128)(2,1)} copy(bf16[1024,896]{1,0:T(8,128)(2,1)} %all-gather.5.cloned.1.call-done) | data formatting | bytes 3670016 | tf_op jit(solution)/shard_map/all_gather | solution.py:47
  108.2 0.0 copy-start.4
  108.2 0.0 copy-start.5
  108.2 4.4 %fusion.28 = f32[128,8,112]{0,2,1:T(8,128)S(1)} fusion(bf16[1024,8,112]{0,2,1:T(8,128)(2,1)} %bitcast.74, f32[8,1024,128]{2,1,0:T(8,128)} %copy-done.1, f32[128,8]{0,1:T(8,128)S(1)} %max.13, pred[1024]{0:T(1024)(128)(4,1)S(1)} %fusion.44), kind=kOutput, calls=%fused_computation.29 | convolution fusion | flops 240123904 | bytes 6493184 | tf_op jit(solution)/shard_map/qhk,khd->qhd/dot_general | solution.py:25
  112.6 0.0 copy-start.7
  112.6 0.0 copy-start.6
  112.6 0.0 copy-start.2
  112.6 0.0 copy-done.4
  112.6 0.0 copy-done.5
  112.6 0.3 fusion.34
  112.9 0.0 copy-done
  112.9 1.4 convolution_convert_fusion.1
  114.4 0.0 reduce-scatter.2.cloned.1.call-update
  114.4 0.0 copy-done.7
  114.4 0.1 copy.41
  114.5 0.1 reshape.146
  114.7 0.7 fusion.43
  115.4 1.0 reduce_window_sum.11
  116.4 0.0 copy-done.6
  116.4 0.2 select_reduce_fusion
  116.6 6.2 %reduce-scatter.2.cloned.1.call-done = bf16[64,1792]{1,0:T(8,128)(2,1)} async-done(((bf16[128,1792]{1,0:T(8,128)(2,1)}), bf16[64,1792]{1,0:T(8,128)(2,1)}) %reduce-scatter.2.cloned.1.call-update) | async-done | bytes 229392 | tf_op jit(solution)/shard_map/reduce_scatter | solution.py:94
  122.8 0.0 copy-done.2
  122.8 1.1 fusion.39
  123.9 1.2 multiply_reduce_fusion.1
  125.1 1.1 add_convert_fusion.1
  126.2 1.0 broadcast_in_dim.51
  127.2 2.0 reshape.147
  129.2 1.4 convolution_convert_fusion
  130.6 28.9 %all_to_all.10 = bf16[16,16,1792]{2,1,0:T(8,128)(2,1)} all-to-all(bf16[16,16,1792]{2,1,0:T(8,128)(2,1)S(1)} %bitcast.71), channel_id=1, replica_groups=mesh['group'=2,'patch'=8,'expert'=2] {'patch','expert'}, dimensions={0} | all-to-all | bytes 1835008 | tf_op jit(solution)/shard_map/all_to_all | solution.py:127
  159.5 16.5 %fusion.20 = bf16[256,1792]{1,0:T(8,128)(2,1)} fusion(bf16[1,3584,1792]{2,1,0:T(8,128)(2,1)} %param.21, bf16[256,1792]{1,0:T(8,128)(2,1)} %bitcast.76, bf16[1,1792,3584]{2,1,0:T(8,128)(2,1)} %param.20), kind=kOutput, calls=%fused_computation.21 | convolution fusion | flops 6585384960 | bytes 27525120 | tf_op jit(solution)/shard_map/dot_general | solution.py:70
  176.0 4.2 %all-to-all-start.1 = ((bf16[16,16,1792]{2,1,0:T(8,128)(2,1)}), bf16[16,16,1792]{2,1,0:T(8,128)(2,1)}, u32[]{:S(2)}, u32[]{:S(2)}) async-start(bf16[16,16,1792]{2,1,0:T(8,128)(2,1)} %bitcast.75), calls=%async_computation.2 | async-start | bytes 1835008 | tf_op jit(solution)/shard_map/all_to_all | solution.py:125
  180.2 0.1 copy.44
  180.3 0.1 mul.131
  180.5 0.1 sub.48
  180.6 0.1 copy.42
  180.7 0.1 copy.43
  180.8 0.0 copy-done.8
  180.8 0.1 copy.45
  180.9 20.1 %all-to-all-done.1 = bf16[16,16,1792]{2,1,0:T(8,128)(2,1)} async-done(((bf16[16,16,1792]{2,1,0:T(8,128)(2,1)}), bf16[16,16,1792]{2,1,0:T(8,128)(2,1)}, u32[]{:S(2)}, u32[]{:S(2)}) %all-to-all-start.1) | async-done | bytes 917536 | tf_op jit(solution)/shard_map/all_to_all | solution.py:125
  201.1 2.6 %bitcast_convert_fusion = f32[256,1792]{1,0:T(8,128)} fusion(bf16[16,16,1792]{2,1,0:T(8,128)(2,1)} %all-to-all-done.1), kind=kLoop, calls=%fused_computation.35 | loop fusion | flops 458752 | bytes 2752512 | tf_op jit(solution)/shard_map/reshape | solution.py:140
  203.6 3.7 %gather_fusion = f32[128,1792]{1,0:T(8,128)} fusion(f32[256,1792]{1,0:T(8,128)} %bitcast_convert_fusion, s32[1024]{0:T(1024)S(1)} %pad_clamp_fusion), kind=kCustom, calls=%fused_computation | custom fusion | bytes 1835520 | tf_op jit(solution)/shard_map/jit(_take)/gather | solution.py:142
  207.4 2.6 %gather.7 = f32[64,2,1792]{2,1,0:T(2,128)} reshape(f32[128,1792]{1,0:T(8,128)} %gather_fusion) | data formatting | bytes 1835008 | tf_op jit(solution)/shard_map/jit(_take)/gather | solution.py:142
  210.0 2.9 %multiply_reduce_fusion = f32[64,1792]{1,0:T(8,128)S(1)} fusion(f32[64,2,1792]{2,1,0:T(2,128)} %gather.7, pred[64,2]{1,0:T(8,128)(4,1)S(1)} %copy.43, f32[64,2]{1,0:T(8,128)S(1)} %copy.45), kind=kLoop, calls=%fused_computation.36 | loop fusion | flops 573440 | bytes 1376896 | tf_op jit(solution)/shard_map/reduce_sum | solution.py:143
  212.9 1.7 add_convert_fusion
  (12 shorter events, 0.1 us)
Async XLA Ops:
  6.5 106.4 %copy-start = (bf16[896,1792]{1,0:T(8,128)(2,1)S(1)}, bf16[896,1792]{1,0:T(8,128)(2,1)}, u32[]{:S(2)}) copy-start(bf16[896,1792]{1,0:T(8,128)(2,1)} %param.18) | copy-start | bytes 9633796
  6.5 50.3 %all-gather.3.cloned.1.call-start = ((), (), s32[]{:S(2)}) async-start(), calls=%async_computation.3 | async-start | bytes 2064384 | tf_op jit(solution)/shard_map/all_gather | solution.py:46
  7.3 97.1 %all-gather.5.cloned.1.call-start = ((), (), s32[]{:S(2)}) async-start(), calls=%async_computation.4 | async-start | bytes 2064384 | tf_op jit(solution)/shard_map/all_gather | solution.py:47
  8.0 114.8 %reduce-scatter.2.cloned.1.call-start = ((), (), s32[]{:S(2)}) async-start(), calls=%async_computation.5 | async-start | bytes 688128 | tf_op jit(solution)/shard_map/reduce_scatter | solution.py:94
  13.9 0.8 copy-start.3
  63.5 1.9 copy-start.1
  108.2 4.4 %copy-start.4 = (f32[128,8,128]{0,2,1:T(8,128)S(1)}, f32[128,8,128]{0,2,1:T(8,128)}, u32[]{:S(2)}) copy-start(f32[128,8,128]{0,2,1:T(8,128)} %copy-done.3) | copy-start | bytes 1572868
  108.2 4.4 %copy-start.5 = (bf16[128,896]{0,1:T(8,128)(2,1)S(1)}, bf16[128,896]{0,1:T(8,128)(2,1)}, u32[]{:S(2)}) copy-start(bf16[128,896]{0,1:T(8,128)(2,1)} %copy.36) | copy-start | bytes 688132
  112.6 1.9 copy-start.7
  112.6 3.8 %copy-start.6 = (f32[2,1792]{1,0:T(2,128)S(1)}, f32[2,1792]{1,0:T(2,128)}, u32[]{:S(2)}) copy-start(f32[2,1792]{1,0:T(2,128)} %param.19) | copy-start | bytes 43012
  112.6 10.2 %copy-start.2 = (bf16[64,1792]{1,0:T(8,128)(2,1)S(1)}, bf16[64,1792]{1,0:T(8,128)(2,1)}, u32[]{:S(2)}) copy-start(bf16[64,1792]{1,0:T(8,128)(2,1)} %param.17) | copy-start | bytes 688132
  159.5 21.3 %copy-start.8 = (f32[64,2]{0,1:T(2,128)S(1)}, f32[64,2]{0,1:T(2,128)}, u32[]{:S(2)}) copy-start(f32[64,2]{0,1:T(2,128)} %param.23) | copy-start | bytes 1540
  176.0 25.1 %all-to-all-start.1 = ((bf16[16,16,1792]{2,1,0:T(8,128)(2,1)}), bf16[16,16,1792]{2,1,0:T(8,128)(2,1)}, u32[]{:S(2)}, u32[]{:S(2)}) async-start(bf16[16,16,1792]{2,1,0:T(8,128)(2,1)} %bitcast.75), calls=%async_computation.2 | async-start | bytes 1835008 | tf_op jit(solution)/shard_map/all_to_all | solution.py:125
Sparse Core Ops, SparseCore 0:
  9.5 47.2 all-gather.2
  59.0 45.2 all-gather.4
  114.5 8.2 reduce-scatter.1
where the time goes:
time: 223 us; the launch traced here: 221 us
  waiting for transfers between devices  107 us (48%)
  blocking collectives  28.9 us (13%)
  matrix products  28 us (13%)
  local copies, waits for them, and re-layouts  25.3 us (11%)
  other arithmetic  14 us (6%)
  between operations  13.4 us (6%)
  starting transfers between devices  4.29 us (2%)
    all_gather x1, waiting for transfers between devices, attend_keys(): piece_keys = lax.all_gather(stale_keys, 'patch', axis=0, tiled=True)  42 us
    all_gather x1, waiting for transfers between devices, attend_keys(): piece_values = lax.all_gather(stale_values, 'patch', axis=0, tiled=True)  37.5 us
    all_to_all x1, blocking collectives, body(): lax.all_to_all(outgoing, ('patch', 'expert'), split_axis=0, concat_axis=0...  28.9 us
    all_to_all x1, waiting for transfers between devices, body(): lax.all_to_all(expert_slice(lax.all_to_all(outgoing, ('patch', 'expert'),...  20.1 us
    dot_general x1, matrix products, expert_slice(): jnp.dot(hidden_units, down_weight[0], preferred_element_type=jnp.float32)  16.5 us
    unnamed x23, local copies, waits for them, and re-layouts  7.57 us
    gather x2, local copies, waits for them, and re-layouts, body(): jnp.take(expert_out, slot_index, axis=0).reshape(local_rows, TOPK, features)  6.38 us
    reduce_scatter x1, waiting for transfers between devices, body(): lax.psum_scatter(jnp.dot(attended, out_weight, preferred_element_type=jnp...  6.2 us
  transfers between devices with their start and end apart: 4, of which 4 were waited for; matrix products, arithmetic and copies ran while one was open for 8% of the time, Pallas kernels for 0%

commit v1 on v0

v1 whole, which is shorter than its diff:
```python
import functools
import math

import jax
import jax.numpy as jnp
from jax import lax
from jax.experimental import pallas as pl
from jax.experimental.pallas import tpu as pltpu
from jax.sharding import PartitionSpec as P

HEAD_DIM = 112
EXPERTS = 16
TOPK = 2
LANES = 128
SCALE = 1.0 / math.sqrt(HEAD_DIM)
BF16 = jnp.bfloat16
F32 = jnp.float32
VMEM = pl.BlockSpec(memory_space=pltpu.VMEM)
SMEM = pl.BlockSpec(memory_space=pltpu.SMEM)


def contract(a, b, dim_a, dim_b):
    return lax.dot_general(a, b, (((dim_a,), (dim_b,)), ((), ())), preferred_element_type=F32)


def pack_kernel(q_ref, k_ref, v_ref, out_ref):
    for i, ref in enumerate((q_ref, k_ref, v_ref)):
        turned = ref[...].T
        for h in range(out_ref.shape[0]):
            out_ref[h, i * HEAD_DIM : (i + 1) * HEAD_DIM, :] = turned[
                h * HEAD_DIM : (h + 1) * HEAD_DIM
            ]


def with_ones(values):
    return jnp.concatenate([values, jnp.ones((LANES - HEAD_DIM, values.shape[1]), BF16)], axis=0)


def partial_softmax(query, keys, values):
    scores = contract(query, keys, 0, 0)
    top = scores.max(-1, keepdims=True)
    weights = jnp.exp((scores - top) * SCALE).astype(BF16)
    return contract(weights, with_ones(values), 1, 1), top * SCALE


def fresh_kernel(core_ref, q_ref, k_ref, v_ref, own_ref, other_ref):
    q, k, v = q_ref[...].T, k_ref[...].T, v_ref[...].T
    half = q.shape[1] // 2
    first = core_ref[0] == 0
    lane = lax.broadcasted_iota(jnp.int32, (2 * half, LANES), 1)
    for h in range(q.shape[0] // HEAD_DIM):
        rows = slice(h * HEAD_DIM, (h + 1) * HEAD_DIM)
        sums, top = partial_softmax(q[rows], k[rows], v[rows])
        sums = jnp.where(lane == HEAD_DIM + 1, top, sums)
        lanes = slice(h * LANES, (h + 1) * LANES)
        own_ref[:, lanes] = jnp.where(first, sums[:half], sums[half:])
        other_ref[:, lanes] = jnp.where(first, sums[half:], sums[:half])


def attend_kernel(in_ref, out_ref):
    patches, tokens = in_ref.shape[0], in_ref.shape[2]
    half = tokens // 2
    lane = lax.broadcasted_iota(jnp.int32, (tokens, LANES), 1)
    for p in range(patches):
        others = [j for j in range(patches) if j != p]
        keys = jnp.concatenate([in_ref[j, HEAD_DIM : 2 * HEAD_DIM] for j in others], axis=1)
        values = jnp.concatenate([in_ref[j, 2 * HEAD_DIM :] for j in others], axis=1)
        sums, top = partial_softmax(in_ref[p, :HEAD_DIM], keys, values)
        total = sums[:, HEAD_DIM : HEAD_DIM + 1]
        log_total = top + jnp.log(total)
        high = log_total.astype(BF16).astype(F32)
        rest = log_total - high
        middle = rest.astype(BF16).astype(F32)
        result = sums / total
        result = jnp.where(lane == HEAD_DIM, high, result)
        result = jnp.where(lane == HEAD_DIM + 1, middle, result)
        result = jnp.where(lane == HEAD_DIM + 2, rest - middle, result)
        result = result.astype(BF16)
        out_ref[2 * p] = result[:half]
        out_ref[2 * p + 1] = result[half:]


def slots_of(routes, capacity):
    rows = routes.shape[0]
    expert = lax.broadcasted_iota(jnp.int32, (rows, EXPERTS), 1)
    names = [expert == routes[:, k : k + 1] for k in range(TOPK)]
    named = sum(n.astype(F32) for n in names).astype(BF16)
    earlier = (
        lax.broadcasted_iota(jnp.int32, (rows, rows), 1)
        < lax.broadcasted_iota(jnp.int32, (rows, rows), 0)
    ).astype(F32).astype(BF16)
    count = jnp.dot(earlier, named, preferred_element_type=F32)
    return [
        routes[:, k : k + 1] * capacity
        + jnp.where(names[k], count, 0.0).sum(-1, keepdims=True).astype(jnp.int32)
        for k in range(TOPK)
    ]


def chosen(slot, slots):
    return (
        (lax.broadcasted_iota(jnp.int32, (slot.shape[0], slots), 1) == slot).astype(F32).astype(BF16)
    )


def home_kernel(
    core_ref, far_ref, own_ref, other_ref, w_own_ref, w_other_ref, residual_ref, modulation_ref,
    routes_ref, hidden_ref, buffer_ref, attended_ref,
):
    heads = far_ref.shape[0]
    core = core_ref[0]
    projected = None
    for side, (near_ref, w_ref) in enumerate(((own_ref, w_own_ref), (other_ref, w_other_ref))):
        which = core if side == 0 else 1 - core
        for h in range(heads):
            far = far_ref[h, which].astype(F32)
            near = near_ref[:, h * LANES : (h + 1) * LANES]
            far_log = (
                far[:, HEAD_DIM : HEAD_DIM + 1]
                + far[:, HEAD_DIM + 1 : HEAD_DIM + 2]
                + far[:, HEAD_DIM + 2 : HEAD_DIM + 3]
            )
            near_total = near[:, HEAD_DIM : HEAD_DIM + 1]
            near_top = near[:, HEAD_DIM + 1 : HEAD_DIM + 2]
            top = jnp.maximum(far_log, near_top)
            far_weight = jnp.exp(far_log - top)
            near_weight = jnp.exp(near_top - top)
            scale = 1.0 / (far_weight + near_total * near_weight)
            merged = far * (far_weight * scale) + near * (near_weight * scale)
            attended_ref[side, :, h * HEAD_DIM : (h + 1) * HEAD_DIM] = merged[:, :HEAD_DIM].astype(BF16)
        part = jnp.dot(attended_ref[side], w_ref[...], preferred_element_type=F32)
        projected = part if projected is None else projected + part
    hidden = residual_ref[...].astype(F32) + projected
    hidden_ref[...] = hidden
    centered = hidden - hidden.mean(-1, keepdims=True)
    variance = (centered * centered).mean(-1, keepdims=True)
    normed = (
        centered / jnp.sqrt(variance + 1e-06) * (1.0 + modulation_ref[1:2]) + modulation_ref[0:1]
    ).astype(BF16)
    slots = buffer_ref.shape[0]
    picks = [chosen(slot, slots) for slot in slots_of(routes_ref[...], slots // EXPERTS)]
    buffer_ref[...] = contract(picks[0] + picks[1], normed, 0, 0).astype(BF16)


def attention_by_heads(queries, fresh_keys, fresh_values, stale_keys, stale_values, out_weight, residual, modulation, routes):
    tokens, width = queries.shape
    heads = width // HEAD_DIM
    rows, features = residual.shape
    core = lax.axis_index("expert").astype(jnp.int32).reshape(1)
    swap = [(0, 1), (1, 0)]
    packed = pl.pallas_call(
        pack_kernel,
        out_shape=jax.ShapeDtypeStruct((heads, 3 * HEAD_DIM, tokens), BF16),
        in_specs=[VMEM] * 3,
        out_specs=VMEM,
        name="pack",
    )(queries, stale_keys, stale_values)
    w_other = lax.ppermute(out_weight, "expert", swap)
    gathered = lax.all_to_all(packed, "patch", split_axis=0, concat_axis=0, tiled=True)
    fresh_shape = jax.ShapeDtypeStruct((tokens // 2, heads * LANES), F32)
    fresh_own, fresh_away = pl.pallas_call(
        fresh_kernel,
        out_shape=(fresh_shape, fresh_shape),
        in_specs=[SMEM] + [VMEM] * 3,
        out_specs=(VMEM, VMEM),
        cost_estimate=pl.CostEstimate(flops=60_000_000, bytes_accessed=2_000_000, transcendentals=200_000),
        name="fresh",
    )(core, queries, fresh_keys, fresh_values)
    fresh_other = lax.ppermute(fresh_away, "expert", swap)
    stale = pl.pallas_call(
        attend_kernel,
        out_shape=jax.ShapeDtypeStruct((2 * heads, tokens // 2, LANES), BF16),
        in_specs=[VMEM],
        out_specs=VMEM,
        compiler_params=pltpu.CompilerParams(vmem_limit_bytes=32 << 20),
        name="attend",
    )(gathered)
    far = lax.all_to_all(stale, ("patch", "expert"), split_axis=0, concat_axis=0, tiled=True)
    return pl.pallas_call(
        home_kernel,
        out_shape=(
            jax.ShapeDtypeStruct((rows, features), F32),
            jax.ShapeDtypeStruct((EXPERTS * (rows // 4), features), BF16),
        ),
        in_specs=[SMEM] + [VMEM] * 8,
        out_specs=(VMEM, VMEM),
        scratch_shapes=[pltpu.VMEM((2, rows, width), BF16)],
        compiler_params=pltpu.CompilerParams(vmem_limit_bytes=40 << 20),
        name="home",
    )(core, far.reshape(heads, 2, rows, LANES), fresh_own, fresh_other, out_weight, w_other, residual, modulation, routes)


def split_heads(block_rows):
    return block_rows.reshape(block_rows.shape[0], block_rows.shape[1] // HEAD_DIM, HEAD_DIM)


def head_scores(query_heads, key_rows):
    products = jnp.einsum("qhd,khd->qhk", query_heads, split_heads(key_rows), preferred_element_type=F32)
    return products * SCALE


def weighted_values(weights, value_rows):
    return jnp.einsum(
        "qhk,khd->qhd", weights.astype(BF16), split_heads(value_rows), preferred_element_type=F32
    )


def attention_by_gather(queries, fresh_keys, fresh_values, stale_keys, stale_values, out_weight, residual, modulation, routes):
    row_count = queries.shape[0]
    own_start = lax.axis_index("patch") * row_count
    query_heads = split_heads(queries)
    scores = head_scores(query_heads, fresh_keys)
    running_max = scores.max(-1)
    weights = jnp.exp(scores - running_max[..., None])
    denominator, numerator = weights.sum(-1), weighted_values(weights, fresh_values)
    piece_keys = lax.all_gather(stale_keys, "patch", axis=0, tiled=True)
    piece_values = lax.all_gather(stale_values, "patch", axis=0, tiled=True)
    scores = head_scores(query_heads, piece_keys)
    positions = jnp.arange(piece_keys.shape[0], dtype=jnp.int32)
    own_rows = (positions >= own_start) & (positions < own_start + row_count)
    scores = jnp.where(own_rows[None, None, :], -1e30, scores)
    newest = jnp.maximum(running_max, scores.max(-1))
    rescale = jnp.exp(running_max - newest)
    weights = jnp.where(own_rows[None, None, :], 0.0, jnp.exp(scores - newest[..., None]))
    denominator = denominator * rescale + weights.sum(-1)
    numerator = numerator * rescale[..., None] + weighted_values(weights, piece_values)
    attended = (numerator / denominator[..., None]).reshape(queries.shape).astype(BF16)
    hidden = residual.astype(F32) + lax.psum_scatter(
        jnp.dot(attended, out_weight, preferred_element_type=F32).astype(BF16),
        "expert",
        scatter_dimension=0,
        tiled=True,
    ).astype(F32)
    centered = hidden - hidden.mean(-1, keepdims=True)
    variance = (centered * centered).mean(-1, keepdims=True)
    normed = (centered / jnp.sqrt(variance + 1e-06) * (1.0 + modulation[1]) + modulation[0]).astype(BF16)
    capacity = residual.shape[0] // 4
    picks = [chosen(slot, EXPERTS * capacity) for slot in slots_of(routes, capacity)]
    return hidden, contract(picks[0] + picks[1], normed, 0, 0).astype(BF16)


def expert_kernel(x_ref, up_ref, down_ref, out_ref, total_ref):
    step = pl.program_id(0)
    units = jax.nn.gelu(
        jnp.dot(x_ref[...], up_ref[0], preferred_element_type=F32), approximate=True
    ).astype(BF16)
    part = jnp.dot(units, down_ref[0], preferred_element_type=F32)

    @pl.when(step == 0)
    def _():
        total_ref[...] = part

    @pl.when(step > 0)
    def _():
        total_ref[...] += part

    @pl.when(step == pl.num_programs(0) - 1)
    def _():
        out_ref[...] = total_ref[...].astype(BF16)


def expert_slice(inputs, up_weight, down_weight):
    rows, features = inputs.shape
    units = up_weight.shape[2]
    chunk = next(c for c in (512, 256, 128) if units % c == 0)
    return pl.pallas_call(
        expert_kernel,
        grid=(units // chunk,),
        out_shape=jax.ShapeDtypeStruct((rows, features), BF16),
        in_specs=[
            pl.BlockSpec((rows, features), lambda j: (0, 0)),
            pl.BlockSpec((1, features, chunk), lambda j: (0, 0, j)),
            pl.BlockSpec((1, chunk, features), lambda j: (0, j, 0)),
        ],
        out_specs=pl.BlockSpec((rows, features), lambda j: (0, 0)),
        scratch_shapes=[pltpu.VMEM((rows, features), F32)],
        compiler_params=pltpu.CompilerParams(vmem_limit_bytes=40 << 20),
        name="experts",
    )(inputs, up_weight, down_weight)


def combine_kernel(hidden_ref, routes_ref, gates_ref, returned_ref, out_ref):
    slices = returned_ref.shape[1]
    slots = returned_ref.shape[0] * returned_ref.shape[2]
    mixed = hidden_ref[...]
    picks = [chosen(slot, slots) for slot in slots_of(routes_ref[...], slots // EXPERTS)]
    for s in range(slices):
        rows = returned_ref[:, s].reshape(slots, returned_ref.shape[3])
        for k in range(TOPK):
            mixed += gates_ref[:, k : k + 1] * jnp.dot(picks[k], rows, preferred_element_type=F32)
    out_ref[...] = mixed.astype(BF16)


def body(
    queries, fresh_keys, fresh_values, stale_keys, stale_values, residual, out_weight, modulation,
    up_weight, down_weight, routes, gates,
):
    rows, features = residual.shape
    patch_count = lax.axis_size("patch")
    device_count = patch_count * lax.axis_size("expert")
    by_heads = queries.shape[1] // HEAD_DIM == patch_count and lax.axis_size("expert") == 2
    attention = attention_by_heads if by_heads else attention_by_gather
    hidden, buffer = attention(
        queries, fresh_keys, fresh_values, stale_keys, stale_values, out_weight, residual, modulation, routes
    )
    capacity = rows // 4
    slice_count = device_count // EXPERTS
    outgoing = jnp.broadcast_to(
        buffer.reshape(EXPERTS, 1, capacity, features), (EXPERTS, slice_count, capacity, features)
    ).reshape(device_count, capacity, features)
    arrived = lax.all_to_all(outgoing, ("patch", "expert"), split_axis=0, concat_axis=0, tiled=True)
    outputs = expert_slice(arrived.reshape(device_count * capacity, features), up_weight, down_weight)
    returned = lax.all_to_all(
        outputs.reshape(device_count, capacity, features),
        ("patch", "expert"),
        split_axis=0,
        concat_axis=0,
        tiled=True,
    )
    return pl.pallas_call(
        combine_kernel,
        out_shape=jax.ShapeDtypeStruct((rows, features), BF16),
        in_specs=[VMEM] * 4,
        out_specs=VMEM,
        compiler_params=pltpu.CompilerParams(vmem_limit_bytes=32 << 20),
        name="combine",
    )(hidden, routes, gates, returned.reshape(EXPERTS, slice_count, capacity, features))


def solution(mesh):
    tokens = P(("group", "patch"), "expert")
    rows = P(("group", "patch", "expert"), None)
    weight = P(("patch", "expert"), None, None)
    placed = (
        tokens, tokens, tokens, tokens, tokens, rows, P("expert", None), P("group", None), weight, weight, rows, rows,
    )
    return jax.shard_map(body, mesh=mesh, in_specs=placed, out_specs=rows, check_vma=False)
```

time: 223 us -> 124 us (0.56)
  waiting for transfers between devices: 107 us -> 26 us
  Pallas kernels: 0 us -> 29.1 us
  matrix products: 28 us -> 0 us
  blocking collectives: 28.9 us -> 50.8 us
  local copies, waits for them, and re-layouts: 25.3 us -> 7.09 us
  other arithmetic: 14 us -> 0 us
  between operations: 13.4 us -> 0.05 us
  starting transfers between devices: 4.29 us -> 9.37 us
    all_gather x2 -> x0, waiting for transfers between devices: 79.6 us -> none  [the longest x1 42 us: attend_keys(): piece_keys = lax.all_gather(stale_keys, 'patch', axis=0, tiled=True)]
    pallas_call x0 -> x6, Pallas kernels: none -> 29.1 us  [the longest x1 15.1 us: expert_slice(): pl.pallas_call(expert_kernel, grid=(units // chunk,), out_shape=jax.Shape...]
    dot_general x7 -> x0, matrix products: 28 us -> none  [the longest x1 16.5 us: expert_slice(): jnp.dot(hidden_units, down_weight[0], preferred_element_type=jnp.float32)]
    all_to_all x0 -> x1, blocking collectives: none -> 24.6 us  [attention_by_heads(): lax.all_to_all(packed, 'patch', split_axis=0, concat_axis=0, tiled=True)]
    all_gather x2 -> x0, local copies, waits for them, and re-layouts: 7.65 us -> none  [the longest x1 3.83 us: attend_keys(): piece_keys = lax.all_gather(stale_keys, 'patch', axis=0, tiled=True)]
    reduce_sum x6 -> x0, other arithmetic: 6.78 us -> none  [the longest x1 2.86 us: body(): mixed = hidden_state + (picked * gates[..., None]).sum(1)]
    gather x2 -> x0, local copies, waits for them, and re-layouts: 6.38 us -> none  [body(): jnp.take(expert_out, slot_index, axis=0).reshape(local_rows, TOPK, features)]
    reduce_scatter x1 -> x0, waiting for transfers between devices: 6.2 us -> none  [body(): lax.psum_scatter(jnp.dot(attended, out_weight, preferred_element_type=jnp...]
  transfers between devices with their start and end apart: 4 -> 4, of which waited for: 4 -> 3; matrix products, arithmetic and copies ran while one was open for 8% -> 1% of each run, Pallas kernels for 0% -> 7%
where the time goes in v1:
time: 124 us; the launch traced here: 122 us
  blocking collectives  50.8 us (41%)
  Pallas kernels  29.1 us (23%)
  waiting for transfers between devices  26 us (21%)
  starting transfers between devices  9.37 us (8%)
  local copies, waits for them, and re-layouts  7.09 us (6%)
    all_to_all x1, blocking collectives, body(): lax.all_to_all(outgoing, ('patch', 'expert'), split_axis=0, concat_axis=0...  26.2 us
    all_to_all x1, blocking collectives, attention_by_heads(): lax.all_to_all(packed, 'patch', split_axis=0, concat_axis=0, tiled=True)  24.6 us
    all_to_all x1, waiting for transfers between devices, body(): lax.all_to_all(outputs.reshape(device_count, capacity, features), ('patch...  20.7 us
    pallas_call x1, Pallas kernels, expert_slice(): pl.pallas_call(expert_kernel, grid=(units // chunk,), out_shape=jax.Shape...  15.1 us
    unnamed x18, local copies, waits for them, and re-layouts  7.09 us
    all_to_all x1, starting transfers between devices, attention_by_heads(): lax.all_to_all(stale, ('patch', 'expert'), split_axis=0, concat_axis=0, t...  5.05 us
    all_to_all x1, waiting for transfers between devices, attention_by_heads(): lax.all_to_all(stale, ('patch', 'expert'), split_axis=0, concat_axis=0, t...  4.32 us
    all_to_all x1, starting transfers between devices, body(): lax.all_to_all(outputs.reshape(device_count, capacity, features), ('patch...  4.13 us
  transfers between devices with their start and end apart: 4, of which 3 were waited for; matrix products, arithmetic and copies ran while one was open for 1% of the time, Pallas kernels for 7%

profile of v1, /device:TPU:1, one launch (start us, length us, event | category | flops | bytes accessed | tf_op | source)
XLA Modules:
  0.0 122.5 jit_solution(9824541069318168012)
XLA Ops:
  0.0 0.1 collective-permute-start.1
  0.1 2.2 %pack.1 = bf16[8,336,128]{2,1,0:T(8,128)(2,1)} custom-call(bf16[128,896]{1,0:T(8,128)(2,1)} %q_ref.3, bf16[128,896]{1,0:T(8,128)(2,1)} %k_ref.2, bf16[128,896]{1,0:T(8,128)(2,1)} %v_ref.2), custom_call_target="tpu_custom_call" | custom-call | tf_op jit(solution)/shard_map/pack/pallas_call | solution.py:151
  2.3 24.6 %all_to_all.20.in_ref = bf16[8,336,128]{2,1,0:T(8,128)(2,1)S(1)} all-to-all(bf16[8,336,128]{2,1,0:T(8,128)(2,1)} %pack.1), channel_id=1, replica_groups=mesh['group'=2,'patch'=8,'expert'=2] {'patch'}, dimensions={0} | all-to-all | bytes 1376256 | tf_op jit(solution)/shard_map/all_to_all | solution.py:159
  26.9 3.0 %attend.1 = bf16[16,64,128]{2,1,0:T(8,128)(2,1)S(1)} custom-call(bf16[8,336,128]{2,1,0:T(8,128)(2,1)S(1)} %all_to_all.20.in_ref), custom_call_target="tpu_custom_call" | custom-call | tf_op jit(solution)/shard_map/attend/pallas_call | solution.py:170
  29.9 0.0 copy-start.1
  29.9 0.7 copy-done.1
  30.6 5.0 %all-to-all-start.1 = ((bf16[16,64,128]{2,1,0:T(8,128)(2,1)}), bf16[16,64,128]{2,1,0:T(8,128)(2,1)S(1)}, u32[]{:S(2)}, u32[]{:S(2)}) async-start(bf16[16,64,128]{2,1,0:T(8,128)(2,1)} %copy-done.1), calls=%async_computation.1 | async-start | bytes 524288 | tf_op jit(solution)/shard_map/all_to_all | solution.py:178
  35.7 3.3 %fresh.1 = (f32[64,1024]{1,0:T(8,128)}, f32[64,1024]{1,0:T(8,128)}) custom-call(s32[1]{0:T(128)} %bitcast.core_ref, bf16[128,896]{1,0:T(8,128)(2,1)} %q_ref.3, bf16[128,896]{1,0:T(8,128)(2,1)} %k_ref.3, bf16[128,896]{1,0:T(8,128)(2,1)} %v_ref.3), custom_call_target="tpu_custom_call" | custom-call | flops 60000000 | bytes 2000000 | tf_op jit(solution)/shard_map/fresh/pallas_call | solution.py:161
  39.0 0.1 collective-permute-start
  39.1 0.8 copy.13.routes_ref
  39.9 1.0 collective-permute-done.other_ref
  40.8 4.3 %all-to-all-done.1 = bf16[16,64,128]{2,1,0:T(8,128)(2,1)S(1)} async-done(((bf16[16,64,128]{2,1,0:T(8,128)(2,1)}), bf16[16,64,128]{2,1,0:T(8,128)(2,1)S(1)}, u32[]{:S(2)}, u32[]{:S(2)}) %all-to-all-start.1) | async-done | bytes 262176 | tf_op jit(solution)/shard_map/all_to_all | solution.py:178
  45.2 0.0 collective-permute-done.1.w_other_ref
  45.2 0.0 copy-start
  45.2 1.9 %copy-done = bf16[896,1792]{1,0:T(8,128)(2,1)S(1)} copy-done((bf16[896,1792]{1,0:T(8,128)(2,1)S(1)}, bf16[896,1792]{1,0:T(8,128)(2,1)}, u32[]{:S(2)}) %copy-start) | copy-done | bytes 3211288
  47.1 0.0 copy-start.4
  47.1 0.9 copy-done.4
  48.0 0.0 copy-start.5
  48.0 0.9 copy-done.5
  49.0 0.0 copy-start.6
  49.0 0.7 copy-done.6
  49.7 4.0 %home.1 = (f32[64,1792]{1,0:T(8,128)S(1)}, bf16[256,1792]{1,0:T(8,128)(2,1)S(1)}) custom-call(s32[1]{0:T(128)} %bitcast.core_ref, bf16[8,2,64,128]{3,2,1,0:T(8,128)(2,1)S(1)} %bitcast.8, f32[64,1024]{1,0:T(8,128)S(1)} %copy-done.4, f32[64,1024]{1,0:T(8,128)} %collective-permute-done.other_ref, bf16[896,1792]{1,0:T(8,128)(2,1)S(1)} %copy-done, ...), custom_call_target="tpu_custom_call" | custom-call | tf_op jit(solution)/shard_map/home/pallas_call | solution.py:179
  53.7 0.0 copy-start.2
  53.7 26.2 %all_to_all.21 = bf16[16,16,1792]{2,1,0:T(8,128)(2,1)S(1)} all-to-all(bf16[16,16,1792]{2,1,0:T(8,128)(2,1)S(1)} %bitcast.9), channel_id=1, replica_groups=mesh['group'=2,'patch'=8,'expert'=2] {'patch','expert'}, dimensions={0} | all-to-all | bytes 1835008 | tf_op jit(solution)/shard_map/all_to_all | solution.py:311
  79.9 0.0 copy-start.7
  79.9 15.1 %experts.1 = bf16[256,1792]{1,0:T(8,128)(2,1)} custom-call(bf16[256,1792]{1,0:T(8,128)(2,1)S(1)} %bitcast.7, bf16[1,1792,3584]{2,1,0:T(8,128)(2,1)} %up_ref.1, bf16[1,3584,1792]{2,1,0:T(8,128)(2,1)} %down_ref.1), custom_call_target="tpu_custom_call" | custom-call | tf_op jit(solution)/shard_map/experts/pallas_call | solution.py:266
  95.0 0.0 copy-done.2
  95.0 4.1 %all-to-all-start.3 = ((bf16[16,16,1792]{2,1,0:T(8,128)(2,1)}), bf16[16,16,1792]{2,1,0:T(8,128)(2,1)S(1)}, u32[]{:S(2)}, u32[]{:S(2)}) async-start(bf16[16,16,1792]{2,1,0:T(8,128)(2,1)} %bitcast.4), calls=%async_computation.3 | async-start | bytes 1835008 | tf_op jit(solution)/shard_map/all_to_all | solution.py:313
  99.1 0.0 copy-done.7
  99.1 0.1 copy.15.gates_ref
  99.2 20.7 %all-to-all-done.3 = bf16[16,16,1792]{2,1,0:T(8,128)(2,1)S(1)} async-done(((bf16[16,16,1792]{2,1,0:T(8,128)(2,1)}), bf16[16,16,1792]{2,1,0:T(8,128)(2,1)S(1)}, u32[]{:S(2)}, u32[]{:S(2)}) %all-to-all-start.3) | async-done | bytes 917536 | tf_op jit(solution)/shard_map/all_to_all | solution.py:313
  120.0 0.0 copy-start.3
  120.0 1.0 copy-done.3
  121.0 1.5 %combine.1 = bf16[64,1792]{1,0:T(8,128)(2,1)} custom-call(f32[64,1792]{1,0:T(8,128)S(1)} %copy-done.3, s32[64,2]{1,0:T(8,128)S(1)} %copy.13.routes_ref, f32[64,2]{1,0:T(8,128)S(1)} %copy.15.gates_ref, bf16[16,1,16,1792]{3,2,1,0:T(8,128)(2,1)S(1)} %bitcast.6), custom_call_target="tpu_custom_call" | custom-call | tf_op jit(solution)/shard_map/combine/pallas_call | solution.py:320
Async XLA Ops:
  0.0 45.2 %collective-permute-start.1 = (bf16[896,1792]{1,0:T(8,128)(2,1)}, bf16[896,1792]{1,0:T(8,128)(2,1)S(1)}, u32[]{:S(2)}, u32[]{:S(2)}) collective-permute-start(bf16[896,1792]{1,0:T(8,128)(2,1)} %w_own_ref.1), channel_id=1, source_target_pairs={{0,1},{1,0},{2,3},{3,2},{4,5},{5,4},{6,7},{7,6},{8,9},{9,8},{10,11... | collective-permute-start | bytes 9633800 | tf_op jit(solution)/shard_map/ppermute | solution.py:158
  29.9 0.7 copy-start.1
  30.6 14.5 %all-to-all-start.1 = ((bf16[16,64,128]{2,1,0:T(8,128)(2,1)}), bf16[16,64,128]{2,1,0:T(8,128)(2,1)S(1)}, u32[]{:S(2)}, u32[]{:S(2)}) async-start(bf16[16,64,128]{2,1,0:T(8,128)(2,1)} %copy-done.1), calls=%async_computation.1 | async-start | bytes 524288 | tf_op jit(solution)/shard_map/all_to_all | solution.py:178
  39.0 1.9 %collective-permute-start = (f32[64,1024]{1,0:T(8,128)}, f32[64,1024]{1,0:T(8,128)}, u32[]{:S(2)}, u32[]{:S(2)}) collective-permute-start(f32[64,1024]{1,0:T(8,128)} %get-tuple-element.10), channel_id=1, source_target_pairs={{0,1},{1,0},{2,3},{3,2},{4,5},{5,4},{6,7},{7,6},{8,9},{9,8},{10,11... | collective-permute-start | bytes 786440 | tf_op jit(solution)/shard_map/ppermute | solution.py:169
  45.2 1.9 %copy-start = (bf16[896,1792]{1,0:T(8,128)(2,1)S(1)}, bf16[896,1792]{1,0:T(8,128)(2,1)}, u32[]{:S(2)}) copy-start(bf16[896,1792]{1,0:T(8,128)(2,1)} %w_own_ref.1) | copy-start | bytes 9633796
  47.1 0.9 copy-start.4
  48.0 0.9 copy-start.5
  49.0 0.7 copy-start.6
  53.7 41.4 %copy-start.2 = (f32[64,1792]{1,0:T(8,128)}, f32[64,1792]{1,0:T(8,128)S(1)}, u32[]{:S(2)}) copy-start(f32[64,1792]{1,0:T(8,128)S(1)} %get-tuple-element.11.hidden_ref) | copy-start | bytes 1376260
  79.9 19.2 %copy-start.7 = (f32[64,2]{0,1:T(2,128)S(1)}, f32[64,2]{0,1:T(2,128)}, u32[]{:S(2)}) copy-start(f32[64,2]{0,1:T(2,128)} %param.23) | copy-start | bytes 1540
  95.0 25.0 %all-to-all-start.3 = ((bf16[16,16,1792]{2,1,0:T(8,128)(2,1)}), bf16[16,16,1792]{2,1,0:T(8,128)(2,1)S(1)}, u32[]{:S(2)}, u32[]{:S(2)}) async-start(bf16[16,16,1792]{2,1,0:T(8,128)(2,1)} %bitcast.4), calls=%async_computation.3 | async-start | bytes 1835008 | tf_op jit(solution)/shard_map/all_to_all | solution.py:313
  120.0 1.0 copy-start.3

commit v2 on v1

--- a/solution.py
+++ b/solution.py
@@ -17,6 +17,7 @@
 F32 = jnp.float32
 VMEM = pl.BlockSpec(memory_space=pltpu.VMEM)
 SMEM = pl.BlockSpec(memory_space=pltpu.SMEM)
+ANY = pl.BlockSpec(memory_space=pl.ANY)
 
 
 def contract(a, b, dim_a, dim_b):
@@ -43,7 +44,9 @@
     return contract(weights, with_ones(values), 1, 1), top * SCALE
 
 
-def fresh_kernel(core_ref, q_ref, k_ref, v_ref, own_ref, other_ref):
+def fresh_kernel(
+    core_ref, q_ref, k_ref, v_ref, routes_ref, gates_ref, own_ref, other_ref, picks_ref, gates_out_ref
+):
     q, k, v = q_ref[...].T, k_ref[...].T, v_ref[...].T
     half = q.shape[1] // 2
     first = core_ref[0] == 0
@@ -55,9 +58,13 @@
         lanes = slice(h * LANES, (h + 1) * LANES)
         own_ref[:, lanes] = jnp.where(first, sums[:half], sums[half:])
         other_ref[:, lanes] = jnp.where(first, sums[half:], sums[:half])
-
-
-def attend_kernel(in_ref, out_ref):
+    slots = picks_ref.shape[2]
+    for k, slot in enumerate(slots_of(routes_ref[...], slots // EXPERTS)):
+        picks_ref[k] = chosen(slot, slots)
+    gates_out_ref[...] = gates_ref[...]
+
+
+def attend_kernel(in_ref, fresh_ref, out_ref):
     patches, tokens = in_ref.shape[0], in_ref.shape[2]
     half = tokens // 2
     lane = lax.broadcasted_iota(jnp.int32, (tokens, LANES), 1)
@@ -105,7 +112,7 @@
 
 def home_kernel(
     core_ref, far_ref, own_ref, other_ref, w_own_ref, w_other_ref, residual_ref, modulation_ref,
-    routes_ref, hidden_ref, buffer_ref, attended_ref,
+    picks_ref, hidden_ref, buffer_ref, attended_ref,
 ):
     heads = far_ref.shape[0]
     core = core_ref[0]
@@ -137,12 +144,10 @@
     normed = (
         centered / jnp.sqrt(variance + 1e-06) * (1.0 + modulation_ref[1:2]) + modulation_ref[0:1]
     ).astype(BF16)
-    slots = buffer_ref.shape[0]
-    picks = [chosen(slot, slots) for slot in slots_of(routes_ref[...], slots // EXPERTS)]
-    buffer_ref[...] = contract(picks[0] + picks[1], normed, 0, 0).astype(BF16)
-
-
-def attention_by_heads(queries, fresh_keys, fresh_values, stale_keys, stale_values, out_weight, residual, modulation, routes):
+    buffer_ref[...] = contract(picks_ref[0] + picks_ref[1], normed, 0, 0).astype(BF16)
+
+
+def attention_by_heads(queries, fresh_keys, fresh_values, stale_keys, stale_values, out_weight, residual, modulation, routes, gates):
     tokens, width = queries.shape
     heads = width // HEAD_DIM
     rows, features = residual.shape
@@ -158,25 +163,33 @@
     w_other = lax.ppermute(out_weight, "expert", swap)
     gathered = lax.all_to_all(packed, "patch", split_axis=0, concat_axis=0, tiled=True)
     fresh_shape = jax.ShapeDtypeStruct((tokens // 2, heads * LANES), F32)
-    fresh_own, fresh_away = pl.pallas_call(
+    slots = EXPERTS * (rows // 4)
+    fresh_own, fresh_away, picks, gates = pl.pallas_call(
         fresh_kernel,
-        out_shape=(fresh_shape, fresh_shape),
-        in_specs=[SMEM] + [VMEM] * 3,
-        out_specs=(VMEM, VMEM),
-        cost_estimate=pl.CostEstimate(flops=60_000_000, bytes_accessed=2_000_000, transcendentals=200_000),
+        out_shape=(
+            fresh_shape,
+            fresh_shape,
+            jax.ShapeDtypeStruct((TOPK, rows, slots), BF16),
+            jax.ShapeDtypeStruct(gates.shape, F32),
+        ),
+        in_specs=[SMEM] + [VMEM] * 5,
+        out_specs=(VMEM,) * 4,
+        compiler_params=pltpu.CompilerParams(vmem_limit_bytes=16 << 20),
+        cost_estimate=pl.CostEstimate(flops=5_000_000_000, bytes_accessed=2_000_000, transcendentals=200_000),
         name="fresh",
-    )(core, queries, fresh_keys, fresh_values)
+    )(core, queries, fresh_keys, fresh_values, routes, gates)
     fresh_other = lax.ppermute(fresh_away, "expert", swap)
     stale = pl.pallas_call(
         attend_kernel,
         out_shape=jax.ShapeDtypeStruct((2 * heads, tokens // 2, LANES), BF16),
-        in_specs=[VMEM],
+        in_specs=[VMEM, ANY],
         out_specs=VMEM,
-        compiler_params=pltpu.CompilerParams(vmem_limit_bytes=32 << 20),
+        compiler_params=pltpu.CompilerParams(vmem_limit_bytes=16 << 20),
+        cost_estimate=pl.CostEstimate(flops=100_000_000_000, bytes_accessed=2_000_000, transcendentals=1_000_000),
         name="attend",
-    )(gathered)
+    )(gathered, fresh_other)
     far = lax.all_to_all(stale, ("patch", "expert"), split_axis=0, concat_axis=0, tiled=True)
-    return pl.pallas_call(
+    hidden, buffer = pl.pallas_call(
         home_kernel,
         out_shape=(
             jax.ShapeDtypeStruct((rows, features), F32),
@@ -185,9 +198,11 @@
         in_specs=[SMEM] + [VMEM] * 8,
         out_specs=(VMEM, VMEM),
         scratch_shapes=[pltpu.VMEM((2, rows, width), BF16)],
-        compiler_params=pltpu.CompilerParams(vmem_limit_bytes=40 << 20),
+        compiler_params=pltpu.CompilerParams(vmem_limit_bytes=16 << 20),
+        cost_estimate=pl.CostEstimate(flops=200_000_000_000, bytes_accessed=8_000_000, transcendentals=100_000),
         name="home",
-    )(core, far.reshape(heads, 2, rows, LANES), fresh_own, fresh_other, out_weight, w_other, residual, modulation, routes)
+    )(core, far.reshape(heads, 2, rows, LANES), fresh_own, fresh_other, out_weight, w_other, residual, modulation, picks)
+    return hidden, buffer, picks, gates
 
 
 def split_heads(block_rows):
@@ -205,7 +220,7 @@
     )
 
 
-def attention_by_gather(queries, fresh_keys, fresh_values, stale_keys, stale_values, out_weight, residual, modulation, routes):
+def attention_by_gather(queries, fresh_keys, fresh_values, stale_keys, stale_values, out_weight, residual, modulation, routes, gates):
     row_count = queries.shape[0]
     own_start = lax.axis_index("patch") * row_count
     query_heads = split_heads(queries)
@@ -236,58 +251,46 @@
     normed = (centered / jnp.sqrt(variance + 1e-06) * (1.0 + modulation[1]) + modulation[0]).astype(BF16)
     capacity = residual.shape[0] // 4
     picks = [chosen(slot, EXPERTS * capacity) for slot in slots_of(routes, capacity)]
-    return hidden, contract(picks[0] + picks[1], normed, 0, 0).astype(BF16)
-
-
-def expert_kernel(x_ref, up_ref, down_ref, out_ref, total_ref):
-    step = pl.program_id(0)
-    units = jax.nn.gelu(
-        jnp.dot(x_ref[...], up_ref[0], preferred_element_type=F32), approximate=True
-    ).astype(BF16)
-    part = jnp.dot(units, down_ref[0], preferred_element_type=F32)
-
-    @pl.when(step == 0)
-    def _():
-        total_ref[...] = part
-
-    @pl.when(step > 0)
-    def _():
-        total_ref[...] += part
-
-    @pl.when(step == pl.num_programs(0) - 1)
-    def _():
-        out_ref[...] = total_ref[...].astype(BF16)
+    return hidden, contract(picks[0] + picks[1], normed, 0, 0).astype(BF16), jnp.stack(picks), gates
+
+
+def expert_kernel(x_ref, up_ref, down_ref, out_ref, units_ref):
+    for part in chunks(up_ref.shape[2]):
+        units_ref[:, part] = jax.nn.gelu(
+            jnp.dot(x_ref[...], up_ref[0, :, part], preferred_element_type=F32), approximate=True
+        ).astype(BF16)
+    for part in chunks(out_ref.shape[1]):
+        out_ref[:, part] = jnp.dot(
+            units_ref[...], down_ref[0, :, part], preferred_element_type=F32
+        ).astype(BF16)
+
+
+def chunks(width):
+    step = 896 if width % 896 == 0 else LANES
+    return [slice(i, i + step) for i in range(0, width, step)]
 
 
 def expert_slice(inputs, up_weight, down_weight):
     rows, features = inputs.shape
-    units = up_weight.shape[2]
-    chunk = next(c for c in (512, 256, 128) if units % c == 0)
     return pl.pallas_call(
         expert_kernel,
-        grid=(units // chunk,),
         out_shape=jax.ShapeDtypeStruct((rows, features), BF16),
-        in_specs=[
-            pl.BlockSpec((rows, features), lambda j: (0, 0)),
-            pl.BlockSpec((1, features, chunk), lambda j: (0, 0, j)),
-            pl.BlockSpec((1, chunk, features), lambda j: (0, j, 0)),
-        ],
-        out_specs=pl.BlockSpec((rows, features), lambda j: (0, 0)),
-        scratch_shapes=[pltpu.VMEM((rows, features), F32)],
-        compiler_params=pltpu.CompilerParams(vmem_limit_bytes=40 << 20),
+        in_specs=[VMEM] * 3,
+        out_specs=VMEM,
+        scratch_shapes=[pltpu.VMEM((rows, up_weight.shape[2]), BF16)],
+        compiler_params=pltpu.CompilerParams(vmem_limit_bytes=16 << 20),
         name="experts",
     )(inputs, up_weight, down_weight)
 
 
-def combine_kernel(hidden_ref, routes_ref, gates_ref, returned_ref, out_ref):
+def combine_kernel(hidden_ref, picks_ref, gates_ref, returned_ref, out_ref):
     slices = returned_ref.shape[1]
     slots = returned_ref.shape[0] * returned_ref.shape[2]
     mixed = hidden_ref[...]
-    picks = [chosen(slot, slots) for slot in slots_of(routes_ref[...], slots // EXPERTS)]
     for s in range(slices):
         rows = returned_ref[:, s].reshape(slots, returned_ref.shape[3])
         for k in range(TOPK):
-            mixed += gates_ref[:, k : k + 1] * jnp.dot(picks[k], rows, preferred_element_type=F32)
+            mixed += gates_ref[:, k : k + 1] * jnp.dot(picks_ref[k], rows, preferred_element_type=F32)
     out_ref[...] = mixed.astype(BF16)
 
 
@@ -300,8 +303,8 @@
     device_count = patch_count * lax.axis_size("expert")
     by_heads = queries.shape[1] // HEAD_DIM == patch_count and lax.axis_size("expert") == 2
     attention = attention_by_heads if by_heads else attention_by_gather
-    hidden, buffer = attention(
-        queries, fresh_keys, fresh_values, stale_keys, stale_values, out_weight, residual, modulation, routes
+    hidden, buffer, picks, gates = attention(
+        queries, fresh_keys, fresh_values, stale_keys, stale_values, out_weight, residual, modulation, routes, gates
     )
     capacity = rows // 4
     slice_count = device_count // EXPERTS
@@ -324,7 +327,7 @@
         out_specs=VMEM,
         compiler_params=pltpu.CompilerParams(vmem_limit_bytes=32 << 20),
         name="combine",
-    )(hidden, routes, gates, returned.reshape(EXPERTS, slice_count, capacity, features))
+    )(hidden, picks, gates, returned.reshape(EXPERTS, slice_count, capacity, features))
 
 
 def solution(mesh):

time: 124 us -> 112 us (0.903); the launches traced: 122 us -> 112 us
  blocking collectives: 50.8 us -> 68.4 us
  waiting for transfers between devices: 26 us -> 9.85 us
  Pallas kernels: 29.1 us -> 21.9 us
  local copies, waits for them, and re-layouts: 7.09 us -> 4.37 us
  starting transfers between devices: 9.37 us -> 7.48 us
    all_to_all x1 -> x2, blocking collectives: 24.6 us -> 41.8 us  [the longest x1 26.7 us: body(): lax.all_to_all(outputs.reshape(device_count, capacity, features), ('patch...]
    all_to_all x2 -> x1, waiting for transfers between devices: 25.1 us -> 8.76 us  [attention_by_heads(): lax.all_to_all(packed, 'patch', split_axis=0, concat_axis=0, tiled=True)]
    pallas_call x2, Pallas kernels: 18.4 us -> 9.32 us  [the longest x1 7.86 us: expert_slice(): pl.pallas_call(expert_kernel, out_shape=jax.ShapeDtypeStruct((rows, featu...]
    all_to_all x2 -> x1, starting transfers between devices: 9.17 us -> 6.38 us  [attention_by_heads(): lax.all_to_all(packed, 'patch', split_axis=0, concat_axis=0, tiled=True)]
    unnamed x18 -> x16, local copies, waits for them, and re-layouts: 7.09 us -> 4.37 us
    pallas_call x1, Pallas kernels: 3.98 us -> 6.17 us  [attention_by_heads(): pl.pallas_call(home_kernel, out_shape=(jax.ShapeDtypeStruct((rows, featur...]
  transfers between devices with their start and end apart: 4 -> 3, of which waited for: 3 -> 2; matrix products, arithmetic and copies ran while one was open for 1% -> 1% of each run, Pallas kernels for 7% -> 4%
where the time goes in v2:
time: 112 us
  blocking collectives  68.4 us (61%)
  Pallas kernels  21.9 us (20%)
  waiting for transfers between devices  9.85 us (9%)
  starting transfers between devices  7.48 us (7%)
  local copies, waits for them, and re-layouts  4.37 us (4%)
    all_to_all x1, blocking collectives, body(): lax.all_to_all(outputs.reshape(device_count, capacity, features), ('patch...  26.7 us
    all_to_all x1, blocking collectives, body(): lax.all_to_all(outgoing, ('patch', 'expert'), split_axis=0, concat_axis=0...  26.6 us
    all_to_all x1, blocking collectives, attention_by_heads(): lax.all_to_all(stale, ('patch', 'expert'), split_axis=0, concat_axis=0, t...  15.1 us
    all_to_all x1, waiting for transfers between devices, attention_by_heads(): lax.all_to_all(packed, 'patch', split_axis=0, concat_axis=0, tiled=True)  8.76 us
    pallas_call x1, Pallas kernels, expert_slice(): pl.pallas_call(expert_kernel, out_shape=jax.ShapeDtypeStruct((rows, featu...  7.86 us
    all_to_all x1, starting transfers between devices, attention_by_heads(): lax.all_to_all(packed, 'patch', split_axis=0, concat_axis=0, tiled=True)  6.38 us
    pallas_call x1, Pallas kernels, attention_by_heads(): pl.pallas_call(home_kernel, out_shape=(jax.ShapeDtypeStruct((rows, featur...  6.17 us
    unnamed x16, local copies, waits for them, and re-layouts  4.37 us
  transfers between devices with their start and end apart: 3, of which 2 were waited for; matrix products, arithmetic and copies ran while one was open for 1% of the time, Pallas kernels for 4%

profile of v2, /device:TPU:1, one launch (start us, length us, event | category | flops | bytes accessed | tf_op | source)
XLA Modules:
  0.0 112.1 jit_solution(15279258492522055679)
XLA Ops:
  0.0 2.3 %pack.1 = bf16[8,336,128]{2,1,0:T(8,128)(2,1)} custom-call(bf16[128,896]{1,0:T(8,128)(2,1)} %q_ref.3, bf16[128,896]{1,0:T(8,128)(2,1)} %k_ref.2, bf16[128,896]{1,0:T(8,128)(2,1)} %v_ref.2), custom_call_target="tpu_custom_call" | custom-call | tf_op jit(solution)/shard_map/pack/pallas_call | solution.py:156
  2.3 6.4 %all-to-all-start = ((bf16[8,336,128]{2,1,0:T(8,128)(2,1)}), bf16[8,336,128]{2,1,0:T(8,128)(2,1)S(1)}, u32[]{:S(2)}, u32[]{:S(2)}) async-start(bf16[8,336,128]{2,1,0:T(8,128)(2,1)} %pack.1), calls=%async_computation | async-start | bytes 1376256 | tf_op jit(solution)/shard_map/all_to_all | solution.py:164
  8.6 0.8 copy.13.routes_ref
  9.4 0.8 copy.14.gates_ref
  10.2 0.0 copy-start.2
  10.2 0.9 copy-done.2
  11.1 0.0 copy-start.3
  11.1 0.9 copy-done.3
  12.1 0.0 copy-start.4
  12.1 0.9 copy-done.4
  13.0 1.5 %fresh.1 = (f32[64,1024]{1,0:T(8,128)S(1)}, f32[64,1024]{1,0:T(8,128)S(1)}, bf16[2,64,256]{2,1,0:T(8,128)(2,1)S(1)}, f32[64,2]{1,0:T(8,128)S(1)}) custom-call(s32[1]{0:T(128)} %bitcast.core_ref, bf16[128,896]{1,0:T(8,128)(2,1)S(1)} %copy-done.2, bf16[128,896]{1,0:T(8,128)(2,1)S(1)} %copy-done.3, bf16[128,896]{1,0:T(8,128)(2,1)S(1)} %copy-done.4, ...), custom_call_target="tpu_custom_call" | custom-call | flops 5000000000 | bytes 2000000 | tf_op jit(solution)/shard_map/fresh/pallas_call | solution.py:167
  14.5 0.0 copy-start.5
  14.5 0.0 copy-start.6
  14.5 1.0 collective-permute-start
  15.5 0.1 collective-permute-start.1
  15.6 1.1 collective-permute-done.fresh_ref.other_ref
  16.7 8.8 %all-to-all-done.in_ref = bf16[8,336,128]{2,1,0:T(8,128)(2,1)S(1)} async-done(((bf16[8,336,128]{2,1,0:T(8,128)(2,1)}), bf16[8,336,128]{2,1,0:T(8,128)(2,1)S(1)}, u32[]{:S(2)}, u32[]{:S(2)}) %all-to-all-start) | async-done | bytes 688160 | tf_op jit(solution)/shard_map/all_to_all | solution.py:164
  25.4 3.0 %attend.1 = bf16[16,64,128]{2,1,0:T(8,128)(2,1)S(1)} custom-call(bf16[8,336,128]{2,1,0:T(8,128)(2,1)S(1)} %all-to-all-done.in_ref, f32[64,1024]{1,0:T(8,128)S(1)} %collective-permute-done.fresh_ref.other_ref), custom_call_target="tpu_custom_call" | custom-call | flops 99999997952 | bytes 2000000 | tf_op jit(solution)/shard_map/attend/pallas_call | solution.py:182
  28.5 15.1 %all_to_all.20 = bf16[16,64,128]{2,1,0:T(8,128)(2,1)S(1)} all-to-all(bf16[16,64,128]{2,1,0:T(8,128)(2,1)S(1)} %attend.1), channel_id=1, replica_groups=mesh['group'=2,'patch'=8,'expert'=2] {'patch','expert'}, dimensions={0} | all-to-all | bytes 524288 | tf_op jit(solution)/shard_map/all_to_all | solution.py:191
  43.6 0.0 collective-permute-done.1.w_other_ref
  43.6 0.0 copy-done.5
  43.6 0.0 copy-done.6
  43.6 0.0 copy-start
  43.6 0.0 copy-start.1
  43.6 6.2 %home.1 = (f32[64,1792]{1,0:T(8,128)S(1)}, bf16[256,1792]{1,0:T(8,128)(2,1)S(1)}) custom-call(s32[1]{0:T(128)} %bitcast.core_ref, bf16[8,2,64,128]{3,2,1,0:T(8,128)(2,1)S(1)} %bitcast.10, f32[64,1024]{1,0:T(8,128)S(1)} %get-tuple-element.12.own_ref, f32[64,1024]{1,0:T(8,128)S(1)} %collective-permute-done.fresh_ref.other_ref, bf16[896,1792]{1,0:T(8,128)(2,1)} %w_own_ref.1, ...), custom_call_target="tpu_custom_call" | custom-call | flops 199999995904 | bytes 8000000 | tf_op jit(solution)/shard_map/home/pallas_call | solution.py:192
  49.8 26.6 %all_to_all.21 = bf16[16,16,1792]{2,1,0:T(8,128)(2,1)S(1)} all-to-all(bf16[16,16,1792]{2,1,0:T(8,128)(2,1)S(1)} %bitcast.9), channel_id=1, replica_groups=mesh['group'=2,'patch'=8,'expert'=2] {'patch','expert'}, dimensions={0} | all-to-all | bytes 1835008 | tf_op jit(solution)/shard_map/all_to_all | solution.py:314
  76.4 0.0 copy-done
  76.4 0.0 copy-done.1
  76.4 7.9 %experts.1 = bf16[256,1792]{1,0:T(8,128)(2,1)S(1)} custom-call(bf16[256,1792]{1,0:T(8,128)(2,1)S(1)} %bitcast.7, bf16[1,1792,3584]{2,1,0:T(8,128)(2,1)S(1)} %copy-done, bf16[1,3584,1792]{2,1,0:T(8,128)(2,1)S(1)} %copy-done.1), custom_call_target="tpu_custom_call" | custom-call | tf_op jit(solution)/shard_map/experts/pallas_call | solution.py:275
  84.2 26.7 %all_to_all.22 = bf16[16,16,1792]{2,1,0:T(8,128)(2,1)S(1)} all-to-all(bf16[16,16,1792]{2,1,0:T(8,128)(2,1)S(1)} %bitcast.8), channel_id=1, replica_groups=mesh['group'=2,'patch'=8,'expert'=2] {'patch','expert'}, dimensions={0} | all-to-all | bytes 1835008 | tf_op jit(solution)/shard_map/all_to_all | solution.py:316
  111.0 1.1 %combine.1 = bf16[64,1792]{1,0:T(8,128)(2,1)} custom-call(f32[64,1792]{1,0:T(8,128)S(1)} %get-tuple-element.14.hidden_ref, bf16[2,64,256]{2,1,0:T(8,128)(2,1)S(1)} %get-tuple-element.13.picks_ref, f32[64,2]{1,0:T(8,128)S(1)} %get-tuple-element.15.gates_ref, bf16[16,1,16,1792]{3,2,1,0:T(8,128)(2,1)S(1)} %bitcast.6), custom_call_target="tpu_custom_call" | custom-call | tf_op jit(solution)/shard_map/combine/pallas_call | solution.py:323
Async XLA Ops:
  2.3 23.2 %all-to-all-start = ((bf16[8,336,128]{2,1,0:T(8,128)(2,1)}), bf16[8,336,128]{2,1,0:T(8,128)(2,1)S(1)}, u32[]{:S(2)}, u32[]{:S(2)}) async-start(bf16[8,336,128]{2,1,0:T(8,128)(2,1)} %pack.1), calls=%async_computation | async-start | bytes 1376256 | tf_op jit(solution)/shard_map/all_to_all | solution.py:164
  10.2 0.9 copy-start.2
  11.1 0.9 copy-start.3
  12.1 0.9 copy-start.4
  14.5 29.1 %copy-start.5 = (bf16[64,1792]{1,0:T(8,128)(2,1)S(1)}, bf16[64,1792]{1,0:T(8,128)(2,1)}, u32[]{:S(2)}) copy-start(bf16[64,1792]{1,0:T(8,128)(2,1)} %residual_ref.1) | copy-start | bytes 688132
  14.5 29.1 %copy-start.6 = (f32[2,1792]{1,0:T(2,128)S(1)}, f32[2,1792]{1,0:T(2,128)}, u32[]{:S(2)}) copy-start(f32[2,1792]{1,0:T(2,128)} %modulation_ref.1) | copy-start | bytes 43012
  14.5 2.2 %collective-permute-start = (f32[64,1024]{1,0:T(8,128)S(1)}, f32[64,1024]{1,0:T(8,128)S(1)}, u32[]{:S(2)}, u32[]{:S(2)}) collective-permute-start(f32[64,1024]{1,0:T(8,128)S(1)} %get-tuple-element.11), channel_id=1, source_target_pairs={{0,1},{1,0},{2,3},{3,2},{4,5},{5,4},{6,7},{7,6},{8,9},{9,8},{10,11... | collective-permute-start | bytes 786440 | tf_op jit(solution)/shard_map/ppermute | solution.py:181
  15.5 28.1 %collective-permute-start.1 = (bf16[896,1792]{1,0:T(8,128)(2,1)}, bf16[896,1792]{1,0:T(8,128)(2,1)}, u32[]{:S(2)}, u32[]{:S(2)}) collective-permute-start(bf16[896,1792]{1,0:T(8,128)(2,1)} %w_own_ref.1), channel_id=1, source_target_pairs={{0,1},{1,0},{2,3},{3,2},{4,5},{5,4},{6,7},{7,6},{8,9},{9,8},{10,11... | collective-permute-start | bytes 9633800 | tf_op jit(solution)/shard_map/ppermute | solution.py:163
  43.6 32.8 %copy-start = (bf16[1,1792,3584]{2,1,0:T(8,128)(2,1)S(1)}, bf16[1,1792,3584]{2,1,0:T(8,128)(2,1)}, u32[]{:S(2)}) copy-start(bf16[1,1792,3584]{2,1,0:T(8,128)(2,1)} %up_ref.1) | copy-start | bytes 38535172
  43.6 32.8 %copy-start.1 = (bf16[1,3584,1792]{2,1,0:T(8,128)(2,1)S(1)}, bf16[1,3584,1792]{2,1,0:T(8,128)(2,1)}, u32[]{:S(2)}) copy-start(bf16[1,3584,1792]{2,1,0:T(8,128)(2,1)} %down_ref.1) | copy-start | bytes 38535172

commit v3 on v2

--- a/solution.py
+++ b/solution.py
@@ -66,25 +66,44 @@
 
 def attend_kernel(in_ref, fresh_ref, out_ref):
     patches, tokens = in_ref.shape[0], in_ref.shape[2]
-    half = tokens // 2
-    lane = lax.broadcasted_iota(jnp.int32, (tokens, LANES), 1)
-    for p in range(patches):
-        others = [j for j in range(patches) if j != p]
-        keys = jnp.concatenate([in_ref[j, HEAD_DIM : 2 * HEAD_DIM] for j in others], axis=1)
-        values = jnp.concatenate([in_ref[j, 2 * HEAD_DIM :] for j in others], axis=1)
-        sums, top = partial_softmax(in_ref[p, :HEAD_DIM], keys, values)
+    half, rows, steps = tokens // 2, 2 * tokens, patches // 2
+    keys = jnp.concatenate([in_ref[j, HEAD_DIM : 2 * HEAD_DIM] for j in range(patches)], axis=1)
+    values = with_ones(jnp.concatenate([in_ref[j, 2 * HEAD_DIM :] for j in range(patches)], axis=1))
+    lane = lax.broadcasted_iota(jnp.int32, (rows, LANES), 1)
+    own = (lax.broadcasted_iota(jnp.int32, (rows, rows), 0) < tokens) == (
+        lax.broadcasted_iota(jnp.int32, (rows, rows), 1) < tokens
+    )
+
+    def scores_of(step):
+        query = jnp.concatenate([in_ref[2 * step + i, :HEAD_DIM] for i in range(2)], axis=1)
+        scores = contract(query, keys, 0, 0)
+        first, last = step * rows, (step + 1) * rows
+        parts = [jnp.where(own, -1e30, scores[:, first:last])]
+        if step > 0:
+            parts.insert(0, scores[:, :first])
+        if step < steps - 1:
+            parts.append(scores[:, last:])
+        return jnp.concatenate(parts, axis=1)
+
+    scores = scores_of(0)
+    for step in range(steps):
+        following = scores_of(step + 1) if step < steps - 1 else None
+        top = scores.max(-1, keepdims=True)
+        weights = jnp.exp2((scores - top) * (SCALE * math.log2(math.e))).astype(BF16)
+        sums = contract(weights, values, 1, 1)
         total = sums[:, HEAD_DIM : HEAD_DIM + 1]
-        log_total = top + jnp.log(total)
+        log_total = top * SCALE + jnp.log(total)
         high = log_total.astype(BF16).astype(F32)
         rest = log_total - high
         middle = rest.astype(BF16).astype(F32)
-        result = sums / total
+        result = sums * (1.0 / total)
         result = jnp.where(lane == HEAD_DIM, high, result)
         result = jnp.where(lane == HEAD_DIM + 1, middle, result)
         result = jnp.where(lane == HEAD_DIM + 2, rest - middle, result)
         result = result.astype(BF16)
-        out_ref[2 * p] = result[:half]
-        out_ref[2 * p + 1] = result[half:]
+        for i in range(4):
+            out_ref[4 * step + i] = result[i * half : (i + 1) * half]
+        scores = following
 
 
 def slots_of(routes, capacity):
@@ -112,12 +131,18 @@
 
 def home_kernel(
     core_ref, far_ref, own_ref, other_ref, w_own_ref, w_other_ref, residual_ref, modulation_ref,
-    picks_ref, hidden_ref, buffer_ref, attended_ref,
+    picks_ref, hidden_ref, buffer_ref, attended_ref, w_ref, loaded_ref,
 ):
+    loads = [
+        pltpu.make_async_copy(source, w_ref.at[i], loaded_ref.at[i])
+        for i, source in enumerate((w_own_ref, w_other_ref))
+    ]
+    for load in loads:
+        load.start()
     heads = far_ref.shape[0]
     core = core_ref[0]
     projected = None
-    for side, (near_ref, w_ref) in enumerate(((own_ref, w_own_ref), (other_ref, w_other_ref))):
+    for side, near_ref in enumerate((own_ref, other_ref)):
         which = core if side == 0 else 1 - core
         for h in range(heads):
             far = far_ref[h, which].astype(F32)
@@ -135,7 +160,9 @@
             scale = 1.0 / (far_weight + near_total * near_weight)
             merged = far * (far_weight * scale) + near * (near_weight * scale)
             attended_ref[side, :, h * HEAD_DIM : (h + 1) * HEAD_DIM] = merged[:, :HEAD_DIM].astype(BF16)
-        part = jnp.dot(attended_ref[side], w_ref[...], preferred_element_type=F32)
+    for side in range(2):
+        loads[side].wait()
+        part = jnp.dot(attended_ref[side], w_ref[side], preferred_element_type=F32)
         projected = part if projected is None else projected + part
     hidden = residual_ref[...].astype(F32) + projected
     hidden_ref[...] = hidden
@@ -195,10 +222,14 @@
             jax.ShapeDtypeStruct((rows, features), F32),
             jax.ShapeDtypeStruct((EXPERTS * (rows // 4), features), BF16),
         ),
-        in_specs=[SMEM] + [VMEM] * 8,
+        in_specs=[SMEM] + [VMEM] * 3 + [ANY] * 2 + [VMEM] * 3,
         out_specs=(VMEM, VMEM),
-        scratch_shapes=[pltpu.VMEM((2, rows, width), BF16)],
-        compiler_params=pltpu.CompilerParams(vmem_limit_bytes=16 << 20),
+        scratch_shapes=[
+            pltpu.VMEM((2, rows, width), BF16),
+            pltpu.VMEM((2,) + out_weight.shape, BF16),
+            pltpu.SemaphoreType.DMA((2,)),
+        ],
+        compiler_params=pltpu.CompilerParams(vmem_limit_bytes=20 << 20),
         cost_estimate=pl.CostEstimate(flops=200_000_000_000, bytes_accessed=8_000_000, transcendentals=100_000),
         name="home",
     )(core, far.reshape(heads, 2, rows, LANES), fresh_own, fresh_other, out_weight, w_other, residual, modulation, picks)
@@ -301,7 +332,7 @@
     rows, features = residual.shape
     patch_count = lax.axis_size("patch")
     device_count = patch_count * lax.axis_size("expert")
-    by_heads = queries.shape[1] // HEAD_DIM == patch_count and lax.axis_size("expert") == 2
+    by_heads = queries.shape[1] // HEAD_DIM == patch_count and patch_count % 2 == 0 and lax.axis_size("expert") == 2
     attention = attention_by_heads if by_heads else attention_by_gather
     hidden, buffer, picks, gates = attention(
         queries, fresh_keys, fresh_values, stale_keys, stale_values, out_weight, residual, modulation, routes, gates
@@ -325,7 +356,7 @@
         out_shape=jax.ShapeDtypeStruct((rows, features), BF16),
         in_specs=[VMEM] * 4,
         out_specs=VMEM,
-        compiler_params=pltpu.CompilerParams(vmem_limit_bytes=32 << 20),
+        compiler_params=pltpu.CompilerParams(vmem_limit_bytes=20 << 20),
         name="combine",
     )(hidden, picks, gates, returned.reshape(EXPERTS, slice_count, capacity, features))
 

time: 112 us -> 114 us (1.018)
  Pallas kernels: 21.9 us -> 24.1 us
    pallas_call x1, Pallas kernels: 6.17 us -> 9.66 us  [attention_by_heads(): pl.pallas_call(home_kernel, out_shape=(jax.ShapeDtypeStruct((rows, featur...]
    pallas_call x1, Pallas kernels: 3.04 us -> 1.7 us  [attention_by_heads(): pl.pallas_call(attend_kernel, out_shape=jax.ShapeDtypeStruct((2 * heads,...]
  transfers between devices with their start and end apart: 3 -> 3, of which waited for: 2 -> 2; matrix products, arithmetic and copies ran while one was open for 1% -> 1% of each run, Pallas kernels for 4% -> 3%
where the time goes in v3:
time: 114 us
  blocking collectives  68.2 us (60%)
  Pallas kernels  24.1 us (21%)
  waiting for transfers between devices  9.85 us (9%)
  starting transfers between devices  7.48 us (7%)
  local copies, waits for them, and re-layouts  4.37 us (4%)
    all_to_all x1, blocking collectives, body(): lax.all_to_all(outputs.reshape(device_count, capacity, features), ('patch...  26.8 us
    all_to_all x1, blocking collectives, body(): lax.all_to_all(outgoing, ('patch', 'expert'), split_axis=0, concat_axis=0...  26.2 us
    all_to_all x1, blocking collectives, attention_by_heads(): lax.all_to_all(stale, ('patch', 'expert'), split_axis=0, concat_axis=0, t...  15.1 us
    pallas_call x1, Pallas kernels, attention_by_heads(): pl.pallas_call(home_kernel, out_shape=(jax.ShapeDtypeStruct((rows, featur...  9.66 us
    all_to_all x1, waiting for transfers between devices, attention_by_heads(): lax.all_to_all(packed, 'patch', split_axis=0, concat_axis=0, tiled=True)  8.76 us
    pallas_call x1, Pallas kernels, expert_slice(): pl.pallas_call(expert_kernel, out_shape=jax.ShapeDtypeStruct((rows, featu...  7.85 us
    all_to_all x1, starting transfers between devices, attention_by_heads(): lax.all_to_all(packed, 'patch', split_axis=0, concat_axis=0, tiled=True)  6.38 us
    unnamed x16, local copies, waits for them, and re-layouts  4.37 us
  transfers between devices with their start and end apart: 3, of which 2 were waited for; matrix products, arithmetic and copies ran while one was open for 1% of the time, Pallas kernels for 3%

profile of v3, /device:TPU:1, one launch (start us, length us, event | category | flops | bytes accessed | tf_op | source)
XLA Modules:
  0.0 114.0 jit_solution(4997522542562667335)
XLA Ops:
  0.0 2.3 %pack.1 = bf16[8,336,128]{2,1,0:T(8,128)(2,1)} custom-call(bf16[128,896]{1,0:T(8,128)(2,1)} %q_ref.3, bf16[128,896]{1,0:T(8,128)(2,1)} %k_ref.2, bf16[128,896]{1,0:T(8,128)(2,1)} %v_ref.2), custom_call_target="tpu_custom_call" | custom-call | tf_op jit(solution)/shard_map/pack/pallas_call | solution.py:183
  2.3 6.4 %all-to-all-start = ((bf16[8,336,128]{2,1,0:T(8,128)(2,1)}), bf16[8,336,128]{2,1,0:T(8,128)(2,1)S(1)}, u32[]{:S(2)}, u32[]{:S(2)}) async-start(bf16[8,336,128]{2,1,0:T(8,128)(2,1)} %pack.1), calls=%async_computation | async-start | bytes 1376256 | tf_op jit(solution)/shard_map/all_to_all | solution.py:191
  8.6 0.8 copy.13.routes_ref
  9.4 0.8 copy.14.gates_ref
  10.2 0.0 copy-start.2
  10.2 0.9 copy-done.2
  11.1 0.0 copy-start.3
  11.1 0.9 copy-done.3
  12.1 0.0 copy-start.4
  12.1 0.9 copy-done.4
  13.0 1.5 %fresh.1 = (f32[64,1024]{1,0:T(8,128)S(1)}, f32[64,1024]{1,0:T(8,128)S(1)}, bf16[2,64,256]{2,1,0:T(8,128)(2,1)S(1)}, f32[64,2]{1,0:T(8,128)S(1)}) custom-call(s32[1]{0:T(128)} %bitcast.core_ref, bf16[128,896]{1,0:T(8,128)(2,1)S(1)} %copy-done.2, bf16[128,896]{1,0:T(8,128)(2,1)S(1)} %copy-done.3, bf16[128,896]{1,0:T(8,128)(2,1)S(1)} %copy-done.4, ...), custom_call_target="tpu_custom_call" | custom-call | flops 5000000000 | bytes 2000000 | tf_op jit(solution)/shard_map/fresh/pallas_call | solution.py:194
  14.5 0.0 copy-start.5
  14.5 0.0 copy-start.6
  14.5 1.0 collective-permute-start
  15.5 0.1 collective-permute-start.1
  15.6 1.1 collective-permute-done.fresh_ref.other_ref
  16.7 8.8 %all-to-all-done.in_ref = bf16[8,336,128]{2,1,0:T(8,128)(2,1)S(1)} async-done(((bf16[8,336,128]{2,1,0:T(8,128)(2,1)}), bf16[8,336,128]{2,1,0:T(8,128)(2,1)S(1)}, u32[]{:S(2)}, u32[]{:S(2)}) %all-to-all-start) | async-done | bytes 688160 | tf_op jit(solution)/shard_map/all_to_all | solution.py:191
  25.4 1.7 %attend.1 = bf16[16,64,128]{2,1,0:T(8,128)(2,1)S(1)} custom-call(bf16[8,336,128]{2,1,0:T(8,128)(2,1)S(1)} %all-to-all-done.in_ref, f32[64,1024]{1,0:T(8,128)S(1)} %collective-permute-done.fresh_ref.other_ref), custom_call_target="tpu_custom_call" | custom-call | flops 99999997952 | bytes 2000000 | tf_op jit(solution)/shard_map/attend/pallas_call | solution.py:209
  27.1 15.1 %all_to_all.20 = bf16[16,64,128]{2,1,0:T(8,128)(2,1)S(1)} all-to-all(bf16[16,64,128]{2,1,0:T(8,128)(2,1)S(1)} %attend.1), channel_id=1, replica_groups=mesh['group'=2,'patch'=8,'expert'=2] {'patch','expert'}, dimensions={0} | all-to-all | bytes 524288 | tf_op jit(solution)/shard_map/all_to_all | solution.py:218
  42.2 0.0 collective-permute-done.1.w_other_ref
  42.2 0.0 copy-done.5
  42.2 0.0 copy-done.6
  42.3 0.0 copy-start
  42.3 0.0 copy-start.1
  42.3 9.7 %home.1 = (f32[64,1792]{1,0:T(8,128)S(1)}, bf16[256,1792]{1,0:T(8,128)(2,1)S(1)}) custom-call(s32[1]{0:T(128)} %bitcast.core_ref, bf16[8,2,64,128]{3,2,1,0:T(8,128)(2,1)S(1)} %bitcast.10, f32[64,1024]{1,0:T(8,128)S(1)} %get-tuple-element.12.own_ref, f32[64,1024]{1,0:T(8,128)S(1)} %collective-permute-done.fresh_ref.other_ref, bf16[896,1792]{1,0:T(8,128)(2,1)} %w_own_ref.1, ...), custom_call_target="tpu_custom_call" | custom-call | flops 199999995904 | bytes 8000000 | tf_op jit(solution)/shard_map/home/pallas_call | solution.py:219
  51.9 26.2 %all_to_all.21 = bf16[16,16,1792]{2,1,0:T(8,128)(2,1)S(1)} all-to-all(bf16[16,16,1792]{2,1,0:T(8,128)(2,1)S(1)} %bitcast.9), channel_id=1, replica_groups=mesh['group'=2,'patch'=8,'expert'=2] {'patch','expert'}, dimensions={0} | all-to-all | bytes 1835008 | tf_op jit(solution)/shard_map/all_to_all | solution.py:345
  78.2 0.0 copy-done
  78.2 0.0 copy-done.1
  78.2 7.9 %experts.1 = bf16[256,1792]{1,0:T(8,128)(2,1)S(1)} custom-call(bf16[256,1792]{1,0:T(8,128)(2,1)S(1)} %bitcast.7, bf16[1,1792,3584]{2,1,0:T(8,128)(2,1)S(1)} %copy-done, bf16[1,3584,1792]{2,1,0:T(8,128)(2,1)S(1)} %copy-done.1), custom_call_target="tpu_custom_call" | custom-call | tf_op jit(solution)/shard_map/experts/pallas_call | solution.py:306
  86.1 26.8 %all_to_all.22 = bf16[16,16,1792]{2,1,0:T(8,128)(2,1)S(1)} all-to-all(bf16[16,16,1792]{2,1,0:T(8,128)(2,1)S(1)} %bitcast.8), channel_id=1, replica_groups=mesh['group'=2,'patch'=8,'expert'=2] {'patch','expert'}, dimensions={0} | all-to-all | bytes 1835008 | tf_op jit(solution)/shard_map/all_to_all | solution.py:347
  112.9 1.1 combine.1
Async XLA Ops:
  2.3 23.2 %all-to-all-start = ((bf16[8,336,128]{2,1,0:T(8,128)(2,1)}), bf16[8,336,128]{2,1,0:T(8,128)(2,1)S(1)}, u32[]{:S(2)}, u32[]{:S(2)}) async-start(bf16[8,336,128]{2,1,0:T(8,128)(2,1)} %pack.1), calls=%async_computation | async-start | bytes 1376256 | tf_op jit(solution)/shard_map/all_to_all | solution.py:191
  10.2 0.9 copy-start.2
  11.1 0.9 copy-start.3
  12.1 0.9 copy-start.4
  14.5 27.8 %copy-start.5 = (bf16[64,1792]{1,0:T(8,128)(2,1)S(1)}, bf16[64,1792]{1,0:T(8,128)(2,1)}, u32[]{:S(2)}) copy-start(bf16[64,1792]{1,0:T(8,128)(2,1)} %residual_ref.1) | copy-start | bytes 688132
  14.5 27.8 %copy-start.6 = (f32[2,1792]{1,0:T(2,128)S(1)}, f32[2,1792]{1,0:T(2,128)}, u32[]{:S(2)}) copy-start(f32[2,1792]{1,0:T(2,128)} %modulation_ref.1) | copy-start | bytes 43012
  14.5 2.2 %collective-permute-start = (f32[64,1024]{1,0:T(8,128)S(1)}, f32[64,1024]{1,0:T(8,128)S(1)}, u32[]{:S(2)}, u32[]{:S(2)}) collective-permute-start(f32[64,1024]{1,0:T(8,128)S(1)} %get-tuple-element.11), channel_id=1, source_target_pairs={{0,1},{1,0},{2,3},{3,2},{4,5},{5,4},{6,7},{7,6},{8,9},{9,8},{10,11... | collective-permute-start | bytes 786440 | tf_op jit(solution)/shard_map/ppermute | solution.py:208
  15.5 26.7 %collective-permute-start.1 = (bf16[896,1792]{1,0:T(8,128)(2,1)}, bf16[896,1792]{1,0:T(8,128)(2,1)}, u32[]{:S(2)}, u32[]{:S(2)}) collective-permute-start(bf16[896,1792]{1,0:T(8,128)(2,1)} %w_own_ref.1), channel_id=1, source_target_pairs={{0,1},{1,0},{2,3},{3,2},{4,5},{5,4},{6,7},{7,6},{8,9},{9,8},{10,11... | collective-permute-start | bytes 9633800 | tf_op jit(solution)/shard_map/ppermute | solution.py:190
  42.3 35.9 %copy-start = (bf16[1,1792,3584]{2,1,0:T(8,128)(2,1)S(1)}, bf16[1,1792,3584]{2,1,0:T(8,128)(2,1)}, u32[]{:S(2)}) copy-start(bf16[1,1792,3584]{2,1,0:T(8,128)(2,1)} %up_ref.1) | copy-start | bytes 38535172
  42.3 35.9 %copy-start.1 = (bf16[1,3584,1792]{2,1,0:T(8,128)(2,1)S(1)}, bf16[1,3584,1792]{2,1,0:T(8,128)(2,1)}, u32[]{:S(2)}) copy-start(bf16[1,3584,1792]{2,1,0:T(8,128)(2,1)} %down_ref.1) | copy-start | bytes 38535172

commit v4 on v3

--- a/solution.py
+++ b/solution.py
@@ -131,7 +131,7 @@
 
 def home_kernel(
     core_ref, far_ref, own_ref, other_ref, w_own_ref, w_other_ref, residual_ref, modulation_ref,
-    picks_ref, hidden_ref, buffer_ref, attended_ref, w_ref, loaded_ref,
+    hidden_ref, normed_ref, attended_ref, w_ref, loaded_ref,
 ):
     loads = [
         pltpu.make_async_copy(source, w_ref.at[i], loaded_ref.at[i])
@@ -168,10 +168,13 @@
     hidden_ref[...] = hidden
     centered = hidden - hidden.mean(-1, keepdims=True)
     variance = (centered * centered).mean(-1, keepdims=True)
-    normed = (
+    normed_ref[...] = (
         centered / jnp.sqrt(variance + 1e-06) * (1.0 + modulation_ref[1:2]) + modulation_ref[0:1]
     ).astype(BF16)
-    buffer_ref[...] = contract(picks_ref[0] + picks_ref[1], normed, 0, 0).astype(BF16)
+
+
+def slots_kernel(normed_ref, picks_ref, buffer_ref):
+    buffer_ref[...] = contract(picks_ref[0] + picks_ref[1], normed_ref[...], 0, 0).astype(BF16)
 
 
 def attention_by_heads(queries, fresh_keys, fresh_values, stale_keys, stale_values, out_weight, residual, modulation, routes, gates):
@@ -216,13 +219,13 @@
         name="attend",
     )(gathered, fresh_other)
     far = lax.all_to_all(stale, ("patch", "expert"), split_axis=0, concat_axis=0, tiled=True)
-    hidden, buffer = pl.pallas_call(
+    hidden, normed = pl.pallas_call(
         home_kernel,
         out_shape=(
             jax.ShapeDtypeStruct((rows, features), F32),
-            jax.ShapeDtypeStruct((EXPERTS * (rows // 4), features), BF16),
+            jax.ShapeDtypeStruct((rows, features), BF16),
         ),
-        in_specs=[SMEM] + [VMEM] * 3 + [ANY] * 2 + [VMEM] * 3,
+        in_specs=[SMEM] + [VMEM] * 3 + [ANY] * 2 + [VMEM] * 2,
         out_specs=(VMEM, VMEM),
         scratch_shapes=[
             pltpu.VMEM((2, rows, width), BF16),
@@ -230,9 +233,18 @@
             pltpu.SemaphoreType.DMA((2,)),
         ],
         compiler_params=pltpu.CompilerParams(vmem_limit_bytes=20 << 20),
+        cost_estimate=pl.CostEstimate(flops=4_000_000_000, bytes_accessed=8_000_000, transcendentals=100_000),
+        name="home",
+    )(core, far.reshape(heads, 2, rows, LANES), fresh_own, fresh_other, out_weight, w_other, residual, modulation)
+    buffer = pl.pallas_call(
+        slots_kernel,
+        out_shape=jax.ShapeDtypeStruct((slots, features), BF16),
+        in_specs=[VMEM] * 2,
+        out_specs=VMEM,
+        compiler_params=pltpu.CompilerParams(vmem_limit_bytes=12 << 20),
         cost_estimate=pl.CostEstimate(flops=200_000_000_000, bytes_accessed=8_000_000, transcendentals=100_000),
-        name="home",
-    )(core, far.reshape(heads, 2, rows, LANES), fresh_own, fresh_other, out_weight, w_other, residual, modulation, picks)
+        name="slots",
+    )(normed, picks)
     return hidden, buffer, picks, gates
 
 

time: 114 us -> 113 us (level)
  Pallas kernels: 24.1 us -> 22.6 us
    pallas_call x1, Pallas kernels: 9.66 us -> 7.71 us  [attention_by_heads(): pl.pallas_call(home_kernel, out_shape=(jax.ShapeDtypeStruct((rows, featur...]
where the time goes in v4:
time: 113 us
  blocking collectives  68.4 us (61%)
  Pallas kernels  22.6 us (20%)
  waiting for transfers between devices  9.85 us (9%)
  starting transfers between devices  7.48 us (7%)
  local copies, waits for them, and re-layouts  4.37 us (4%)
    all_to_all x1, blocking collectives, body(): lax.all_to_all(outputs.reshape(device_count, capacity, features), ('patch...  26.7 us
    all_to_all x1, blocking collectives, body(): lax.all_to_all(outgoing, ('patch', 'expert'), split_axis=0, concat_axis=0...  26.6 us
    all_to_all x1, blocking collectives, attention_by_heads(): lax.all_to_all(stale, ('patch', 'expert'), split_axis=0, concat_axis=0, t...  15.1 us
    all_to_all x1, waiting for transfers between devices, attention_by_heads(): lax.all_to_all(packed, 'patch', split_axis=0, concat_axis=0, tiled=True)  8.76 us
    pallas_call x1, Pallas kernels, expert_slice(): pl.pallas_call(expert_kernel, out_shape=jax.ShapeDtypeStruct((rows, featu...  7.85 us
    pallas_call x1, Pallas kernels, attention_by_heads(): pl.pallas_call(home_kernel, out_shape=(jax.ShapeDtypeStruct((rows, featur...  7.71 us
    all_to_all x1, starting transfers between devices, attention_by_heads(): lax.all_to_all(packed, 'patch', split_axis=0, concat_axis=0, tiled=True)  6.38 us
    unnamed x16, local copies, waits for them, and re-layouts  4.37 us
  transfers between devices with their start and end apart: 3, of which 2 were waited for; matrix products, arithmetic and copies ran while one was open for 1% of the time, Pallas kernels for 3%

profile of v4, /device:TPU:1, one launch (start us, length us, event | category | flops | bytes accessed | tf_op | source)
XLA Modules:
  0.0 112.7 jit_solution(11234843907950523509)
XLA Ops:
  0.0 2.3 %pack.1 = bf16[8,336,128]{2,1,0:T(8,128)(2,1)} custom-call(bf16[128,896]{1,0:T(8,128)(2,1)} %q_ref.3, bf16[128,896]{1,0:T(8,128)(2,1)} %k_ref.2, bf16[128,896]{1,0:T(8,128)(2,1)} %v_ref.2), custom_call_target="tpu_custom_call" | custom-call | tf_op jit(solution)/shard_map/pack/pallas_call | solution.py:186
  2.3 6.4 %all-to-all-start = ((bf16[8,336,128]{2,1,0:T(8,128)(2,1)}), bf16[8,336,128]{2,1,0:T(8,128)(2,1)S(1)}, u32[]{:S(2)}, u32[]{:S(2)}) async-start(bf16[8,336,128]{2,1,0:T(8,128)(2,1)} %pack.1), calls=%async_computation | async-start | bytes 1376256 | tf_op jit(solution)/shard_map/all_to_all | solution.py:194
  8.6 0.8 copy.13.routes_ref
  9.4 0.8 copy.14.gates_ref
  10.2 0.0 copy-start.2
  10.2 0.9 copy-done.2
  11.1 0.0 copy-start.3
  11.1 0.9 copy-done.3
  12.1 0.0 copy-start.4
  12.1 0.9 copy-done.4
  13.0 1.5 %fresh.1 = (f32[64,1024]{1,0:T(8,128)S(1)}, f32[64,1024]{1,0:T(8,128)S(1)}, bf16[2,64,256]{2,1,0:T(8,128)(2,1)S(1)}, f32[64,2]{1,0:T(8,128)S(1)}) custom-call(s32[1]{0:T(128)} %bitcast.core_ref, bf16[128,896]{1,0:T(8,128)(2,1)S(1)} %copy-done.2, bf16[128,896]{1,0:T(8,128)(2,1)S(1)} %copy-done.3, bf16[128,896]{1,0:T(8,128)(2,1)S(1)} %copy-done.4, ...), custom_call_target="tpu_custom_call" | custom-call | flops 5000000000 | bytes 2000000 | tf_op jit(solution)/shard_map/fresh/pallas_call | solution.py:197
  14.5 0.0 copy-start.5
  14.5 0.0 copy-start.6
  14.5 1.0 collective-permute-start
  15.5 0.1 collective-permute-start.1
  15.6 1.1 collective-permute-done.fresh_ref.other_ref
  16.7 8.8 %all-to-all-done.in_ref = bf16[8,336,128]{2,1,0:T(8,128)(2,1)S(1)} async-done(((bf16[8,336,128]{2,1,0:T(8,128)(2,1)}), bf16[8,336,128]{2,1,0:T(8,128)(2,1)S(1)}, u32[]{:S(2)}, u32[]{:S(2)}) %all-to-all-start) | async-done | bytes 688160 | tf_op jit(solution)/shard_map/all_to_all | solution.py:194
  25.4 1.7 %attend.1 = bf16[16,64,128]{2,1,0:T(8,128)(2,1)S(1)} custom-call(bf16[8,336,128]{2,1,0:T(8,128)(2,1)S(1)} %all-to-all-done.in_ref, f32[64,1024]{1,0:T(8,128)S(1)} %collective-permute-done.fresh_ref.other_ref), custom_call_target="tpu_custom_call" | custom-call | flops 99999997952 | bytes 2000000 | tf_op jit(solution)/shard_map/attend/pallas_call | solution.py:212
  27.1 15.1 %all_to_all.20 = bf16[16,64,128]{2,1,0:T(8,128)(2,1)S(1)} all-to-all(bf16[16,64,128]{2,1,0:T(8,128)(2,1)S(1)} %attend.1), channel_id=1, replica_groups=mesh['group'=2,'patch'=8,'expert'=2] {'patch','expert'}, dimensions={0} | all-to-all | bytes 524288 | tf_op jit(solution)/shard_map/all_to_all | solution.py:221
  42.2 0.0 collective-permute-done.1.w_other_ref
  42.2 0.0 copy-done.5
  42.2 0.0 copy-done.6
  42.3 7.7 %home.1 = (f32[64,1792]{1,0:T(8,128)S(1)}, bf16[64,1792]{1,0:T(8,128)(2,1)S(1)}) custom-call(s32[1]{0:T(128)} %bitcast.core_ref, bf16[8,2,64,128]{3,2,1,0:T(8,128)(2,1)S(1)} %bitcast.10, f32[64,1024]{1,0:T(8,128)S(1)} %get-tuple-element.12.own_ref, f32[64,1024]{1,0:T(8,128)S(1)} %collective-permute-done.fresh_ref.other_ref, bf16[896,1792]{1,0:T(8,128)(2,1)} %w_own_ref.1, ...), custom_call_target="tpu_custom_call" | custom-call | flops 4000000000 | bytes 8000000 | tf_op jit(solution)/shard_map/home/pallas_call | solution.py:222
  50.0 0.0 copy-start
  50.0 0.0 copy-start.1
  50.0 0.4 slots.1
  50.4 26.6 %all_to_all.21 = bf16[16,16,1792]{2,1,0:T(8,128)(2,1)S(1)} all-to-all(bf16[16,16,1792]{2,1,0:T(8,128)(2,1)S(1)} %bitcast.9), channel_id=1, replica_groups=mesh['group'=2,'patch'=8,'expert'=2] {'patch','expert'}, dimensions={0} | all-to-all | bytes 1835008 | tf_op jit(solution)/shard_map/all_to_all | solution.py:357
  77.0 0.0 copy-done
  77.0 0.0 copy-done.1
  77.0 7.9 %experts.1 = bf16[256,1792]{1,0:T(8,128)(2,1)S(1)} custom-call(bf16[256,1792]{1,0:T(8,128)(2,1)S(1)} %bitcast.7, bf16[1,1792,3584]{2,1,0:T(8,128)(2,1)S(1)} %copy-done, bf16[1,3584,1792]{2,1,0:T(8,128)(2,1)S(1)} %copy-done.1), custom_call_target="tpu_custom_call" | custom-call | tf_op jit(solution)/shard_map/experts/pallas_call | solution.py:318
  84.9 26.7 %all_to_all.22 = bf16[16,16,1792]{2,1,0:T(8,128)(2,1)S(1)} all-to-all(bf16[16,16,1792]{2,1,0:T(8,128)(2,1)S(1)} %bitcast.8), channel_id=1, replica_groups=mesh['group'=2,'patch'=8,'expert'=2] {'patch','expert'}, dimensions={0} | all-to-all | bytes 1835008 | tf_op jit(solution)/shard_map/all_to_all | solution.py:359
  111.6 1.1 %combine.1 = bf16[64,1792]{1,0:T(8,128)(2,1)} custom-call(f32[64,1792]{1,0:T(8,128)S(1)} %get-tuple-element.13.hidden_ref, bf16[2,64,256]{2,1,0:T(8,128)(2,1)S(1)} %get-tuple-element.14.picks_ref, f32[64,2]{1,0:T(8,128)S(1)} %get-tuple-element.15.gates_ref, bf16[16,1,16,1792]{3,2,1,0:T(8,128)(2,1)S(1)} %bitcast.6), custom_call_target="tpu_custom_call" | custom-call | tf_op jit(solution)/shard_map/combine/pallas_call | solution.py:366
Async XLA Ops:
  2.3 23.2 %all-to-all-start = ((bf16[8,336,128]{2,1,0:T(8,128)(2,1)}), bf16[8,336,128]{2,1,0:T(8,128)(2,1)S(1)}, u32[]{:S(2)}, u32[]{:S(2)}) async-start(bf16[8,336,128]{2,1,0:T(8,128)(2,1)} %pack.1), calls=%async_computation | async-start | bytes 1376256 | tf_op jit(solution)/shard_map/all_to_all | solution.py:194
  10.2 0.9 copy-start.2
  11.1 0.9 copy-start.3
  12.1 0.9 copy-start.4
  14.5 27.8 %copy-start.5 = (bf16[64,1792]{1,0:T(8,128)(2,1)S(1)}, bf16[64,1792]{1,0:T(8,128)(2,1)}, u32[]{:S(2)}) copy-start(bf16[64,1792]{1,0:T(8,128)(2,1)} %residual_ref.1) | copy-start | bytes 688132
  14.5 27.8 %copy-start.6 = (f32[2,1792]{1,0:T(2,128)S(1)}, f32[2,1792]{1,0:T(2,128)}, u32[]{:S(2)}) copy-start(f32[2,1792]{1,0:T(2,128)} %modulation_ref.1) | copy-start | bytes 43012
  14.5 2.2 %collective-permute-start = (f32[64,1024]{1,0:T(8,128)S(1)}, f32[64,1024]{1,0:T(8,128)S(1)}, u32[]{:S(2)}, u32[]{:S(2)}) collective-permute-start(f32[64,1024]{1,0:T(8,128)S(1)} %get-tuple-element.11), channel_id=1, source_target_pairs={{0,1},{1,0},{2,3},{3,2},{4,5},{5,4},{6,7},{7,6},{8,9},{9,8},{10,11... | collective-permute-start | bytes 786440 | tf_op jit(solution)/shard_map/ppermute | solution.py:211
  15.5 26.7 %collective-permute-start.1 = (bf16[896,1792]{1,0:T(8,128)(2,1)}, bf16[896,1792]{1,0:T(8,128)(2,1)}, u32[]{:S(2)}, u32[]{:S(2)}) collective-permute-start(bf16[896,1792]{1,0:T(8,128)(2,1)} %w_own_ref.1), channel_id=1, source_target_pairs={{0,1},{1,0},{2,3},{3,2},{4,5},{5,4},{6,7},{7,6},{8,9},{9,8},{10,11... | collective-permute-start | bytes 9633800 | tf_op jit(solution)/shard_map/ppermute | solution.py:193
  50.0 27.0 %copy-start = (bf16[1,1792,3584]{2,1,0:T(8,128)(2,1)S(1)}, bf16[1,1792,3584]{2,1,0:T(8,128)(2,1)}, u32[]{:S(2)}) copy-start(bf16[1,1792,3584]{2,1,0:T(8,128)(2,1)} %up_ref.1) | copy-start | bytes 38535172
  50.0 27.0 %copy-start.1 = (bf16[1,3584,1792]{2,1,0:T(8,128)(2,1)S(1)}, bf16[1,3584,1792]{2,1,0:T(8,128)(2,1)}, u32[]{:S(2)}) copy-start(bf16[1,3584,1792]{2,1,0:T(8,128)(2,1)} %down_ref.1) | copy-start | bytes 38535172

commit v5 on v4

--- a/solution.py
+++ b/solution.py
@@ -133,11 +133,18 @@
     core_ref, far_ref, own_ref, other_ref, w_own_ref, w_other_ref, residual_ref, modulation_ref,
     hidden_ref, normed_ref, attended_ref, w_ref, loaded_ref,
 ):
+    parts = loaded_ref.shape[1]
+    share = w_own_ref.shape[0] // parts
     loads = [
-        pltpu.make_async_copy(source, w_ref.at[i], loaded_ref.at[i])
+        [
+            pltpu.make_async_copy(
+                source.at[pl.ds(j * share, share)], w_ref.at[i, pl.ds(j * share, share)], loaded_ref.at[i, j]
+            )
+            for j in range(parts)
+        ]
         for i, source in enumerate((w_own_ref, w_other_ref))
     ]
-    for load in loads:
+    for load in loads[0] + loads[1]:
         load.start()
     heads = far_ref.shape[0]
     core = core_ref[0]
@@ -161,7 +168,8 @@
             merged = far * (far_weight * scale) + near * (near_weight * scale)
             attended_ref[side, :, h * HEAD_DIM : (h + 1) * HEAD_DIM] = merged[:, :HEAD_DIM].astype(BF16)
     for side in range(2):
-        loads[side].wait()
+        for load in loads[side]:
+            load.wait()
         part = jnp.dot(attended_ref[side], w_ref[side], preferred_element_type=F32)
         projected = part if projected is None else projected + part
     hidden = residual_ref[...].astype(F32) + projected
@@ -230,7 +238,7 @@
         scratch_shapes=[
             pltpu.VMEM((2, rows, width), BF16),
             pltpu.VMEM((2,) + out_weight.shape, BF16),
-            pltpu.SemaphoreType.DMA((2,)),
+            pltpu.SemaphoreType.DMA((2, 7)),
         ],
         compiler_params=pltpu.CompilerParams(vmem_limit_bytes=20 << 20),
         cost_estimate=pl.CostEstimate(flops=4_000_000_000, bytes_accessed=8_000_000, transcendentals=100_000),

time: 113 us -> 114 us (level)
  no operation moved by 1% of the time
where the time goes in v5:
time: 114 us
  blocking collectives  68.4 us (60%)
  Pallas kernels  23.6 us (21%)
  waiting for transfers between devices  9.85 us (9%)
  starting transfers between devices  7.48 us (7%)
  local copies, waits for them, and re-layouts  4.37 us (4%)
    all_to_all x1, blocking collectives, body(): lax.all_to_all(outputs.reshape(device_count, capacity, features), ('patch...  26.7 us
    all_to_all x1, blocking collectives, body(): lax.all_to_all(outgoing, ('patch', 'expert'), split_axis=0, concat_axis=0...  26.6 us
    all_to_all x1, blocking collectives, attention_by_heads(): lax.all_to_all(stale, ('patch', 'expert'), split_axis=0, concat_axis=0, t...  15.1 us
    all_to_all x1, waiting for transfers between devices, attention_by_heads(): lax.all_to_all(packed, 'patch', split_axis=0, concat_axis=0, tiled=True)  8.76 us
    pallas_call x1, Pallas kernels, attention_by_heads(): pl.pallas_call(home_kernel, out_shape=(jax.ShapeDtypeStruct((rows, featur...  8.73 us
    pallas_call x1, Pallas kernels, expert_slice(): pl.pallas_call(expert_kernel, out_shape=jax.ShapeDtypeStruct((rows, featu...  7.86 us
    all_to_all x1, starting transfers between devices, attention_by_heads(): lax.all_to_all(packed, 'patch', split_axis=0, concat_axis=0, tiled=True)  6.38 us
    unnamed x16, local copies, waits for them, and re-layouts  4.37 us
  transfers between devices with their start and end apart: 3, of which 2 were waited for; matrix products, arithmetic and copies ran while one was open for 1% of the time, Pallas kernels for 3%

profile of v5, /device:TPU:1, one launch (start us, length us, event | category | flops | bytes accessed | tf_op | source)
XLA Modules:
  0.0 113.7 jit_solution(14186541191946802628)
XLA Ops:
  0.0 2.3 %pack.1 = bf16[8,336,128]{2,1,0:T(8,128)(2,1)} custom-call(bf16[128,896]{1,0:T(8,128)(2,1)} %q_ref.3, bf16[128,896]{1,0:T(8,128)(2,1)} %k_ref.2, bf16[128,896]{1,0:T(8,128)(2,1)} %v_ref.2), custom_call_target="tpu_custom_call" | custom-call | tf_op jit(solution)/shard_map/pack/pallas_call | solution.py:194
  2.3 6.4 %all-to-all-start = ((bf16[8,336,128]{2,1,0:T(8,128)(2,1)}), bf16[8,336,128]{2,1,0:T(8,128)(2,1)S(1)}, u32[]{:S(2)}, u32[]{:S(2)}) async-start(bf16[8,336,128]{2,1,0:T(8,128)(2,1)} %pack.1), calls=%async_computation | async-start | bytes 1376256 | tf_op jit(solution)/shard_map/all_to_all | solution.py:202
  8.6 0.8 copy.13.routes_ref
  9.4 0.8 copy.14.gates_ref
  10.2 0.0 copy-start.2
  10.2 0.9 copy-done.2
  11.1 0.0 copy-start.3
  11.1 0.9 copy-done.3
  12.1 0.0 copy-start.4
  12.1 0.9 copy-done.4
  13.0 1.5 %fresh.1 = (f32[64,1024]{1,0:T(8,128)S(1)}, f32[64,1024]{1,0:T(8,128)S(1)}, bf16[2,64,256]{2,1,0:T(8,128)(2,1)S(1)}, f32[64,2]{1,0:T(8,128)S(1)}) custom-call(s32[1]{0:T(128)} %bitcast.core_ref, bf16[128,896]{1,0:T(8,128)(2,1)S(1)} %copy-done.2, bf16[128,896]{1,0:T(8,128)(2,1)S(1)} %copy-done.3, bf16[128,896]{1,0:T(8,128)(2,1)S(1)} %copy-done.4, ...), custom_call_target="tpu_custom_call" | custom-call | flops 5000000000 | bytes 2000000 | tf_op jit(solution)/shard_map/fresh/pallas_call | solution.py:205
  14.5 0.0 copy-start.5
  14.5 0.0 copy-start.6
  14.5 1.0 collective-permute-start
  15.5 0.1 collective-permute-start.1
  15.6 1.1 collective-permute-done.fresh_ref.other_ref
  16.7 8.8 %all-to-all-done.in_ref = bf16[8,336,128]{2,1,0:T(8,128)(2,1)S(1)} async-done(((bf16[8,336,128]{2,1,0:T(8,128)(2,1)}), bf16[8,336,128]{2,1,0:T(8,128)(2,1)S(1)}, u32[]{:S(2)}, u32[]{:S(2)}) %all-to-all-start) | async-done | bytes 688160 | tf_op jit(solution)/shard_map/all_to_all | solution.py:202
  25.4 1.7 %attend.1 = bf16[16,64,128]{2,1,0:T(8,128)(2,1)S(1)} custom-call(bf16[8,336,128]{2,1,0:T(8,128)(2,1)S(1)} %all-to-all-done.in_ref, f32[64,1024]{1,0:T(8,128)S(1)} %collective-permute-done.fresh_ref.other_ref), custom_call_target="tpu_custom_call" | custom-call | flops 99999997952 | bytes 2000000 | tf_op jit(solution)/shard_map/attend/pallas_call | solution.py:220
  27.1 15.1 %all_to_all.20 = bf16[16,64,128]{2,1,0:T(8,128)(2,1)S(1)} all-to-all(bf16[16,64,128]{2,1,0:T(8,128)(2,1)S(1)} %attend.1), channel_id=1, replica_groups=mesh['group'=2,'patch'=8,'expert'=2] {'patch','expert'}, dimensions={0} | all-to-all | bytes 524288 | tf_op jit(solution)/shard_map/all_to_all | solution.py:229
  42.2 0.0 collective-permute-done.1.w_other_ref
  42.2 0.0 copy-done.5
  42.2 0.0 copy-done.6
  42.3 8.7 %home.1 = (f32[64,1792]{1,0:T(8,128)S(1)}, bf16[64,1792]{1,0:T(8,128)(2,1)S(1)}) custom-call(s32[1]{0:T(128)} %bitcast.core_ref, bf16[8,2,64,128]{3,2,1,0:T(8,128)(2,1)S(1)} %bitcast.10, f32[64,1024]{1,0:T(8,128)S(1)} %get-tuple-element.12.own_ref, f32[64,1024]{1,0:T(8,128)S(1)} %collective-permute-done.fresh_ref.other_ref, bf16[896,1792]{1,0:T(8,128)(2,1)} %w_own_ref.1, ...), custom_call_target="tpu_custom_call" | custom-call | flops 4000000000 | bytes 8000000 | tf_op jit(solution)/shard_map/home/pallas_call | solution.py:230
  51.0 0.0 copy-start
  51.0 0.0 copy-start.1
  51.0 0.4 slots.1
  51.4 26.6 %all_to_all.21 = bf16[16,16,1792]{2,1,0:T(8,128)(2,1)S(1)} all-to-all(bf16[16,16,1792]{2,1,0:T(8,128)(2,1)S(1)} %bitcast.9), channel_id=1, replica_groups=mesh['group'=2,'patch'=8,'expert'=2] {'patch','expert'}, dimensions={0} | all-to-all | bytes 1835008 | tf_op jit(solution)/shard_map/all_to_all | solution.py:365
  78.0 0.0 copy-done
  78.0 0.0 copy-done.1
  78.0 7.9 %experts.1 = bf16[256,1792]{1,0:T(8,128)(2,1)S(1)} custom-call(bf16[256,1792]{1,0:T(8,128)(2,1)S(1)} %bitcast.7, bf16[1,1792,3584]{2,1,0:T(8,128)(2,1)S(1)} %copy-done, bf16[1,3584,1792]{2,1,0:T(8,128)(2,1)S(1)} %copy-done.1), custom_call_target="tpu_custom_call" | custom-call | tf_op jit(solution)/shard_map/experts/pallas_call | solution.py:326
  85.9 26.7 %all_to_all.22 = bf16[16,16,1792]{2,1,0:T(8,128)(2,1)S(1)} all-to-all(bf16[16,16,1792]{2,1,0:T(8,128)(2,1)S(1)} %bitcast.8), channel_id=1, replica_groups=mesh['group'=2,'patch'=8,'expert'=2] {'patch','expert'}, dimensions={0} | all-to-all | bytes 1835008 | tf_op jit(solution)/shard_map/all_to_all | solution.py:367
  112.6 1.1 combine.1
Async XLA Ops:
  2.3 23.2 %all-to-all-start = ((bf16[8,336,128]{2,1,0:T(8,128)(2,1)}), bf16[8,336,128]{2,1,0:T(8,128)(2,1)S(1)}, u32[]{:S(2)}, u32[]{:S(2)}) async-start(bf16[8,336,128]{2,1,0:T(8,128)(2,1)} %pack.1), calls=%async_computation | async-start | bytes 1376256 | tf_op jit(solution)/shard_map/all_to_all | solution.py:202
  10.2 0.9 copy-start.2
  11.1 0.9 copy-start.3
  12.1 0.9 copy-start.4
  14.5 27.8 %copy-start.5 = (bf16[64,1792]{1,0:T(8,128)(2,1)S(1)}, bf16[64,1792]{1,0:T(8,128)(2,1)}, u32[]{:S(2)}) copy-start(bf16[64,1792]{1,0:T(8,128)(2,1)} %residual_ref.1) | copy-start | bytes 688132
  14.5 27.8 %copy-start.6 = (f32[2,1792]{1,0:T(2,128)S(1)}, f32[2,1792]{1,0:T(2,128)}, u32[]{:S(2)}) copy-start(f32[2,1792]{1,0:T(2,128)} %modulation_ref.1) | copy-start | bytes 43012
  14.5 2.2 %collective-permute-start = (f32[64,1024]{1,0:T(8,128)S(1)}, f32[64,1024]{1,0:T(8,128)S(1)}, u32[]{:S(2)}, u32[]{:S(2)}) collective-permute-start(f32[64,1024]{1,0:T(8,128)S(1)} %get-tuple-element.11), channel_id=1, source_target_pairs={{0,1},{1,0},{2,3},{3,2},{4,5},{5,4},{6,7},{7,6},{8,9},{9,8},{10,11... | collective-permute-start | bytes 786440 | tf_op jit(solution)/shard_map/ppermute | solution.py:219
  15.5 26.7 %collective-permute-start.1 = (bf16[896,1792]{1,0:T(8,128)(2,1)}, bf16[896,1792]{1,0:T(8,128)(2,1)}, u32[]{:S(2)}, u32[]{:S(2)}) collective-permute-start(bf16[896,1792]{1,0:T(8,128)(2,1)} %w_own_ref.1), channel_id=1, source_target_pairs={{0,1},{1,0},{2,3},{3,2},{4,5},{5,4},{6,7},{7,6},{8,9},{9,8},{10,11... | collective-permute-start | bytes 9633800 | tf_op jit(solution)/shard_map/ppermute | solution.py:201
  51.0 27.0 %copy-start = (bf16[1,1792,3584]{2,1,0:T(8,128)(2,1)S(1)}, bf16[1,1792,3584]{2,1,0:T(8,128)(2,1)}, u32[]{:S(2)}) copy-start(bf16[1,1792,3584]{2,1,0:T(8,128)(2,1)} %up_ref.1) | copy-start | bytes 38535172
  51.0 27.0 %copy-start.1 = (bf16[1,3584,1792]{2,1,0:T(8,128)(2,1)S(1)}, bf16[1,3584,1792]{2,1,0:T(8,128)(2,1)}, u32[]{:S(2)}) copy-start(bf16[1,3584,1792]{2,1,0:T(8,128)(2,1)} %down_ref.1) | copy-start | bytes 38535172

commit v6 on v4

--- a/solution.py
+++ b/solution.py
@@ -131,14 +131,8 @@
 
 def home_kernel(
     core_ref, far_ref, own_ref, other_ref, w_own_ref, w_other_ref, residual_ref, modulation_ref,
-    hidden_ref, normed_ref, attended_ref, w_ref, loaded_ref,
+    hidden_ref, normed_ref, attended_ref,
 ):
-    loads = [
-        pltpu.make_async_copy(source, w_ref.at[i], loaded_ref.at[i])
-        for i, source in enumerate((w_own_ref, w_other_ref))
-    ]
-    for load in loads:
-        load.start()
     heads = far_ref.shape[0]
     core = core_ref[0]
     projected = None
@@ -160,9 +154,8 @@
             scale = 1.0 / (far_weight + near_total * near_weight)
             merged = far * (far_weight * scale) + near * (near_weight * scale)
             attended_ref[side, :, h * HEAD_DIM : (h + 1) * HEAD_DIM] = merged[:, :HEAD_DIM].astype(BF16)
-    for side in range(2):
-        loads[side].wait()
-        part = jnp.dot(attended_ref[side], w_ref[side], preferred_element_type=F32)
+    for side, w_ref in enumerate((w_own_ref, w_other_ref)):
+        part = jnp.dot(attended_ref[side], w_ref[...], preferred_element_type=F32)
         projected = part if projected is None else projected + part
     hidden = residual_ref[...].astype(F32) + projected
     hidden_ref[...] = hidden
@@ -225,13 +218,9 @@
             jax.ShapeDtypeStruct((rows, features), F32),
             jax.ShapeDtypeStruct((rows, features), BF16),
         ),
-        in_specs=[SMEM] + [VMEM] * 3 + [ANY] * 2 + [VMEM] * 2,
+        in_specs=[SMEM] + [VMEM] * 7,
         out_specs=(VMEM, VMEM),
-        scratch_shapes=[
-            pltpu.VMEM((2, rows, width), BF16),
-            pltpu.VMEM((2,) + out_weight.shape, BF16),
-            pltpu.SemaphoreType.DMA((2,)),
-        ],
+        scratch_shapes=[pltpu.VMEM((2, rows, width), BF16)],
         compiler_params=pltpu.CompilerParams(vmem_limit_bytes=20 << 20),
         cost_estimate=pl.CostEstimate(flops=4_000_000_000, bytes_accessed=8_000_000, transcendentals=100_000),
         name="home",

time: 113 us -> 111 us (0.982)
  Pallas kernels: 22.6 us -> 20.4 us
    pallas_call x1, Pallas kernels: 7.71 us -> 5.56 us  [attention_by_heads(): pl.pallas_call(home_kernel, out_shape=(jax.ShapeDtypeStruct((rows, featur...]
where the time goes in v6:
time: 111 us
  blocking collectives  68.4 us (62%)
  Pallas kernels  20.4 us (18%)
  waiting for transfers between devices  9.85 us (9%)
  starting transfers between devices  7.48 us (7%)
  local copies, waits for them, and re-layouts  4.37 us (4%)
    all_to_all x1, blocking collectives, body(): lax.all_to_all(outputs.reshape(device_count, capacity, features), ('patch...  26.7 us
    all_to_all x1, blocking collectives, body(): lax.all_to_all(outgoing, ('patch', 'expert'), split_axis=0, concat_axis=0...  26.6 us
    all_to_all x1, blocking collectives, attention_by_heads(): lax.all_to_all(stale, ('patch', 'expert'), split_axis=0, concat_axis=0, t...  15.1 us
    all_to_all x1, waiting for transfers between devices, attention_by_heads(): lax.all_to_all(packed, 'patch', split_axis=0, concat_axis=0, tiled=True)  8.76 us
    pallas_call x1, Pallas kernels, expert_slice(): pl.pallas_call(expert_kernel, out_shape=jax.ShapeDtypeStruct((rows, featu...  7.85 us
    all_to_all x1, starting transfers between devices, attention_by_heads(): lax.all_to_all(packed, 'patch', split_axis=0, concat_axis=0, tiled=True)  6.38 us
    pallas_call x1, Pallas kernels, attention_by_heads(): pl.pallas_call(home_kernel, out_shape=(jax.ShapeDtypeStruct((rows, featur...  5.56 us
    unnamed x16, local copies, waits for them, and re-layouts  4.37 us
  transfers between devices with their start and end apart: 3, of which 2 were waited for; matrix products, arithmetic and copies ran while one was open for 1% of the time, Pallas kernels for 3%

profile of v6, /device:TPU:1, one launch (start us, length us, event | category | flops | bytes accessed | tf_op | source)
XLA Modules:
  0.0 110.6 jit_solution(12056767538836243358)
XLA Ops:
  0.0 2.3 %pack.1 = bf16[8,336,128]{2,1,0:T(8,128)(2,1)} custom-call(bf16[128,896]{1,0:T(8,128)(2,1)} %q_ref.3, bf16[128,896]{1,0:T(8,128)(2,1)} %k_ref.2, bf16[128,896]{1,0:T(8,128)(2,1)} %v_ref.2), custom_call_target="tpu_custom_call" | custom-call | tf_op jit(solution)/shard_map/pack/pallas_call | solution.py:179
  2.3 6.4 %all-to-all-start = ((bf16[8,336,128]{2,1,0:T(8,128)(2,1)}), bf16[8,336,128]{2,1,0:T(8,128)(2,1)S(1)}, u32[]{:S(2)}, u32[]{:S(2)}) async-start(bf16[8,336,128]{2,1,0:T(8,128)(2,1)} %pack.1), calls=%async_computation | async-start | bytes 1376256 | tf_op jit(solution)/shard_map/all_to_all | solution.py:187
  8.6 0.8 copy.13.routes_ref
  9.4 0.8 copy.14.gates_ref
  10.2 0.0 copy-start.2
  10.2 0.9 copy-done.2
  11.1 0.0 copy-start.3
  11.1 0.9 copy-done.3
  12.1 0.0 copy-start.4
  12.1 0.9 copy-done.4
  13.0 1.5 %fresh.1 = (f32[64,1024]{1,0:T(8,128)S(1)}, f32[64,1024]{1,0:T(8,128)S(1)}, bf16[2,64,256]{2,1,0:T(8,128)(2,1)S(1)}, f32[64,2]{1,0:T(8,128)S(1)}) custom-call(s32[1]{0:T(128)} %bitcast.core_ref, bf16[128,896]{1,0:T(8,128)(2,1)S(1)} %copy-done.2, bf16[128,896]{1,0:T(8,128)(2,1)S(1)} %copy-done.3, bf16[128,896]{1,0:T(8,128)(2,1)S(1)} %copy-done.4, ...), custom_call_target="tpu_custom_call" | custom-call | flops 5000000000 | bytes 2000000 | tf_op jit(solution)/shard_map/fresh/pallas_call | solution.py:190
  14.5 0.0 copy-start.5
  14.5 0.0 copy-start.6
  14.5 1.0 collective-permute-start
  15.5 0.1 collective-permute-start.1
  15.6 1.1 collective-permute-done.fresh_ref.other_ref
  16.7 8.8 %all-to-all-done.in_ref = bf16[8,336,128]{2,1,0:T(8,128)(2,1)S(1)} async-done(((bf16[8,336,128]{2,1,0:T(8,128)(2,1)}), bf16[8,336,128]{2,1,0:T(8,128)(2,1)S(1)}, u32[]{:S(2)}, u32[]{:S(2)}) %all-to-all-start) | async-done | bytes 688160 | tf_op jit(solution)/shard_map/all_to_all | solution.py:187
  25.4 1.7 %attend.1 = bf16[16,64,128]{2,1,0:T(8,128)(2,1)S(1)} custom-call(bf16[8,336,128]{2,1,0:T(8,128)(2,1)S(1)} %all-to-all-done.in_ref, f32[64,1024]{1,0:T(8,128)S(1)} %collective-permute-done.fresh_ref.other_ref), custom_call_target="tpu_custom_call" | custom-call | flops 99999997952 | bytes 2000000 | tf_op jit(solution)/shard_map/attend/pallas_call | solution.py:205
  27.1 15.1 %all_to_all.20 = bf16[16,64,128]{2,1,0:T(8,128)(2,1)S(1)} all-to-all(bf16[16,64,128]{2,1,0:T(8,128)(2,1)S(1)} %attend.1), channel_id=1, replica_groups=mesh['group'=2,'patch'=8,'expert'=2] {'patch','expert'}, dimensions={0} | all-to-all | bytes 524288 | tf_op jit(solution)/shard_map/all_to_all | solution.py:214
  42.2 0.0 collective-permute-done.1.w_other_ref
  42.2 0.0 copy-done.5
  42.2 0.0 copy-done.6
  42.3 5.6 %home.1 = (f32[64,1792]{1,0:T(8,128)S(1)}, bf16[64,1792]{1,0:T(8,128)(2,1)S(1)}) custom-call(s32[1]{0:T(128)} %bitcast.core_ref, bf16[8,2,64,128]{3,2,1,0:T(8,128)(2,1)S(1)} %bitcast.10, f32[64,1024]{1,0:T(8,128)S(1)} %get-tuple-element.12.own_ref, f32[64,1024]{1,0:T(8,128)S(1)} %collective-permute-done.fresh_ref.other_ref, bf16[896,1792]{1,0:T(8,128)(2,1)} %w_own_ref.1, ...), custom_call_target="tpu_custom_call" | custom-call | flops 4000000000 | bytes 8000000 | tf_op jit(solution)/shard_map/home/pallas_call | solution.py:215
  47.8 0.0 copy-start
  47.8 0.0 copy-start.1
  47.8 0.4 slots.1
  48.3 26.6 %all_to_all.21 = bf16[16,16,1792]{2,1,0:T(8,128)(2,1)S(1)} all-to-all(bf16[16,16,1792]{2,1,0:T(8,128)(2,1)S(1)} %bitcast.9), channel_id=1, replica_groups=mesh['group'=2,'patch'=8,'expert'=2] {'patch','expert'}, dimensions={0} | all-to-all | bytes 1835008 | tf_op jit(solution)/shard_map/all_to_all | solution.py:346
  74.8 0.0 copy-done
  74.8 0.0 copy-done.1
  74.9 7.9 %experts.1 = bf16[256,1792]{1,0:T(8,128)(2,1)S(1)} custom-call(bf16[256,1792]{1,0:T(8,128)(2,1)S(1)} %bitcast.7, bf16[1,1792,3584]{2,1,0:T(8,128)(2,1)S(1)} %copy-done, bf16[1,3584,1792]{2,1,0:T(8,128)(2,1)S(1)} %copy-done.1), custom_call_target="tpu_custom_call" | custom-call | tf_op jit(solution)/shard_map/experts/pallas_call | solution.py:307
  82.7 26.7 %all_to_all.22 = bf16[16,16,1792]{2,1,0:T(8,128)(2,1)S(1)} all-to-all(bf16[16,16,1792]{2,1,0:T(8,128)(2,1)S(1)} %bitcast.8), channel_id=1, replica_groups=mesh['group'=2,'patch'=8,'expert'=2] {'patch','expert'}, dimensions={0} | all-to-all | bytes 1835008 | tf_op jit(solution)/shard_map/all_to_all | solution.py:348
  109.4 1.1 %combine.1 = bf16[64,1792]{1,0:T(8,128)(2,1)} custom-call(f32[64,1792]{1,0:T(8,128)S(1)} %get-tuple-element.13.hidden_ref, bf16[2,64,256]{2,1,0:T(8,128)(2,1)S(1)} %get-tuple-element.14.picks_ref, f32[64,2]{1,0:T(8,128)S(1)} %get-tuple-element.15.gates_ref, bf16[16,1,16,1792]{3,2,1,0:T(8,128)(2,1)S(1)} %bitcast.6), custom_call_target="tpu_custom_call" | custom-call | tf_op jit(solution)/shard_map/combine/pallas_call | solution.py:355
Async XLA Ops:
  2.3 23.2 %all-to-all-start = ((bf16[8,336,128]{2,1,0:T(8,128)(2,1)}), bf16[8,336,128]{2,1,0:T(8,128)(2,1)S(1)}, u32[]{:S(2)}, u32[]{:S(2)}) async-start(bf16[8,336,128]{2,1,0:T(8,128)(2,1)} %pack.1), calls=%async_computation | async-start | bytes 1376256 | tf_op jit(solution)/shard_map/all_to_all | solution.py:187
  10.2 0.9 copy-start.2
  11.1 0.9 copy-start.3
  12.1 0.9 copy-start.4
  14.5 27.8 %copy-start.5 = (bf16[64,1792]{1,0:T(8,128)(2,1)S(1)}, bf16[64,1792]{1,0:T(8,128)(2,1)}, u32[]{:S(2)}) copy-start(bf16[64,1792]{1,0:T(8,128)(2,1)} %residual_ref.1) | copy-start | bytes 688132
  14.5 27.8 %copy-start.6 = (f32[2,1792]{1,0:T(2,128)S(1)}, f32[2,1792]{1,0:T(2,128)}, u32[]{:S(2)}) copy-start(f32[2,1792]{1,0:T(2,128)} %modulation_ref.1) | copy-start | bytes 43012
  14.5 2.2 %collective-permute-start = (f32[64,1024]{1,0:T(8,128)S(1)}, f32[64,1024]{1,0:T(8,128)S(1)}, u32[]{:S(2)}, u32[]{:S(2)}) collective-permute-start(f32[64,1024]{1,0:T(8,128)S(1)} %get-tuple-element.11), channel_id=1, source_target_pairs={{0,1},{1,0},{2,3},{3,2},{4,5},{5,4},{6,7},{7,6},{8,9},{9,8},{10,11... | collective-permute-start | bytes 786440 | tf_op jit(solution)/shard_map/ppermute | solution.py:204
  15.5 26.7 %collective-permute-start.1 = (bf16[896,1792]{1,0:T(8,128)(2,1)}, bf16[896,1792]{1,0:T(8,128)(2,1)}, u32[]{:S(2)}, u32[]{:S(2)}) collective-permute-start(bf16[896,1792]{1,0:T(8,128)(2,1)} %w_own_ref.1), channel_id=1, source_target_pairs={{0,1},{1,0},{2,3},{3,2},{4,5},{5,4},{6,7},{7,6},{8,9},{9,8},{10,11... | collective-permute-start | bytes 9633800 | tf_op jit(solution)/shard_map/ppermute | solution.py:186
  47.8 27.0 %copy-start = (bf16[1,1792,3584]{2,1,0:T(8,128)(2,1)S(1)}, bf16[1,1792,3584]{2,1,0:T(8,128)(2,1)}, u32[]{:S(2)}) copy-start(bf16[1,1792,3584]{2,1,0:T(8,128)(2,1)} %up_ref.1) | copy-start | bytes 38535172
  47.8 27.0 %copy-start.1 = (bf16[1,3584,1792]{2,1,0:T(8,128)(2,1)S(1)}, bf16[1,3584,1792]{2,1,0:T(8,128)(2,1)}, u32[]{:S(2)}) copy-start(bf16[1,3584,1792]{2,1,0:T(8,128)(2,1)} %down_ref.1) | copy-start | bytes 38535172

commit v7 on v6

--- a/solution.py
+++ b/solution.py
@@ -45,8 +45,19 @@
 
 
 def fresh_kernel(
-    core_ref, q_ref, k_ref, v_ref, routes_ref, gates_ref, own_ref, other_ref, picks_ref, gates_out_ref
+    core_ref, q_ref, k_ref, v_ref, routes_ref, gates_ref, w_own_ref, w_other_ref,
+    own_ref, other_ref, picks_ref, gates_out_ref, w_ref, done_ref,
 ):
+    share = w_own_ref.shape[0] // 2
+    copies = [
+        pltpu.make_async_copy(
+            source.at[pl.ds(j * share, share)], w_ref.at[i, pl.ds(j * share, share)], done_ref.at[i, j]
+        )
+        for i, source in enumerate((w_own_ref, w_other_ref))
+        for j in range(2)
+    ]
+    for copy in copies:
+        copy.start()
     q, k, v = q_ref[...].T, k_ref[...].T, v_ref[...].T
     half = q.shape[1] // 2
     first = core_ref[0] == 0
@@ -62,6 +73,8 @@
     for k, slot in enumerate(slots_of(routes_ref[...], slots // EXPERTS)):
         picks_ref[k] = chosen(slot, slots)
     gates_out_ref[...] = gates_ref[...]
+    for copy in copies:
+        copy.wait()
 
 
 def attend_kernel(in_ref, fresh_ref, out_ref):
@@ -130,7 +143,7 @@
 
 
 def home_kernel(
-    core_ref, far_ref, own_ref, other_ref, w_own_ref, w_other_ref, residual_ref, modulation_ref,
+    core_ref, far_ref, own_ref, other_ref, w_ref, residual_ref, modulation_ref,
     hidden_ref, normed_ref, attended_ref,
 ):
     heads = far_ref.shape[0]
@@ -154,8 +167,8 @@
             scale = 1.0 / (far_weight + near_total * near_weight)
             merged = far * (far_weight * scale) + near * (near_weight * scale)
             attended_ref[side, :, h * HEAD_DIM : (h + 1) * HEAD_DIM] = merged[:, :HEAD_DIM].astype(BF16)
-    for side, w_ref in enumerate((w_own_ref, w_other_ref)):
-        part = jnp.dot(attended_ref[side], w_ref[...], preferred_element_type=F32)
+    for side in range(2):
+        part = jnp.dot(attended_ref[side], w_ref[side], preferred_element_type=F32)
         projected = part if projected is None else projected + part
     hidden = residual_ref[...].astype(F32) + projected
     hidden_ref[...] = hidden
@@ -187,20 +200,22 @@
     gathered = lax.all_to_all(packed, "patch", split_axis=0, concat_axis=0, tiled=True)
     fresh_shape = jax.ShapeDtypeStruct((tokens // 2, heads * LANES), F32)
     slots = EXPERTS * (rows // 4)
-    fresh_own, fresh_away, picks, gates = pl.pallas_call(
+    fresh_own, fresh_away, picks, gates, weights = pl.pallas_call(
         fresh_kernel,
         out_shape=(
             fresh_shape,
             fresh_shape,
             jax.ShapeDtypeStruct((TOPK, rows, slots), BF16),
             jax.ShapeDtypeStruct(gates.shape, F32),
+            jax.ShapeDtypeStruct((2,) + out_weight.shape, BF16),
         ),
-        in_specs=[SMEM] + [VMEM] * 5,
-        out_specs=(VMEM,) * 4,
+        in_specs=[SMEM] + [VMEM] * 5 + [ANY] * 2,
+        out_specs=(VMEM,) * 4 + (ANY,),
+        scratch_shapes=[pltpu.SemaphoreType.DMA((2, 2))],
         compiler_params=pltpu.CompilerParams(vmem_limit_bytes=16 << 20),
         cost_estimate=pl.CostEstimate(flops=5_000_000_000, bytes_accessed=2_000_000, transcendentals=200_000),
         name="fresh",
-    )(core, queries, fresh_keys, fresh_values, routes, gates)
+    )(core, queries, fresh_keys, fresh_values, routes, gates, out_weight, w_other)
     fresh_other = lax.ppermute(fresh_away, "expert", swap)
     stale = pl.pallas_call(
         attend_kernel,
@@ -218,20 +233,20 @@
             jax.ShapeDtypeStruct((rows, features), F32),
             jax.ShapeDtypeStruct((rows, features), BF16),
         ),
-        in_specs=[SMEM] + [VMEM] * 7,
+        in_specs=[SMEM] + [VMEM] * 6,
         out_specs=(VMEM, VMEM),
         scratch_shapes=[pltpu.VMEM((2, rows, width), BF16)],
         compiler_params=pltpu.CompilerParams(vmem_limit_bytes=20 << 20),
         cost_estimate=pl.CostEstimate(flops=4_000_000_000, bytes_accessed=8_000_000, transcendentals=100_000),
         name="home",
-    )(core, far.reshape(heads, 2, rows, LANES), fresh_own, fresh_other, out_weight, w_other, residual, modulation)
+    )(core, far.reshape(heads, 2, rows, LANES), fresh_own, fresh_other, weights, residual, modulation)
     buffer = pl.pallas_call(
         slots_kernel,
         out_shape=jax.ShapeDtypeStruct((slots, features), BF16),
         in_specs=[VMEM] * 2,
         out_specs=VMEM,
         compiler_params=pltpu.CompilerParams(vmem_limit_bytes=12 << 20),
-        cost_estimate=pl.CostEstimate(flops=200_000_000_000, bytes_accessed=8_000_000, transcendentals=100_000),
+        cost_estimate=pl.CostEstimate(flops=100_000_000_000, bytes_accessed=8_000_000, transcendentals=100_000),
         name="slots",
     )(normed, picks)
     return hidden, buffer, picks, gates

time: 111 us -> 109 us (0.982)
  local copies, waits for them, and re-layouts: 4.37 us -> 8.97 us
  waiting for transfers between devices: 9.85 us -> 6.37 us
  Pallas kernels: 20.4 us -> 18.3 us
    unnamed x16 -> x34, local copies, waits for them, and re-layouts: 4.37 us -> 8.97 us
    pallas_call x1, Pallas kernels: 5.56 us -> 2.67 us  [attention_by_heads(): pl.pallas_call(home_kernel, out_shape=(jax.ShapeDtypeStruct((rows, featur...]
    all_to_all x1, waiting for transfers between devices: 8.76 us -> 6.36 us  [attention_by_heads(): lax.all_to_all(packed, 'patch', split_axis=0, concat_axis=0, tiled=True)]
  transfers between devices with their start and end apart: 3 -> 3, of which waited for: 2 -> 1; matrix products, arithmetic and copies ran while one was open for 1% -> 1% of each run, Pallas kernels for 3% -> 4%
where the time goes in v7:
time: 109 us
  blocking collectives  67.5 us (62%)
  Pallas kernels  18.3 us (17%)
  local copies, waits for them, and re-layouts  8.97 us (8%)
  starting transfers between devices  7.34 us (7%)
  waiting for transfers between devices  6.37 us (6%)
    all_to_all x1, blocking collectives, body(): lax.all_to_all(outputs.reshape(device_count, capacity, features), ('patch...  26.7 us
    all_to_all x1, blocking collectives, body(): lax.all_to_all(outgoing, ('patch', 'expert'), split_axis=0, concat_axis=0...  26.6 us
    all_to_all x1, blocking collectives, attention_by_heads(): lax.all_to_all(stale, ('patch', 'expert'), split_axis=0, concat_axis=0, t...  14.2 us
    unnamed x34, local copies, waits for them, and re-layouts  8.97 us
    pallas_call x1, Pallas kernels, expert_slice(): pl.pallas_call(expert_kernel, out_shape=jax.ShapeDtypeStruct((rows, featu...  7.86 us
    all_to_all x1, starting transfers between devices, attention_by_heads(): lax.all_to_all(packed, 'patch', split_axis=0, concat_axis=0, tiled=True)  7 us
    all_to_all x1, waiting for transfers between devices, attention_by_heads(): lax.all_to_all(packed, 'patch', split_axis=0, concat_axis=0, tiled=True)  6.36 us
    pallas_call x1, Pallas kernels, attention_by_heads(): pl.pallas_call(home_kernel, out_shape=(jax.ShapeDtypeStruct((rows, featur...  2.67 us
  transfers between devices with their start and end apart: 3, of which 1 were waited for; matrix products, arithmetic and copies ran while one was open for 1% of the time, Pallas kernels for 4%

profile of v7, /device:TPU:1, one launch (start us, length us, event | category | flops | bytes accessed | tf_op | source)
XLA Modules:
  0.0 108.7 jit_solution(13447886315577804056)
XLA Ops:
  0.0 0.1 collective-permute-start
  0.1 2.3 %pack.1 = bf16[8,336,128]{2,1,0:T(8,128)(2,1)} custom-call(bf16[128,896]{1,0:T(8,128)(2,1)} %q_ref.3, bf16[128,896]{1,0:T(8,128)(2,1)} %k_ref.2, bf16[128,896]{1,0:T(8,128)(2,1)} %v_ref.2), custom_call_target="tpu_custom_call" | custom-call | tf_op jit(solution)/shard_map/pack/pallas_call | solution.py:192
  2.3 7.0 %all-to-all-start = ((bf16[8,336,128]{2,1,0:T(8,128)(2,1)}), bf16[8,336,128]{2,1,0:T(8,128)(2,1)S(1)}, u32[]{:S(2)}, u32[]{:S(2)}) async-start(bf16[8,336,128]{2,1,0:T(8,128)(2,1)} %pack.1), calls=%async_computation | async-start | bytes 1376256 | tf_op jit(solution)/shard_map/all_to_all | solution.py:200
  9.3 0.8 copy.13.routes_ref
  10.1 0.8 copy.14.gates_ref
  10.8 0.0 collective-permute-done.w_other_ref
  10.9 0.0 copy-start
  10.9 0.9 copy-done
  11.8 0.0 copy-start.1
  11.8 1.9 %copy-done.1 = bf16[896,1792]{1,0:T(8,128)(2,1)S(1)} copy-done((bf16[896,1792]{1,0:T(8,128)(2,1)S(1)}, bf16[896,1792]{1,0:T(8,128)(2,1)}, u32[]{:S(2)}) %copy-start.1) | copy-done | bytes 3211288
  13.7 0.0 copy-start.2
  13.7 0.9 copy-done.2
  14.6 0.0 copy-start.3
  14.6 0.9 copy-done.3
  15.6 2.3 %fresh.1 = (f32[64,1024]{1,0:T(8,128)S(1)}, f32[64,1024]{1,0:T(8,128)S(1)}, bf16[2,64,256]{2,1,0:T(8,128)(2,1)S(1)}, f32[64,2]{1,0:T(8,128)S(1)}, bf16[2,896,1792]{2,1,0:T(8,128)(2,1)S(1)}) custom-call(s32[1]{0:T(128)} %bitcast.core_ref, bf16[128,896]{1,0:T(8,128)(2,1)S(1)} %copy-done, bf16[128,896]{1,0:T(8,128)(2,1)S(1)} %copy-done.2, ...), custom_call_target="tpu_custom_call" | custom-call | flops 5000000000 | bytes 2000000 | tf_op jit(solution)/shard_map/fresh/pallas_call | solution.py:203
  17.9 0.0 copy-start.6
  17.9 2.7 %copy-done.6 = bf16[2,896,1792]{2,1,0:T(8,128)(2,1)} copy-done((bf16[2,896,1792]{2,1,0:T(8,128)(2,1)}, bf16[2,896,1792]{2,1,0:T(8,128)(2,1)S(1)}, u32[]{:S(2)}) %copy-start.6) | copy-done | bytes 6422552
  20.6 0.0 copy-start.4
  20.6 0.0 copy-start.5
  20.6 0.3 collective-permute-start.1
  20.8 6.4 %all-to-all-done.in_ref = bf16[8,336,128]{2,1,0:T(8,128)(2,1)S(1)} async-done(((bf16[8,336,128]{2,1,0:T(8,128)(2,1)}), bf16[8,336,128]{2,1,0:T(8,128)(2,1)S(1)}, u32[]{:S(2)}, u32[]{:S(2)}) %all-to-all-start) | async-done | bytes 688160 | tf_op jit(solution)/shard_map/all_to_all | solution.py:200
  27.2 0.0 copy-start.7
  27.2 0.0 collective-permute-done.1.fresh_ref.other_ref
  27.2 1.7 %attend.1 = bf16[16,64,128]{2,1,0:T(8,128)(2,1)S(1)} custom-call(bf16[8,336,128]{2,1,0:T(8,128)(2,1)S(1)} %all-to-all-done.in_ref, f32[64,1024]{1,0:T(8,128)S(1)} %collective-permute-done.1.fresh_ref.other_ref), custom_call_target="tpu_custom_call" | custom-call | flops 99999997952 | bytes 2000000 | tf_op jit(solution)/shard_map/attend/pallas_call | solution.py:220
  28.9 14.2 %all_to_all.20 = bf16[16,64,128]{2,1,0:T(8,128)(2,1)S(1)} all-to-all(bf16[16,64,128]{2,1,0:T(8,128)(2,1)S(1)} %attend.1), channel_id=1, replica_groups=mesh['group'=2,'patch'=8,'expert'=2] {'patch','expert'}, dimensions={0} | all-to-all | bytes 524288 | tf_op jit(solution)/shard_map/all_to_all | solution.py:229
  43.1 0.0 copy-done.4
  43.1 0.0 copy-done.5
  43.1 0.0 copy-done.7
  43.1 2.7 %home.1 = (f32[64,1792]{1,0:T(8,128)S(1)}, bf16[64,1792]{1,0:T(8,128)(2,1)S(1)}) custom-call(s32[1]{0:T(128)} %bitcast.core_ref, bf16[8,2,64,128]{3,2,1,0:T(8,128)(2,1)S(1)} %bitcast.14, f32[64,1024]{1,0:T(8,128)S(1)} %get-tuple-element.13.own_ref, f32[64,1024]{1,0:T(8,128)S(1)} %collective-permute-done.1.fresh_ref.other_ref, ...), custom_call_target="tpu_custom_call" | custom-call | flops 4000000000 | bytes 8000000 | tf_op jit(solution)/shard_map/home/pallas_call | solution.py:230
  45.8 0.0 slice-start
  45.8 0.0 slice-start.4
  45.8 0.0 slice-start.1
  45.8 0.0 slice-start.2
  45.8 0.0 slice-start.3
  45.8 0.0 slice-start.5
  45.8 0.0 slice-start.6
  45.9 0.0 slice-start.7
  45.9 0.4 slots.1
  46.3 26.6 %all_to_all.21 = bf16[16,16,1792]{2,1,0:T(8,128)(2,1)S(1)} all-to-all(bf16[16,16,1792]{2,1,0:T(8,128)(2,1)S(1)} %bitcast.13), channel_id=1, replica_groups=mesh['group'=2,'patch'=8,'expert'=2] {'patch','expert'}, dimensions={0} | all-to-all | bytes 1835008 | tf_op jit(solution)/shard_map/all_to_all | solution.py:361
  72.9 0.0 slice-done
  72.9 0.0 slice-done.4
  72.9 0.0 slice-done.1
  72.9 0.0 slice-done.2
  72.9 0.0 slice-done.3
  72.9 0.0 slice-done.5
  72.9 0.0 slice-done.6
  72.9 0.0 slice-done.7
  73.0 7.9 %experts.1 = bf16[256,1792]{1,0:T(8,128)(2,1)S(1)} custom-call(bf16[256,1792]{1,0:T(8,128)(2,1)S(1)} %bitcast.11, bf16[1,1792,3584]{2,1,0:T(8,128)(2,1)S(1)} %bitcast.7, bf16[1,3584,1792]{2,1,0:T(8,128)(2,1)S(1)} %bitcast.9), custom_call_target="tpu_custom_call" | custom-call | tf_op jit(solution)/shard_map/experts/pallas_call | solution.py:322
  80.8 26.7 %all_to_all.22 = bf16[16,16,1792]{2,1,0:T(8,128)(2,1)S(1)} all-to-all(bf16[16,16,1792]{2,1,0:T(8,128)(2,1)S(1)} %bitcast.12), channel_id=1, replica_groups=mesh['group'=2,'patch'=8,'expert'=2] {'patch','expert'}, dimensions={0} | all-to-all | bytes 1835008 | tf_op jit(solution)/shard_map/all_to_all | solution.py:363
  107.5 1.1 %combine.1 = bf16[64,1792]{1,0:T(8,128)(2,1)} custom-call(f32[64,1792]{1,0:T(8,128)S(1)} %get-tuple-element.15.hidden_ref, bf16[2,64,256]{2,1,0:T(8,128)(2,1)S(1)} %get-tuple-element.16.picks_ref, f32[64,2]{1,0:T(8,128)S(1)} %get-tuple-element.17.gates_ref, bf16[16,1,16,1792]{3,2,1,0:T(8,128)(2,1)S(1)} %bitcast.10), custom_call_target="tpu_custom_call" | custom-call | tf_op jit(solution)/shard_map/combine/pallas_call | solution.py:370
  (2 shorter events, 0.0 us)
Async XLA Ops:
  0.0 10.9 %collective-permute-start = (bf16[896,1792]{1,0:T(8,128)(2,1)}, bf16[896,1792]{1,0:T(8,128)(2,1)}, u32[]{:S(2)}, u32[]{:S(2)}) collective-permute-start(bf16[896,1792]{1,0:T(8,128)(2,1)} %w_own_ref.1), channel_id=1, source_target_pairs={{0,1},{1,0},{2,3},{3,2},{4,5},{5,4},{6,7},{7,6},{8,9},{9,8},{10,11... | collective-permute-start | bytes 9633800 | tf_op jit(solution)/shard_map/ppermute | solution.py:199
  2.3 24.9 %all-to-all-start = ((bf16[8,336,128]{2,1,0:T(8,128)(2,1)}), bf16[8,336,128]{2,1,0:T(8,128)(2,1)S(1)}, u32[]{:S(2)}, u32[]{:S(2)}) async-start(bf16[8,336,128]{2,1,0:T(8,128)(2,1)} %pack.1), calls=%async_computation | async-start | bytes 1376256 | tf_op jit(solution)/shard_map/all_to_all | solution.py:200
  10.9 0.9 copy-start
  11.8 1.9 %copy-start.1 = (bf16[896,1792]{1,0:T(8,128)(2,1)S(1)}, bf16[896,1792]{1,0:T(8,128)(2,1)}, u32[]{:S(2)}) copy-start(bf16[896,1792]{1,0:T(8,128)(2,1)} %w_own_ref.1) | copy-start | bytes 9633796
  13.7 0.9 copy-start.2
  14.6 0.9 copy-start.3
  17.9 2.7 %copy-start.6 = (bf16[2,896,1792]{2,1,0:T(8,128)(2,1)}, bf16[2,896,1792]{2,1,0:T(8,128)(2,1)S(1)}, u32[]{:S(2)}) copy-start(bf16[2,896,1792]{2,1,0:T(8,128)(2,1)S(1)} %get-tuple-element.14.w_ref) | copy-start | bytes 19267588
  20.6 22.5 %copy-start.4 = (bf16[64,1792]{1,0:T(8,128)(2,1)S(1)}, bf16[64,1792]{1,0:T(8,128)(2,1)}, u32[]{:S(2)}) copy-start(bf16[64,1792]{1,0:T(8,128)(2,1)} %residual_ref.1) | copy-start | bytes 688132
  20.6 22.5 %copy-start.5 = (f32[2,1792]{1,0:T(2,128)S(1)}, f32[2,1792]{1,0:T(2,128)}, u32[]{:S(2)}) copy-start(f32[2,1792]{1,0:T(2,128)} %modulation_ref.1) | copy-start | bytes 43012
  20.6 6.7 %collective-permute-start.1 = (f32[64,1024]{1,0:T(8,128)S(1)}, f32[64,1024]{1,0:T(8,128)S(1)}, u32[]{:S(2)}, u32[]{:S(2)}) collective-permute-start(f32[64,1024]{1,0:T(8,128)S(1)} %get-tuple-element.12), channel_id=1, source_target_pairs={{0,1},{1,0},{2,3},{3,2},{4,5},{5,4},{6,7},{7,6},{8,9},{9,8},{10,11... | collective-permute-start | bytes 786440 | tf_op jit(solution)/shard_map/ppermute | solution.py:219
  27.2 15.9 %copy-start.7 = (bf16[2,896,1792]{2,1,0:T(8,128)(2,1)S(1)}, bf16[2,896,1792]{2,1,0:T(8,128)(2,1)}, u32[]{:S(2)}) copy-start(bf16[2,896,1792]{2,1,0:T(8,128)(2,1)} %copy-done.6) | copy-start | bytes 19267588
  45.8 27.1 %slice-start = ((s8[12845056]{0:T(1024)(128)(4,1)}), s8[4194304]{0:T(1024)(128)(4,1)S(1)}, s32[]{:S(2)}) async-start(s8[12845056]{0:T(1024)(128)(4,1)} %bitcast.6), calls=%async_computation.4 | async-start | bytes 8388608
  45.8 27.1 %slice-start.4 = ((s8[12845056]{0:T(1024)(128)(4,1)}), s8[4194304]{0:T(1024)(128)(4,1)S(1)}, s32[]{:S(2)}) async-start(s8[12845056]{0:T(1024)(128)(4,1)} %bitcast.8), calls=%async_computation.8 | async-start | bytes 8388608
  45.8 27.1 %slice-start.1 = ((s8[12845056]{0:T(1024)(128)(4,1)}), s8[4194304]{0:T(1024)(128)(4,1)S(1)}, s32[]{:S(2)}) async-start(s8[12845056]{0:T(1024)(128)(4,1)} %bitcast.6), calls=%async_computation.5 | async-start | bytes 8388608
  45.8 27.1 %slice-start.2 = ((s8[12845056]{0:T(1024)(128)(4,1)}), s8[4194304]{0:T(1024)(128)(4,1)S(1)}, s32[]{:S(2)}) async-start(s8[12845056]{0:T(1024)(128)(4,1)} %bitcast.6), calls=%async_computation.6 | async-start | bytes 8388608
  45.8 27.1 %slice-start.3 = ((s8[12845056]{0:T(1024)(128)(4,1)}), s8[262144]{0:T(1024)(128)(4,1)S(1)}, s32[]{:S(2)}) async-start(s8[12845056]{0:T(1024)(128)(4,1)} %bitcast.6), calls=%async_computation.7 | async-start | bytes 524288
  45.8 27.1 %slice-start.5 = ((s8[12845056]{0:T(1024)(128)(4,1)}), s8[4194304]{0:T(1024)(128)(4,1)S(1)}, s32[]{:S(2)}) async-start(s8[12845056]{0:T(1024)(128)(4,1)} %bitcast.8), calls=%async_computation.9 | async-start | bytes 8388608
  45.8 27.1 %slice-start.6 = ((s8[12845056]{0:T(1024)(128)(4,1)}), s8[4194304]{0:T(1024)(128)(4,1)S(1)}, s32[]{:S(2)}) async-start(s8[12845056]{0:T(1024)(128)(4,1)} %bitcast.8), calls=%async_computation.10 | async-start | bytes 8388608
  45.9 27.1 %slice-start.7 = ((s8[12845056]{0:T(1024)(128)(4,1)}), s8[262144]{0:T(1024)(128)(4,1)S(1)}, s32[]{:S(2)}) async-start(s8[12845056]{0:T(1024)(128)(4,1)} %bitcast.8), calls=%async_computation.11 | async-start | bytes 524288

commit v8 on v7

--- a/solution.py
+++ b/solution.py
@@ -24,13 +24,28 @@
     return lax.dot_general(a, b, (((dim_a,), (dim_b,)), ((), ())), preferred_element_type=F32)
 
 
-def pack_kernel(q_ref, k_ref, v_ref, out_ref):
-    for i, ref in enumerate((q_ref, k_ref, v_ref)):
-        turned = ref[...].T
-        for h in range(out_ref.shape[0]):
-            out_ref[h, i * HEAD_DIM : (i + 1) * HEAD_DIM, :] = turned[
-                h * HEAD_DIM : (h + 1) * HEAD_DIM
-            ]
+def pack_kernel(q_ref, k_ref, v_ref, out_ref, rows_ref, turned_ref, in_sem, out_sem):
+    loads = [
+        pltpu.make_async_copy(ref, rows_ref.at[i], in_sem.at[i]) for i, ref in enumerate((q_ref, k_ref, v_ref))
+    ]
+    stores = [
+        pltpu.make_async_copy(
+            turned_ref.at[:, pl.ds(i * HEAD_DIM, HEAD_DIM)],
+            out_ref.at[:, pl.ds(i * HEAD_DIM, HEAD_DIM)],
+            out_sem.at[i],
+        )
+        for i in range(3)
+    ]
+    for load in loads:
+        load.start()
+    for i in range(3):
+        loads[i].wait()
+        turned = rows_ref[i].T
+        for h in range(turned_ref.shape[0]):
+            turned_ref[h, i * HEAD_DIM : (i + 1) * HEAD_DIM, :] = turned[h * HEAD_DIM : (h + 1) * HEAD_DIM]
+        stores[i].start()
+    for store in stores:
+        store.wait()
 
 
 def with_ones(values):
@@ -144,7 +159,7 @@
 
 def home_kernel(
     core_ref, far_ref, own_ref, other_ref, w_ref, residual_ref, modulation_ref,
-    hidden_ref, normed_ref, attended_ref,
+    picks_ref, hidden_ref, buffer_ref, attended_ref,
 ):
     heads = far_ref.shape[0]
     core = core_ref[0]
@@ -174,13 +189,10 @@
     hidden_ref[...] = hidden
     centered = hidden - hidden.mean(-1, keepdims=True)
     variance = (centered * centered).mean(-1, keepdims=True)
-    normed_ref[...] = (
+    normed = (
         centered / jnp.sqrt(variance + 1e-06) * (1.0 + modulation_ref[1:2]) + modulation_ref[0:1]
     ).astype(BF16)
-
-
-def slots_kernel(normed_ref, picks_ref, buffer_ref):
-    buffer_ref[...] = contract(picks_ref[0] + picks_ref[1], normed_ref[...], 0, 0).astype(BF16)
+    buffer_ref[...] = contract(picks_ref[0] + picks_ref[1], normed, 0, 0).astype(BF16)
 
 
 def attention_by_heads(queries, fresh_keys, fresh_values, stale_keys, stale_values, out_weight, residual, modulation, routes, gates):
@@ -192,8 +204,15 @@
     packed = pl.pallas_call(
         pack_kernel,
         out_shape=jax.ShapeDtypeStruct((heads, 3 * HEAD_DIM, tokens), BF16),
-        in_specs=[VMEM] * 3,
-        out_specs=VMEM,
+        in_specs=[ANY] * 3,
+        out_specs=ANY,
+        scratch_shapes=[
+            pltpu.VMEM((3, tokens, width), BF16),
+            pltpu.VMEM((heads, 3 * HEAD_DIM, tokens), BF16),
+            pltpu.SemaphoreType.DMA((3,)),
+            pltpu.SemaphoreType.DMA((3,)),
+        ],
+        compiler_params=pltpu.CompilerParams(vmem_limit_bytes=56 << 20),
         name="pack",
     )(queries, stale_keys, stale_values)
     w_other = lax.ppermute(out_weight, "expert", swap)
@@ -227,28 +246,19 @@
         name="attend",
     )(gathered, fresh_other)
     far = lax.all_to_all(stale, ("patch", "expert"), split_axis=0, concat_axis=0, tiled=True)
-    hidden, normed = pl.pallas_call(
+    hidden, buffer = pl.pallas_call(
         home_kernel,
         out_shape=(
             jax.ShapeDtypeStruct((rows, features), F32),
-            jax.ShapeDtypeStruct((rows, features), BF16),
+            jax.ShapeDtypeStruct((slots, features), BF16),
         ),
-        in_specs=[SMEM] + [VMEM] * 6,
+        in_specs=[SMEM] + [VMEM] * 7,
         out_specs=(VMEM, VMEM),
         scratch_shapes=[pltpu.VMEM((2, rows, width), BF16)],
         compiler_params=pltpu.CompilerParams(vmem_limit_bytes=20 << 20),
-        cost_estimate=pl.CostEstimate(flops=4_000_000_000, bytes_accessed=8_000_000, transcendentals=100_000),
+        cost_estimate=pl.CostEstimate(flops=100_000_000_000, bytes_accessed=8_000_000, transcendentals=100_000),
         name="home",
-    )(core, far.reshape(heads, 2, rows, LANES), fresh_own, fresh_other, weights, residual, modulation)
-    buffer = pl.pallas_call(
-        slots_kernel,
-        out_shape=jax.ShapeDtypeStruct((slots, features), BF16),
-        in_specs=[VMEM] * 2,
-        out_specs=VMEM,
-        compiler_params=pltpu.CompilerParams(vmem_limit_bytes=12 << 20),
-        cost_estimate=pl.CostEstimate(flops=100_000_000_000, bytes_accessed=8_000_000, transcendentals=100_000),
-        name="slots",
-    )(normed, picks)
+    )(core, far.reshape(heads, 2, rows, LANES), fresh_own, fresh_other, weights, residual, modulation, picks)
     return hidden, buffer, picks, gates
 
 

time: 109 us -> 109 us (level)
  no operation moved by 1% of the time
where the time goes in v8:
time: 109 us
  blocking collectives  67.5 us (62%)
  Pallas kernels  18.2 us (17%)
  local copies, waits for them, and re-layouts  8.96 us (8%)
  starting transfers between devices  7.35 us (7%)
  waiting for transfers between devices  6.37 us (6%)
    all_to_all x1, blocking collectives, body(): lax.all_to_all(outputs.reshape(device_count, capacity, features), ('patch...  26.7 us
    all_to_all x1, blocking collectives, body(): lax.all_to_all(outgoing, ('patch', 'expert'), split_axis=0, concat_axis=0...  26.6 us
    all_to_all x1, blocking collectives, attention_by_heads(): lax.all_to_all(stale, ('patch', 'expert'), split_axis=0, concat_axis=0, t...  14.2 us
    unnamed x34, local copies, waits for them, and re-layouts  8.96 us
    pallas_call x1, Pallas kernels, expert_slice(): pl.pallas_call(expert_kernel, out_shape=jax.ShapeDtypeStruct((rows, featu...  7.86 us
    all_to_all x1, starting transfers between devices, attention_by_heads(): lax.all_to_all(packed, 'patch', split_axis=0, concat_axis=0, tiled=True)  7.01 us
    all_to_all x1, waiting for transfers between devices, attention_by_heads(): lax.all_to_all(packed, 'patch', split_axis=0, concat_axis=0, tiled=True)  6.36 us
    pallas_call x1, Pallas kernels, attention_by_heads(): pl.pallas_call(home_kernel, out_shape=(jax.ShapeDtypeStruct((rows, featur...  3.14 us
  transfers between devices with their start and end apart: 3, of which 1 were waited for; matrix products, arithmetic and copies ran while one was open for 1% of the time, Pallas kernels for 4%

profile of v8, /device:TPU:1, one launch (start us, length us, event | category | flops | bytes accessed | tf_op | source)
XLA Modules:
  0.0 108.5 jit_solution(3394151880272780962)
XLA Ops:
  0.0 0.1 collective-permute-start
  0.1 2.1 %pack.1 = bf16[8,336,128]{2,1,0:T(8,128)(2,1)} custom-call(bf16[128,896]{1,0:T(8,128)(2,1)} %q_ref.3, bf16[128,896]{1,0:T(8,128)(2,1)} %k_ref.2, bf16[128,896]{1,0:T(8,128)(2,1)} %v_ref.2), custom_call_target="tpu_custom_call" | custom-call | tf_op jit(solution)/shard_map/pack/pallas_call | solution.py:204
  2.1 7.0 %all-to-all-start = ((bf16[8,336,128]{2,1,0:T(8,128)(2,1)}), bf16[8,336,128]{2,1,0:T(8,128)(2,1)S(1)}, u32[]{:S(2)}, u32[]{:S(2)}) async-start(bf16[8,336,128]{2,1,0:T(8,128)(2,1)} %pack.1), calls=%async_computation | async-start | bytes 1376256 | tf_op jit(solution)/shard_map/all_to_all | solution.py:219
  9.1 0.8 copy.13.routes_ref
  9.9 0.8 copy.14.gates_ref
  10.7 0.0 collective-permute-done.w_other_ref
  10.7 0.0 copy-start
  10.7 0.9 copy-done
  11.6 0.0 copy-start.1
  11.6 1.9 %copy-done.1 = bf16[896,1792]{1,0:T(8,128)(2,1)S(1)} copy-done((bf16[896,1792]{1,0:T(8,128)(2,1)S(1)}, bf16[896,1792]{1,0:T(8,128)(2,1)}, u32[]{:S(2)}) %copy-start.1) | copy-done | bytes 3211288
  13.5 0.0 copy-start.2
  13.5 0.9 copy-done.2
  14.5 0.0 copy-start.3
  14.5 0.9 copy-done.3
  15.4 2.3 %fresh.1 = (f32[64,1024]{1,0:T(8,128)S(1)}, f32[64,1024]{1,0:T(8,128)S(1)}, bf16[2,64,256]{2,1,0:T(8,128)(2,1)S(1)}, f32[64,2]{1,0:T(8,128)S(1)}, bf16[2,896,1792]{2,1,0:T(8,128)(2,1)S(1)}) custom-call(s32[1]{0:T(128)} %bitcast.core_ref, bf16[128,896]{1,0:T(8,128)(2,1)S(1)} %copy-done, bf16[128,896]{1,0:T(8,128)(2,1)S(1)} %copy-done.2, ...), custom_call_target="tpu_custom_call" | custom-call | flops 5000000000 | bytes 2000000 | tf_op jit(solution)/shard_map/fresh/pallas_call | solution.py:222
  17.7 0.0 copy-start.6
  17.7 2.7 %copy-done.6 = bf16[2,896,1792]{2,1,0:T(8,128)(2,1)} copy-done((bf16[2,896,1792]{2,1,0:T(8,128)(2,1)}, bf16[2,896,1792]{2,1,0:T(8,128)(2,1)S(1)}, u32[]{:S(2)}) %copy-start.6) | copy-done | bytes 6422552
  20.4 0.0 copy-start.4
  20.4 0.0 copy-start.5
  20.4 0.3 collective-permute-start.1
  20.7 6.4 %all-to-all-done.in_ref = bf16[8,336,128]{2,1,0:T(8,128)(2,1)S(1)} async-done(((bf16[8,336,128]{2,1,0:T(8,128)(2,1)}), bf16[8,336,128]{2,1,0:T(8,128)(2,1)S(1)}, u32[]{:S(2)}, u32[]{:S(2)}) %all-to-all-start) | async-done | bytes 688160 | tf_op jit(solution)/shard_map/all_to_all | solution.py:219
  27.0 0.0 copy-start.7
  27.0 0.0 collective-permute-done.1.fresh_ref.other_ref
  27.0 1.7 %attend.1 = bf16[16,64,128]{2,1,0:T(8,128)(2,1)S(1)} custom-call(bf16[8,336,128]{2,1,0:T(8,128)(2,1)S(1)} %all-to-all-done.in_ref, f32[64,1024]{1,0:T(8,128)S(1)} %collective-permute-done.1.fresh_ref.other_ref), custom_call_target="tpu_custom_call" | custom-call | flops 99999997952 | bytes 2000000 | tf_op jit(solution)/shard_map/attend/pallas_call | solution.py:239
  28.7 14.2 %all_to_all.20 = bf16[16,64,128]{2,1,0:T(8,128)(2,1)S(1)} all-to-all(bf16[16,64,128]{2,1,0:T(8,128)(2,1)S(1)} %attend.1), channel_id=1, replica_groups=mesh['group'=2,'patch'=8,'expert'=2] {'patch','expert'}, dimensions={0} | all-to-all | bytes 524288 | tf_op jit(solution)/shard_map/all_to_all | solution.py:248
  42.9 0.0 slice-start
  42.9 0.0 slice-start.4
  42.9 0.0 copy-done.4
  42.9 0.0 copy-done.5
  42.9 0.0 copy-done.7
  42.9 0.0 slice-start.1
  42.9 0.0 slice-start.2
  43.0 0.0 slice-start.3
  43.0 0.0 slice-start.5
  43.0 0.0 slice-start.6
  43.0 0.0 slice-start.7
  43.0 3.1 %home.1 = (f32[64,1792]{1,0:T(8,128)S(1)}, bf16[256,1792]{1,0:T(8,128)(2,1)S(1)}) custom-call(s32[1]{0:T(128)} %bitcast.core_ref, bf16[8,2,64,128]{3,2,1,0:T(8,128)(2,1)S(1)} %bitcast.14, f32[64,1024]{1,0:T(8,128)S(1)} %get-tuple-element.13.own_ref, f32[64,1024]{1,0:T(8,128)S(1)} %collective-permute-done.1.fresh_ref.other_ref, ...), custom_call_target="tpu_custom_call" | custom-call | flops 99999997952 | bytes 8000000 | tf_op jit(solution)/shard_map/home/pallas_call | solution.py:249
  46.1 26.6 %all_to_all.21 = bf16[16,16,1792]{2,1,0:T(8,128)(2,1)S(1)} all-to-all(bf16[16,16,1792]{2,1,0:T(8,128)(2,1)S(1)} %bitcast.13), channel_id=1, replica_groups=mesh['group'=2,'patch'=8,'expert'=2] {'patch','expert'}, dimensions={0} | all-to-all | bytes 1835008 | tf_op jit(solution)/shard_map/all_to_all | solution.py:371
  72.7 0.0 slice-done
  72.7 0.0 slice-done.4
  72.7 0.0 slice-done.1
  72.7 0.0 slice-done.2
  72.7 0.0 slice-done.3
  72.8 0.0 slice-done.5
  72.8 0.0 slice-done.6
  72.8 0.0 slice-done.7
  72.8 7.9 %experts.1 = bf16[256,1792]{1,0:T(8,128)(2,1)S(1)} custom-call(bf16[256,1792]{1,0:T(8,128)(2,1)S(1)} %bitcast.11, bf16[1,1792,3584]{2,1,0:T(8,128)(2,1)S(1)} %bitcast.7, bf16[1,3584,1792]{2,1,0:T(8,128)(2,1)S(1)} %bitcast.9), custom_call_target="tpu_custom_call" | custom-call | tf_op jit(solution)/shard_map/experts/pallas_call | solution.py:332
  80.7 26.7 %all_to_all.22 = bf16[16,16,1792]{2,1,0:T(8,128)(2,1)S(1)} all-to-all(bf16[16,16,1792]{2,1,0:T(8,128)(2,1)S(1)} %bitcast.12), channel_id=1, replica_groups=mesh['group'=2,'patch'=8,'expert'=2] {'patch','expert'}, dimensions={0} | all-to-all | bytes 1835008 | tf_op jit(solution)/shard_map/all_to_all | solution.py:373
  107.4 1.1 %combine.1 = bf16[64,1792]{1,0:T(8,128)(2,1)} custom-call(f32[64,1792]{1,0:T(8,128)S(1)} %get-tuple-element.16.hidden_ref, bf16[2,64,256]{2,1,0:T(8,128)(2,1)S(1)} %get-tuple-element.15.picks_ref, f32[64,2]{1,0:T(8,128)S(1)} %get-tuple-element.17.gates_ref, bf16[16,1,16,1792]{3,2,1,0:T(8,128)(2,1)S(1)} %bitcast.10), custom_call_target="tpu_custom_call" | custom-call | tf_op jit(solution)/shard_map/combine/pallas_call | solution.py:380
  (2 shorter events, 0.0 us)
Async XLA Ops:
  0.0 10.7 %collective-permute-start = (bf16[896,1792]{1,0:T(8,128)(2,1)}, bf16[896,1792]{1,0:T(8,128)(2,1)}, u32[]{:S(2)}, u32[]{:S(2)}) collective-permute-start(bf16[896,1792]{1,0:T(8,128)(2,1)} %w_own_ref.1), channel_id=1, source_target_pairs={{0,1},{1,0},{2,3},{3,2},{4,5},{5,4},{6,7},{7,6},{8,9},{9,8},{10,11... | collective-permute-start | bytes 9633800 | tf_op jit(solution)/shard_map/ppermute | solution.py:218
  2.1 24.9 %all-to-all-start = ((bf16[8,336,128]{2,1,0:T(8,128)(2,1)}), bf16[8,336,128]{2,1,0:T(8,128)(2,1)S(1)}, u32[]{:S(2)}, u32[]{:S(2)}) async-start(bf16[8,336,128]{2,1,0:T(8,128)(2,1)} %pack.1), calls=%async_computation | async-start | bytes 1376256 | tf_op jit(solution)/shard_map/all_to_all | solution.py:219
  10.7 0.9 copy-start
  11.6 1.9 %copy-start.1 = (bf16[896,1792]{1,0:T(8,128)(2,1)S(1)}, bf16[896,1792]{1,0:T(8,128)(2,1)}, u32[]{:S(2)}) copy-start(bf16[896,1792]{1,0:T(8,128)(2,1)} %w_own_ref.1) | copy-start | bytes 9633796
  13.5 0.9 copy-start.2
  14.5 0.9 copy-start.3
  17.7 2.7 %copy-start.6 = (bf16[2,896,1792]{2,1,0:T(8,128)(2,1)}, bf16[2,896,1792]{2,1,0:T(8,128)(2,1)S(1)}, u32[]{:S(2)}) copy-start(bf16[2,896,1792]{2,1,0:T(8,128)(2,1)S(1)} %get-tuple-element.14.w_ref) | copy-start | bytes 19267588
  20.4 22.5 %copy-start.4 = (bf16[64,1792]{1,0:T(8,128)(2,1)S(1)}, bf16[64,1792]{1,0:T(8,128)(2,1)}, u32[]{:S(2)}) copy-start(bf16[64,1792]{1,0:T(8,128)(2,1)} %residual_ref.1) | copy-start | bytes 688132
  20.4 22.5 %copy-start.5 = (f32[2,1792]{1,0:T(2,128)S(1)}, f32[2,1792]{1,0:T(2,128)}, u32[]{:S(2)}) copy-start(f32[2,1792]{1,0:T(2,128)} %modulation_ref.1) | copy-start | bytes 43012
  20.4 6.7 %collective-permute-start.1 = (f32[64,1024]{1,0:T(8,128)S(1)}, f32[64,1024]{1,0:T(8,128)S(1)}, u32[]{:S(2)}, u32[]{:S(2)}) collective-permute-start(f32[64,1024]{1,0:T(8,128)S(1)} %get-tuple-element.12), channel_id=1, source_target_pairs={{0,1},{1,0},{2,3},{3,2},{4,5},{5,4},{6,7},{7,6},{8,9},{9,8},{10,11... | collective-permute-start | bytes 786440 | tf_op jit(solution)/shard_map/ppermute | solution.py:238
  27.0 15.9 %copy-start.7 = (bf16[2,896,1792]{2,1,0:T(8,128)(2,1)S(1)}, bf16[2,896,1792]{2,1,0:T(8,128)(2,1)}, u32[]{:S(2)}) copy-start(bf16[2,896,1792]{2,1,0:T(8,128)(2,1)} %copy-done.6) | copy-start | bytes 19267588
  42.9 29.8 %slice-start = ((s8[12845056]{0:T(1024)(128)(4,1)}), s8[4194304]{0:T(1024)(128)(4,1)S(1)}, s32[]{:S(2)}) async-start(s8[12845056]{0:T(1024)(128)(4,1)} %bitcast.6), calls=%async_computation.4 | async-start | bytes 8388608
  42.9 29.8 %slice-start.4 = ((s8[12845056]{0:T(1024)(128)(4,1)}), s8[4194304]{0:T(1024)(128)(4,1)S(1)}, s32[]{:S(2)}) async-start(s8[12845056]{0:T(1024)(128)(4,1)} %bitcast.8), calls=%async_computation.8 | async-start | bytes 8388608
  42.9 29.8 %slice-start.1 = ((s8[12845056]{0:T(1024)(128)(4,1)}), s8[4194304]{0:T(1024)(128)(4,1)S(1)}, s32[]{:S(2)}) async-start(s8[12845056]{0:T(1024)(128)(4,1)} %bitcast.6), calls=%async_computation.5 | async-start | bytes 8388608
  42.9 29.8 %slice-start.2 = ((s8[12845056]{0:T(1024)(128)(4,1)}), s8[4194304]{0:T(1024)(128)(4,1)S(1)}, s32[]{:S(2)}) async-start(s8[12845056]{0:T(1024)(128)(4,1)} %bitcast.6), calls=%async_computation.6 | async-start | bytes 8388608
  43.0 29.8 %slice-start.3 = ((s8[12845056]{0:T(1024)(128)(4,1)}), s8[262144]{0:T(1024)(128)(4,1)S(1)}, s32[]{:S(2)}) async-start(s8[12845056]{0:T(1024)(128)(4,1)} %bitcast.6), calls=%async_computation.7 | async-start | bytes 524288
  43.0 29.8 %slice-start.5 = ((s8[12845056]{0:T(1024)(128)(4,1)}), s8[4194304]{0:T(1024)(128)(4,1)S(1)}, s32[]{:S(2)}) async-start(s8[12845056]{0:T(1024)(128)(4,1)} %bitcast.8), calls=%async_computation.9 | async-start | bytes 8388608
  43.0 29.8 %slice-start.6 = ((s8[12845056]{0:T(1024)(128)(4,1)}), s8[4194304]{0:T(1024)(128)(4,1)S(1)}, s32[]{:S(2)}) async-start(s8[12845056]{0:T(1024)(128)(4,1)} %bitcast.8), calls=%async_computation.10 | async-start | bytes 8388608
  43.0 29.8 %slice-start.7 = ((s8[12845056]{0:T(1024)(128)(4,1)}), s8[262144]{0:T(1024)(128)(4,1)S(1)}, s32[]{:S(2)}) async-start(s8[12845056]{0:T(1024)(128)(4,1)} %bitcast.8), calls=%async_computation.11 | async-start | bytes 524288

commit v9 on v8

--- a/solution.py
+++ b/solution.py
@@ -323,7 +323,7 @@
 
 
 def chunks(width):
-    step = 896 if width % 896 == 0 else LANES
+    step = next(c for c in (1792, 896, LANES) if width % c == 0)
     return [slice(i, i + step) for i in range(0, width, step)]
 
 

time: 109 us -> 108 us (level)
  no operation moved by 1% of the time
where the time goes in v9:
time: 108 us
  blocking collectives  67.5 us (62%)
  Pallas kernels  17.3 us (16%)
  local copies, waits for them, and re-layouts  8.96 us (8%)
  starting transfers between devices  7.35 us (7%)
  waiting for transfers between devices  6.37 us (6%)
    all_to_all x1, blocking collectives, body(): lax.all_to_all(outputs.reshape(device_count, capacity, features), ('patch...  26.7 us
    all_to_all x1, blocking collectives, body(): lax.all_to_all(outgoing, ('patch', 'expert'), split_axis=0, concat_axis=0...  26.6 us
    all_to_all x1, blocking collectives, attention_by_heads(): lax.all_to_all(stale, ('patch', 'expert'), split_axis=0, concat_axis=0, t...  14.2 us
    unnamed x34, local copies, waits for them, and re-layouts  8.96 us
    all_to_all x1, starting transfers between devices, attention_by_heads(): lax.all_to_all(packed, 'patch', split_axis=0, concat_axis=0, tiled=True)  7.01 us
    pallas_call x1, Pallas kernels, expert_slice(): pl.pallas_call(expert_kernel, out_shape=jax.ShapeDtypeStruct((rows, featu...  6.94 us
    all_to_all x1, waiting for transfers between devices, attention_by_heads(): lax.all_to_all(packed, 'patch', split_axis=0, concat_axis=0, tiled=True)  6.36 us
    pallas_call x1, Pallas kernels, attention_by_heads(): pl.pallas_call(home_kernel, out_shape=(jax.ShapeDtypeStruct((rows, featur...  3.14 us
  transfers between devices with their start and end apart: 3, of which 1 were waited for; matrix products, arithmetic and copies ran while one was open for 1% of the time, Pallas kernels for 4%

profile of v9, /device:TPU:1, one launch (start us, length us, event | category | flops | bytes accessed | tf_op | source)
XLA Modules:
  0.0 107.6 jit_solution(16333221436241104769)
XLA Ops:
  0.0 0.1 collective-permute-start
  0.1 2.1 %pack.1 = bf16[8,336,128]{2,1,0:T(8,128)(2,1)} custom-call(bf16[128,896]{1,0:T(8,128)(2,1)} %q_ref.3, bf16[128,896]{1,0:T(8,128)(2,1)} %k_ref.2, bf16[128,896]{1,0:T(8,128)(2,1)} %v_ref.2), custom_call_target="tpu_custom_call" | custom-call | tf_op jit(solution)/shard_map/pack/pallas_call | solution.py:204
  2.1 7.0 %all-to-all-start = ((bf16[8,336,128]{2,1,0:T(8,128)(2,1)}), bf16[8,336,128]{2,1,0:T(8,128)(2,1)S(1)}, u32[]{:S(2)}, u32[]{:S(2)}) async-start(bf16[8,336,128]{2,1,0:T(8,128)(2,1)} %pack.1), calls=%async_computation | async-start | bytes 1376256 | tf_op jit(solution)/shard_map/all_to_all | solution.py:219
  9.1 0.8 copy.13.routes_ref
  9.9 0.8 copy.14.gates_ref
  10.7 0.0 collective-permute-done.w_other_ref
  10.7 0.0 copy-start
  10.7 0.9 copy-done
  11.6 0.0 copy-start.1
  11.6 1.9 %copy-done.1 = bf16[896,1792]{1,0:T(8,128)(2,1)S(1)} copy-done((bf16[896,1792]{1,0:T(8,128)(2,1)S(1)}, bf16[896,1792]{1,0:T(8,128)(2,1)}, u32[]{:S(2)}) %copy-start.1) | copy-done | bytes 3211288
  13.5 0.0 copy-start.2
  13.5 0.9 copy-done.2
  14.5 0.0 copy-start.3
  14.5 0.9 copy-done.3
  15.4 2.3 %fresh.1 = (f32[64,1024]{1,0:T(8,128)S(1)}, f32[64,1024]{1,0:T(8,128)S(1)}, bf16[2,64,256]{2,1,0:T(8,128)(2,1)S(1)}, f32[64,2]{1,0:T(8,128)S(1)}, bf16[2,896,1792]{2,1,0:T(8,128)(2,1)S(1)}) custom-call(s32[1]{0:T(128)} %bitcast.core_ref, bf16[128,896]{1,0:T(8,128)(2,1)S(1)} %copy-done, bf16[128,896]{1,0:T(8,128)(2,1)S(1)} %copy-done.2, ...), custom_call_target="tpu_custom_call" | custom-call | flops 5000000000 | bytes 2000000 | tf_op jit(solution)/shard_map/fresh/pallas_call | solution.py:222
  17.7 0.0 copy-start.6
  17.7 2.7 %copy-done.6 = bf16[2,896,1792]{2,1,0:T(8,128)(2,1)} copy-done((bf16[2,896,1792]{2,1,0:T(8,128)(2,1)}, bf16[2,896,1792]{2,1,0:T(8,128)(2,1)S(1)}, u32[]{:S(2)}) %copy-start.6) | copy-done | bytes 6422552
  20.4 0.0 copy-start.4
  20.4 0.0 copy-start.5
  20.4 0.3 collective-permute-start.1
  20.7 6.4 %all-to-all-done.in_ref = bf16[8,336,128]{2,1,0:T(8,128)(2,1)S(1)} async-done(((bf16[8,336,128]{2,1,0:T(8,128)(2,1)}), bf16[8,336,128]{2,1,0:T(8,128)(2,1)S(1)}, u32[]{:S(2)}, u32[]{:S(2)}) %all-to-all-start) | async-done | bytes 688160 | tf_op jit(solution)/shard_map/all_to_all | solution.py:219
  27.0 0.0 copy-start.7
  27.0 0.0 collective-permute-done.1.fresh_ref.other_ref
  27.0 1.7 %attend.1 = bf16[16,64,128]{2,1,0:T(8,128)(2,1)S(1)} custom-call(bf16[8,336,128]{2,1,0:T(8,128)(2,1)S(1)} %all-to-all-done.in_ref, f32[64,1024]{1,0:T(8,128)S(1)} %collective-permute-done.1.fresh_ref.other_ref), custom_call_target="tpu_custom_call" | custom-call | flops 99999997952 | bytes 2000000 | tf_op jit(solution)/shard_map/attend/pallas_call | solution.py:239
  28.7 14.2 %all_to_all.20 = bf16[16,64,128]{2,1,0:T(8,128)(2,1)S(1)} all-to-all(bf16[16,64,128]{2,1,0:T(8,128)(2,1)S(1)} %attend.1), channel_id=1, replica_groups=mesh['group'=2,'patch'=8,'expert'=2] {'patch','expert'}, dimensions={0} | all-to-all | bytes 524288 | tf_op jit(solution)/shard_map/all_to_all | solution.py:248
  42.9 0.0 slice-start
  42.9 0.0 slice-start.4
  42.9 0.0 copy-done.4
  42.9 0.0 copy-done.5
  42.9 0.0 copy-done.7
  42.9 0.0 slice-start.1
  42.9 0.0 slice-start.2
  43.0 0.0 slice-start.3
  43.0 0.0 slice-start.5
  43.0 0.0 slice-start.6
  43.0 0.0 slice-start.7
  43.0 3.1 %home.1 = (f32[64,1792]{1,0:T(8,128)S(1)}, bf16[256,1792]{1,0:T(8,128)(2,1)S(1)}) custom-call(s32[1]{0:T(128)} %bitcast.core_ref, bf16[8,2,64,128]{3,2,1,0:T(8,128)(2,1)S(1)} %bitcast.14, f32[64,1024]{1,0:T(8,128)S(1)} %get-tuple-element.13.own_ref, f32[64,1024]{1,0:T(8,128)S(1)} %collective-permute-done.1.fresh_ref.other_ref, ...), custom_call_target="tpu_custom_call" | custom-call | flops 99999997952 | bytes 8000000 | tf_op jit(solution)/shard_map/home/pallas_call | solution.py:249
  46.1 26.6 %all_to_all.21 = bf16[16,16,1792]{2,1,0:T(8,128)(2,1)S(1)} all-to-all(bf16[16,16,1792]{2,1,0:T(8,128)(2,1)S(1)} %bitcast.13), channel_id=1, replica_groups=mesh['group'=2,'patch'=8,'expert'=2] {'patch','expert'}, dimensions={0} | all-to-all | bytes 1835008 | tf_op jit(solution)/shard_map/all_to_all | solution.py:371
  72.7 0.0 slice-done
  72.7 0.0 slice-done.4
  72.7 0.0 slice-done.1
  72.7 0.0 slice-done.2
  72.8 0.0 slice-done.3
  72.8 0.0 slice-done.5
  72.8 0.0 slice-done.6
  72.8 0.0 slice-done.7
  72.8 6.9 %experts.1 = bf16[256,1792]{1,0:T(8,128)(2,1)S(1)} custom-call(bf16[256,1792]{1,0:T(8,128)(2,1)S(1)} %bitcast.11, bf16[1,1792,3584]{2,1,0:T(8,128)(2,1)S(1)} %bitcast.7, bf16[1,3584,1792]{2,1,0:T(8,128)(2,1)S(1)} %bitcast.9), custom_call_target="tpu_custom_call" | custom-call | tf_op jit(solution)/shard_map/experts/pallas_call | solution.py:332
  79.8 26.7 %all_to_all.22 = bf16[16,16,1792]{2,1,0:T(8,128)(2,1)S(1)} all-to-all(bf16[16,16,1792]{2,1,0:T(8,128)(2,1)S(1)} %bitcast.12), channel_id=1, replica_groups=mesh['group'=2,'patch'=8,'expert'=2] {'patch','expert'}, dimensions={0} | all-to-all | bytes 1835008 | tf_op jit(solution)/shard_map/all_to_all | solution.py:373
  106.5 1.1 %combine.1 = bf16[64,1792]{1,0:T(8,128)(2,1)} custom-call(f32[64,1792]{1,0:T(8,128)S(1)} %get-tuple-element.16.hidden_ref, bf16[2,64,256]{2,1,0:T(8,128)(2,1)S(1)} %get-tuple-element.15.picks_ref, f32[64,2]{1,0:T(8,128)S(1)} %get-tuple-element.17.gates_ref, bf16[16,1,16,1792]{3,2,1,0:T(8,128)(2,1)S(1)} %bitcast.10), custom_call_target="tpu_custom_call" | custom-call | tf_op jit(solution)/shard_map/combine/pallas_call | solution.py:380
  (2 shorter events, 0.0 us)
Async XLA Ops:
  0.0 10.7 %collective-permute-start = (bf16[896,1792]{1,0:T(8,128)(2,1)}, bf16[896,1792]{1,0:T(8,128)(2,1)}, u32[]{:S(2)}, u32[]{:S(2)}) collective-permute-start(bf16[896,1792]{1,0:T(8,128)(2,1)} %w_own_ref.1), channel_id=1, source_target_pairs={{0,1},{1,0},{2,3},{3,2},{4,5},{5,4},{6,7},{7,6},{8,9},{9,8},{10,11... | collective-permute-start | bytes 9633800 | tf_op jit(solution)/shard_map/ppermute | solution.py:218
  2.1 24.9 %all-to-all-start = ((bf16[8,336,128]{2,1,0:T(8,128)(2,1)}), bf16[8,336,128]{2,1,0:T(8,128)(2,1)S(1)}, u32[]{:S(2)}, u32[]{:S(2)}) async-start(bf16[8,336,128]{2,1,0:T(8,128)(2,1)} %pack.1), calls=%async_computation | async-start | bytes 1376256 | tf_op jit(solution)/shard_map/all_to_all | solution.py:219
  10.7 0.9 copy-start
  11.6 1.9 %copy-start.1 = (bf16[896,1792]{1,0:T(8,128)(2,1)S(1)}, bf16[896,1792]{1,0:T(8,128)(2,1)}, u32[]{:S(2)}) copy-start(bf16[896,1792]{1,0:T(8,128)(2,1)} %w_own_ref.1) | copy-start | bytes 9633796
  13.5 0.9 copy-start.2
  14.5 0.9 copy-start.3
  17.7 2.7 %copy-start.6 = (bf16[2,896,1792]{2,1,0:T(8,128)(2,1)}, bf16[2,896,1792]{2,1,0:T(8,128)(2,1)S(1)}, u32[]{:S(2)}) copy-start(bf16[2,896,1792]{2,1,0:T(8,128)(2,1)S(1)} %get-tuple-element.14.w_ref) | copy-start | bytes 19267588
  20.4 22.5 %copy-start.4 = (bf16[64,1792]{1,0:T(8,128)(2,1)S(1)}, bf16[64,1792]{1,0:T(8,128)(2,1)}, u32[]{:S(2)}) copy-start(bf16[64,1792]{1,0:T(8,128)(2,1)} %residual_ref.1) | copy-start | bytes 688132
  20.4 22.5 %copy-start.5 = (f32[2,1792]{1,0:T(2,128)S(1)}, f32[2,1792]{1,0:T(2,128)}, u32[]{:S(2)}) copy-start(f32[2,1792]{1,0:T(2,128)} %modulation_ref.1) | copy-start | bytes 43012
  20.4 6.7 %collective-permute-start.1 = (f32[64,1024]{1,0:T(8,128)S(1)}, f32[64,1024]{1,0:T(8,128)S(1)}, u32[]{:S(2)}, u32[]{:S(2)}) collective-permute-start(f32[64,1024]{1,0:T(8,128)S(1)} %get-tuple-element.12), channel_id=1, source_target_pairs={{0,1},{1,0},{2,3},{3,2},{4,5},{5,4},{6,7},{7,6},{8,9},{9,8},{10,11... | collective-permute-start | bytes 786440 | tf_op jit(solution)/shard_map/ppermute | solution.py:238
  27.0 15.9 %copy-start.7 = (bf16[2,896,1792]{2,1,0:T(8,128)(2,1)S(1)}, bf16[2,896,1792]{2,1,0:T(8,128)(2,1)}, u32[]{:S(2)}) copy-start(bf16[2,896,1792]{2,1,0:T(8,128)(2,1)} %copy-done.6) | copy-start | bytes 19267588
  42.9 29.8 %slice-start = ((s8[12845056]{0:T(1024)(128)(4,1)}), s8[4194304]{0:T(1024)(128)(4,1)S(1)}, s32[]{:S(2)}) async-start(s8[12845056]{0:T(1024)(128)(4,1)} %bitcast.6), calls=%async_computation.4 | async-start | bytes 8388608
  42.9 29.8 %slice-start.4 = ((s8[12845056]{0:T(1024)(128)(4,1)}), s8[4194304]{0:T(1024)(128)(4,1)S(1)}, s32[]{:S(2)}) async-start(s8[12845056]{0:T(1024)(128)(4,1)} %bitcast.8), calls=%async_computation.8 | async-start | bytes 8388608
  42.9 29.8 %slice-start.1 = ((s8[12845056]{0:T(1024)(128)(4,1)}), s8[4194304]{0:T(1024)(128)(4,1)S(1)}, s32[]{:S(2)}) async-start(s8[12845056]{0:T(1024)(128)(4,1)} %bitcast.6), calls=%async_computation.5 | async-start | bytes 8388608
  42.9 29.8 %slice-start.2 = ((s8[12845056]{0:T(1024)(128)(4,1)}), s8[4194304]{0:T(1024)(128)(4,1)S(1)}, s32[]{:S(2)}) async-start(s8[12845056]{0:T(1024)(128)(4,1)} %bitcast.6), calls=%async_computation.6 | async-start | bytes 8388608
  43.0 29.8 %slice-start.3 = ((s8[12845056]{0:T(1024)(128)(4,1)}), s8[262144]{0:T(1024)(128)(4,1)S(1)}, s32[]{:S(2)}) async-start(s8[12845056]{0:T(1024)(128)(4,1)} %bitcast.6), calls=%async_computation.7 | async-start | bytes 524288
  43.0 29.8 %slice-start.5 = ((s8[12845056]{0:T(1024)(128)(4,1)}), s8[4194304]{0:T(1024)(128)(4,1)S(1)}, s32[]{:S(2)}) async-start(s8[12845056]{0:T(1024)(128)(4,1)} %bitcast.8), calls=%async_computation.9 | async-start | bytes 8388608
  43.0 29.8 %slice-start.6 = ((s8[12845056]{0:T(1024)(128)(4,1)}), s8[4194304]{0:T(1024)(128)(4,1)S(1)}, s32[]{:S(2)}) async-start(s8[12845056]{0:T(1024)(128)(4,1)} %bitcast.8), calls=%async_computation.10 | async-start | bytes 8388608
  43.0 29.8 %slice-start.7 = ((s8[12845056]{0:T(1024)(128)(4,1)}), s8[262144]{0:T(1024)(128)(4,1)S(1)}, s32[]{:S(2)}) async-start(s8[12845056]{0:T(1024)(128)(4,1)} %bitcast.8), calls=%async_computation.11 | async-start | bytes 524288

commit v10 on v9

--- a/solution.py
+++ b/solution.py
@@ -80,7 +80,8 @@
     for h in range(q.shape[0] // HEAD_DIM):
         rows = slice(h * HEAD_DIM, (h + 1) * HEAD_DIM)
         sums, top = partial_softmax(q[rows], k[rows], v[rows])
-        sums = jnp.where(lane == HEAD_DIM + 1, top, sums)
+        total = sums[:, HEAD_DIM : HEAD_DIM + 1]
+        sums = jnp.where(lane == HEAD_DIM, top + jnp.log(total), sums * (1.0 / total))
         lanes = slice(h * LANES, (h + 1) * LANES)
         own_ref[:, lanes] = jnp.where(first, sums[:half], sums[half:])
         other_ref[:, lanes] = jnp.where(first, sums[half:], sums[:half])
@@ -174,13 +175,9 @@
                 + far[:, HEAD_DIM + 1 : HEAD_DIM + 2]
                 + far[:, HEAD_DIM + 2 : HEAD_DIM + 3]
             )
-            near_total = near[:, HEAD_DIM : HEAD_DIM + 1]
-            near_top = near[:, HEAD_DIM + 1 : HEAD_DIM + 2]
-            top = jnp.maximum(far_log, near_top)
-            far_weight = jnp.exp(far_log - top)
-            near_weight = jnp.exp(near_top - top)
-            scale = 1.0 / (far_weight + near_total * near_weight)
-            merged = far * (far_weight * scale) + near * (near_weight * scale)
+            near_log = near[:, HEAD_DIM : HEAD_DIM + 1]
+            near_share = 1.0 / (1.0 + jnp.exp(jnp.minimum(far_log - near_log, 80.0)))
+            merged = far + (near - far) * near_share
             attended_ref[side, :, h * HEAD_DIM : (h + 1) * HEAD_DIM] = merged[:, :HEAD_DIM].astype(BF16)
     for side in range(2):
         part = jnp.dot(attended_ref[side], w_ref[side], preferred_element_type=F32)

time: 108 us -> 107 us (level)
  waiting for transfers between devices: 6.37 us -> 5.21 us
    all_to_all x1, waiting for transfers between devices: 6.36 us -> 5.2 us  [attention_by_heads(): lax.all_to_all(packed, 'patch', split_axis=0, concat_axis=0, tiled=True)]
    pallas_call x1, Pallas kernels: 2.3 us -> 3.46 us  [attention_by_heads(): pl.pallas_call(fresh_kernel, out_shape=(fresh_shape, fresh_shape, jax.Sha...]
  transfers between devices with their start and end apart: 3 -> 3, of which waited for: 1 -> 1; matrix products, arithmetic and copies ran while one was open for 1% -> 1% of each run, Pallas kernels for 4% -> 5%
where the time goes in v10:
time: 107 us
  blocking collectives  67.5 us (63%)
  Pallas kernels  17.6 us (16%)
  local copies, waits for them, and re-layouts  8.96 us (8%)
  starting transfers between devices  7.35 us (7%)
  waiting for transfers between devices  5.21 us (5%)
    all_to_all x1, blocking collectives, body(): lax.all_to_all(outputs.reshape(device_count, capacity, features), ('patch...  26.7 us
    all_to_all x1, blocking collectives, body(): lax.all_to_all(outgoing, ('patch', 'expert'), split_axis=0, concat_axis=0...  26.6 us
    all_to_all x1, blocking collectives, attention_by_heads(): lax.all_to_all(stale, ('patch', 'expert'), split_axis=0, concat_axis=0, t...  14.2 us
    unnamed x34, local copies, waits for them, and re-layouts  8.96 us
    all_to_all x1, starting transfers between devices, attention_by_heads(): lax.all_to_all(packed, 'patch', split_axis=0, concat_axis=0, tiled=True)  7.01 us
    pallas_call x1, Pallas kernels, expert_slice(): pl.pallas_call(expert_kernel, out_shape=jax.ShapeDtypeStruct((rows, featu...  6.94 us
    all_to_all x1, waiting for transfers between devices, attention_by_heads(): lax.all_to_all(packed, 'patch', split_axis=0, concat_axis=0, tiled=True)  5.2 us
    pallas_call x1, Pallas kernels, attention_by_heads(): pl.pallas_call(fresh_kernel, out_shape=(fresh_shape, fresh_shape, jax.Sha...  3.46 us
  transfers between devices with their start and end apart: 3, of which 1 were waited for; matrix products, arithmetic and copies ran while one was open for 1% of the time, Pallas kernels for 5%

profile of v10, /device:TPU:1, one launch (start us, length us, event | category | flops | bytes accessed | tf_op | source)
XLA Modules:
  0.0 106.8 jit_solution(16947660257913166948)
XLA Ops:
  0.0 0.1 collective-permute-start
  0.1 2.1 %pack.1 = bf16[8,336,128]{2,1,0:T(8,128)(2,1)} custom-call(bf16[128,896]{1,0:T(8,128)(2,1)} %q_ref.3, bf16[128,896]{1,0:T(8,128)(2,1)} %k_ref.2, bf16[128,896]{1,0:T(8,128)(2,1)} %v_ref.2), custom_call_target="tpu_custom_call" | custom-call | tf_op jit(solution)/shard_map/pack/pallas_call | solution.py:201
  2.1 7.0 %all-to-all-start = ((bf16[8,336,128]{2,1,0:T(8,128)(2,1)}), bf16[8,336,128]{2,1,0:T(8,128)(2,1)S(1)}, u32[]{:S(2)}, u32[]{:S(2)}) async-start(bf16[8,336,128]{2,1,0:T(8,128)(2,1)} %pack.1), calls=%async_computation | async-start | bytes 1376256 | tf_op jit(solution)/shard_map/all_to_all | solution.py:216
  9.1 0.8 copy.13.routes_ref
  9.9 0.8 copy.14.gates_ref
  10.7 0.0 collective-permute-done.w_other_ref
  10.7 0.0 copy-start
  10.7 0.9 copy-done
  11.6 0.0 copy-start.1
  11.6 1.9 %copy-done.1 = bf16[896,1792]{1,0:T(8,128)(2,1)S(1)} copy-done((bf16[896,1792]{1,0:T(8,128)(2,1)S(1)}, bf16[896,1792]{1,0:T(8,128)(2,1)}, u32[]{:S(2)}) %copy-start.1) | copy-done | bytes 3211288
  13.5 0.0 copy-start.2
  13.5 0.9 copy-done.2
  14.5 0.0 copy-start.3
  14.5 0.9 copy-done.3
  15.4 3.5 %fresh.1 = (f32[64,1024]{1,0:T(8,128)S(1)}, f32[64,1024]{1,0:T(8,128)S(1)}, bf16[2,64,256]{2,1,0:T(8,128)(2,1)S(1)}, f32[64,2]{1,0:T(8,128)S(1)}, bf16[2,896,1792]{2,1,0:T(8,128)(2,1)S(1)}) custom-call(s32[1]{0:T(128)} %bitcast.core_ref, bf16[128,896]{1,0:T(8,128)(2,1)S(1)} %copy-done, bf16[128,896]{1,0:T(8,128)(2,1)S(1)} %copy-done.2, ...), custom_call_target="tpu_custom_call" | custom-call | flops 5000000000 | bytes 2000000 | tf_op jit(solution)/shard_map/fresh/pallas_call | solution.py:219
  18.9 0.0 copy-start.6
  18.9 2.7 %copy-done.6 = bf16[2,896,1792]{2,1,0:T(8,128)(2,1)} copy-done((bf16[2,896,1792]{2,1,0:T(8,128)(2,1)}, bf16[2,896,1792]{2,1,0:T(8,128)(2,1)S(1)}, u32[]{:S(2)}) %copy-start.6) | copy-done | bytes 6422552
  21.5 0.0 copy-start.4
  21.5 0.0 copy-start.5
  21.5 0.3 collective-permute-start.1
  21.8 5.2 %all-to-all-done.in_ref = bf16[8,336,128]{2,1,0:T(8,128)(2,1)S(1)} async-done(((bf16[8,336,128]{2,1,0:T(8,128)(2,1)}), bf16[8,336,128]{2,1,0:T(8,128)(2,1)S(1)}, u32[]{:S(2)}, u32[]{:S(2)}) %all-to-all-start) | async-done | bytes 688160 | tf_op jit(solution)/shard_map/all_to_all | solution.py:216
  27.0 0.0 copy-start.7
  27.0 0.0 collective-permute-done.1.fresh_ref.other_ref
  27.0 1.7 %attend.1 = bf16[16,64,128]{2,1,0:T(8,128)(2,1)S(1)} custom-call(bf16[8,336,128]{2,1,0:T(8,128)(2,1)S(1)} %all-to-all-done.in_ref, f32[64,1024]{1,0:T(8,128)S(1)} %collective-permute-done.1.fresh_ref.other_ref), custom_call_target="tpu_custom_call" | custom-call | flops 99999997952 | bytes 2000000 | tf_op jit(solution)/shard_map/attend/pallas_call | solution.py:236
  28.7 14.2 %all_to_all.20 = bf16[16,64,128]{2,1,0:T(8,128)(2,1)S(1)} all-to-all(bf16[16,64,128]{2,1,0:T(8,128)(2,1)S(1)} %attend.1), channel_id=1, replica_groups=mesh['group'=2,'patch'=8,'expert'=2] {'patch','expert'}, dimensions={0} | all-to-all | bytes 524288 | tf_op jit(solution)/shard_map/all_to_all | solution.py:245
  42.9 0.0 slice-start
  42.9 0.0 slice-start.4
  42.9 0.0 copy-done.4
  42.9 0.0 copy-done.5
  42.9 0.0 copy-done.7
  42.9 0.0 slice-start.1
  42.9 0.0 slice-start.2
  43.0 0.0 slice-start.3
  43.0 0.0 slice-start.5
  43.0 0.0 slice-start.6
  43.0 0.0 slice-start.7
  43.0 2.3 %home.1 = (f32[64,1792]{1,0:T(8,128)S(1)}, bf16[256,1792]{1,0:T(8,128)(2,1)S(1)}) custom-call(s32[1]{0:T(128)} %bitcast.core_ref, bf16[8,2,64,128]{3,2,1,0:T(8,128)(2,1)S(1)} %bitcast.14, f32[64,1024]{1,0:T(8,128)S(1)} %get-tuple-element.13.own_ref, f32[64,1024]{1,0:T(8,128)S(1)} %collective-permute-done.1.fresh_ref.other_ref, ...), custom_call_target="tpu_custom_call" | custom-call | flops 99999997952 | bytes 8000000 | tf_op jit(solution)/shard_map/home/pallas_call | solution.py:246
  45.3 26.6 %all_to_all.21 = bf16[16,16,1792]{2,1,0:T(8,128)(2,1)S(1)} all-to-all(bf16[16,16,1792]{2,1,0:T(8,128)(2,1)S(1)} %bitcast.13), channel_id=1, replica_groups=mesh['group'=2,'patch'=8,'expert'=2] {'patch','expert'}, dimensions={0} | all-to-all | bytes 1835008 | tf_op jit(solution)/shard_map/all_to_all | solution.py:368
  71.9 0.0 slice-done
  71.9 0.0 slice-done.4
  71.9 0.0 slice-done.1
  71.9 0.0 slice-done.2
  71.9 0.0 slice-done.3
  71.9 0.0 slice-done.5
  71.9 0.0 slice-done.6
  72.0 0.0 slice-done.7
  72.0 6.9 %experts.1 = bf16[256,1792]{1,0:T(8,128)(2,1)S(1)} custom-call(bf16[256,1792]{1,0:T(8,128)(2,1)S(1)} %bitcast.11, bf16[1,1792,3584]{2,1,0:T(8,128)(2,1)S(1)} %bitcast.7, bf16[1,3584,1792]{2,1,0:T(8,128)(2,1)S(1)} %bitcast.9), custom_call_target="tpu_custom_call" | custom-call | tf_op jit(solution)/shard_map/experts/pallas_call | solution.py:329
  78.9 26.7 %all_to_all.22 = bf16[16,16,1792]{2,1,0:T(8,128)(2,1)S(1)} all-to-all(bf16[16,16,1792]{2,1,0:T(8,128)(2,1)S(1)} %bitcast.12), channel_id=1, replica_groups=mesh['group'=2,'patch'=8,'expert'=2] {'patch','expert'}, dimensions={0} | all-to-all | bytes 1835008 | tf_op jit(solution)/shard_map/all_to_all | solution.py:370
  105.7 1.1 %combine.1 = bf16[64,1792]{1,0:T(8,128)(2,1)} custom-call(f32[64,1792]{1,0:T(8,128)S(1)} %get-tuple-element.16.hidden_ref, bf16[2,64,256]{2,1,0:T(8,128)(2,1)S(1)} %get-tuple-element.15.picks_ref, f32[64,2]{1,0:T(8,128)S(1)} %get-tuple-element.17.gates_ref, bf16[16,1,16,1792]{3,2,1,0:T(8,128)(2,1)S(1)} %bitcast.10), custom_call_target="tpu_custom_call" | custom-call | tf_op jit(solution)/shard_map/combine/pallas_call | solution.py:377
  (2 shorter events, 0.0 us)
Async XLA Ops:
  0.0 10.7 %collective-permute-start = (bf16[896,1792]{1,0:T(8,128)(2,1)}, bf16[896,1792]{1,0:T(8,128)(2,1)}, u32[]{:S(2)}, u32[]{:S(2)}) collective-permute-start(bf16[896,1792]{1,0:T(8,128)(2,1)} %w_own_ref.1), channel_id=1, source_target_pairs={{0,1},{1,0},{2,3},{3,2},{4,5},{5,4},{6,7},{7,6},{8,9},{9,8},{10,11... | collective-permute-start | bytes 9633800 | tf_op jit(solution)/shard_map/ppermute | solution.py:215
  2.1 24.9 %all-to-all-start = ((bf16[8,336,128]{2,1,0:T(8,128)(2,1)}), bf16[8,336,128]{2,1,0:T(8,128)(2,1)S(1)}, u32[]{:S(2)}, u32[]{:S(2)}) async-start(bf16[8,336,128]{2,1,0:T(8,128)(2,1)} %pack.1), calls=%async_computation | async-start | bytes 1376256 | tf_op jit(solution)/shard_map/all_to_all | solution.py:216
  10.7 0.9 copy-start
  11.6 1.9 %copy-start.1 = (bf16[896,1792]{1,0:T(8,128)(2,1)S(1)}, bf16[896,1792]{1,0:T(8,128)(2,1)}, u32[]{:S(2)}) copy-start(bf16[896,1792]{1,0:T(8,128)(2,1)} %w_own_ref.1) | copy-start | bytes 9633796
  13.5 0.9 copy-start.2
  14.5 0.9 copy-start.3
  18.9 2.7 %copy-start.6 = (bf16[2,896,1792]{2,1,0:T(8,128)(2,1)}, bf16[2,896,1792]{2,1,0:T(8,128)(2,1)S(1)}, u32[]{:S(2)}) copy-start(bf16[2,896,1792]{2,1,0:T(8,128)(2,1)S(1)} %get-tuple-element.14.w_ref) | copy-start | bytes 19267588
  21.5 21.4 %copy-start.4 = (bf16[64,1792]{1,0:T(8,128)(2,1)S(1)}, bf16[64,1792]{1,0:T(8,128)(2,1)}, u32[]{:S(2)}) copy-start(bf16[64,1792]{1,0:T(8,128)(2,1)} %residual_ref.1) | copy-start | bytes 688132
  21.5 21.4 %copy-start.5 = (f32[2,1792]{1,0:T(2,128)S(1)}, f32[2,1792]{1,0:T(2,128)}, u32[]{:S(2)}) copy-start(f32[2,1792]{1,0:T(2,128)} %modulation_ref.1) | copy-start | bytes 43012
  21.5 5.5 %collective-permute-start.1 = (f32[64,1024]{1,0:T(8,128)S(1)}, f32[64,1024]{1,0:T(8,128)S(1)}, u32[]{:S(2)}, u32[]{:S(2)}) collective-permute-start(f32[64,1024]{1,0:T(8,128)S(1)} %get-tuple-element.12), channel_id=1, source_target_pairs={{0,1},{1,0},{2,3},{3,2},{4,5},{5,4},{6,7},{7,6},{8,9},{9,8},{10,11... | collective-permute-start | bytes 786440 | tf_op jit(solution)/shard_map/ppermute | solution.py:235
  27.0 15.9 %copy-start.7 = (bf16[2,896,1792]{2,1,0:T(8,128)(2,1)S(1)}, bf16[2,896,1792]{2,1,0:T(8,128)(2,1)}, u32[]{:S(2)}) copy-start(bf16[2,896,1792]{2,1,0:T(8,128)(2,1)} %copy-done.6) | copy-start | bytes 19267588
  42.9 29.0 %slice-start = ((s8[12845056]{0:T(1024)(128)(4,1)}), s8[4194304]{0:T(1024)(128)(4,1)S(1)}, s32[]{:S(2)}) async-start(s8[12845056]{0:T(1024)(128)(4,1)} %bitcast.6), calls=%async_computation.4 | async-start | bytes 8388608
  42.9 29.0 %slice-start.4 = ((s8[12845056]{0:T(1024)(128)(4,1)}), s8[4194304]{0:T(1024)(128)(4,1)S(1)}, s32[]{:S(2)}) async-start(s8[12845056]{0:T(1024)(128)(4,1)} %bitcast.8), calls=%async_computation.8 | async-start | bytes 8388608
  42.9 29.0 %slice-start.1 = ((s8[12845056]{0:T(1024)(128)(4,1)}), s8[4194304]{0:T(1024)(128)(4,1)S(1)}, s32[]{:S(2)}) async-start(s8[12845056]{0:T(1024)(128)(4,1)} %bitcast.6), calls=%async_computation.5 | async-start | bytes 8388608
  42.9 29.0 %slice-start.2 = ((s8[12845056]{0:T(1024)(128)(4,1)}), s8[4194304]{0:T(1024)(128)(4,1)S(1)}, s32[]{:S(2)}) async-start(s8[12845056]{0:T(1024)(128)(4,1)} %bitcast.6), calls=%async_computation.6 | async-start | bytes 8388608
  43.0 29.0 %slice-start.3 = ((s8[12845056]{0:T(1024)(128)(4,1)}), s8[262144]{0:T(1024)(128)(4,1)S(1)}, s32[]{:S(2)}) async-start(s8[12845056]{0:T(1024)(128)(4,1)} %bitcast.6), calls=%async_computation.7 | async-start | bytes 524288
  43.0 29.0 %slice-start.5 = ((s8[12845056]{0:T(1024)(128)(4,1)}), s8[4194304]{0:T(1024)(128)(4,1)S(1)}, s32[]{:S(2)}) async-start(s8[12845056]{0:T(1024)(128)(4,1)} %bitcast.8), calls=%async_computation.9 | async-start | bytes 8388608
  43.0 29.0 %slice-start.6 = ((s8[12845056]{0:T(1024)(128)(4,1)}), s8[4194304]{0:T(1024)(128)(4,1)S(1)}, s32[]{:S(2)}) async-start(s8[12845056]{0:T(1024)(128)(4,1)} %bitcast.8), calls=%async_computation.10 | async-start | bytes 8388608
  43.0 29.0 %slice-start.7 = ((s8[12845056]{0:T(1024)(128)(4,1)}), s8[262144]{0:T(1024)(128)(4,1)S(1)}, s32[]{:S(2)}) async-start(s8[12845056]{0:T(1024)(128)(4,1)} %bitcast.8), calls=%async_computation.11 | async-start | bytes 524288

commit v11 on v10

--- a/solution.py
+++ b/solution.py
@@ -343,8 +343,9 @@
     mixed = hidden_ref[...]
     for s in range(slices):
         rows = returned_ref[:, s].reshape(slots, returned_ref.shape[3])
+        picked = jnp.dot(picks_ref[...].reshape(-1, slots), rows, preferred_element_type=F32)
         for k in range(TOPK):
-            mixed += gates_ref[:, k : k + 1] * jnp.dot(picks_ref[k], rows, preferred_element_type=F32)
+            mixed += gates_ref[:, k : k + 1] * picked[k * mixed.shape[0] : (k + 1) * mixed.shape[0]]
     out_ref[...] = mixed.astype(BF16)
 
 

time: 107 us -> 107 us (level)
  no operation moved by 1% of the time
where the time goes in v11:
time: 107 us
  blocking collectives  67.5 us (63%)
  Pallas kernels  17.5 us (16%)
  local copies, waits for them, and re-layouts  8.96 us (8%)
  starting transfers between devices  7.35 us (7%)
  waiting for transfers between devices  5.21 us (5%)
    all_to_all x1, blocking collectives, body(): lax.all_to_all(outputs.reshape(device_count, capacity, features), ('patch...  26.7 us
    all_to_all x1, blocking collectives, body(): lax.all_to_all(outgoing, ('patch', 'expert'), split_axis=0, concat_axis=0...  26.6 us
    all_to_all x1, blocking collectives, attention_by_heads(): lax.all_to_all(stale, ('patch', 'expert'), split_axis=0, concat_axis=0, t...  14.2 us
    unnamed x34, local copies, waits for them, and re-layouts  8.96 us
    all_to_all x1, starting transfers between devices, attention_by_heads(): lax.all_to_all(packed, 'patch', split_axis=0, concat_axis=0, tiled=True)  7.01 us
    pallas_call x1, Pallas kernels, expert_slice(): pl.pallas_call(expert_kernel, out_shape=jax.ShapeDtypeStruct((rows, featu...  6.94 us
    all_to_all x1, waiting for transfers between devices, attention_by_heads(): lax.all_to_all(packed, 'patch', split_axis=0, concat_axis=0, tiled=True)  5.2 us
    pallas_call x1, Pallas kernels, attention_by_heads(): pl.pallas_call(fresh_kernel, out_shape=(fresh_shape, fresh_shape, jax.Sha...  3.46 us
  transfers between devices with their start and end apart: 3, of which 1 were waited for; matrix products, arithmetic and copies ran while one was open for 1% of the time, Pallas kernels for 5%

profile of v11, /device:TPU:1, one launch (start us, length us, event | category | flops | bytes accessed | tf_op | source)
XLA Modules:
  0.0 106.7 jit_solution(502131231859132991)
XLA Ops:
  0.0 0.1 collective-permute-start
  0.1 2.1 %pack.1 = bf16[8,336,128]{2,1,0:T(8,128)(2,1)} custom-call(bf16[128,896]{1,0:T(8,128)(2,1)} %q_ref.3, bf16[128,896]{1,0:T(8,128)(2,1)} %k_ref.2, bf16[128,896]{1,0:T(8,128)(2,1)} %v_ref.2), custom_call_target="tpu_custom_call" | custom-call | tf_op jit(solution)/shard_map/pack/pallas_call | solution.py:201
  2.1 7.0 %all-to-all-start = ((bf16[8,336,128]{2,1,0:T(8,128)(2,1)}), bf16[8,336,128]{2,1,0:T(8,128)(2,1)S(1)}, u32[]{:S(2)}, u32[]{:S(2)}) async-start(bf16[8,336,128]{2,1,0:T(8,128)(2,1)} %pack.1), calls=%async_computation | async-start | bytes 1376256 | tf_op jit(solution)/shard_map/all_to_all | solution.py:216
  9.1 0.8 copy.13.routes_ref
  9.9 0.8 copy.14.gates_ref
  10.7 0.0 collective-permute-done.w_other_ref
  10.7 0.0 copy-start
  10.7 0.9 copy-done
  11.6 0.0 copy-start.1
  11.6 1.9 %copy-done.1 = bf16[896,1792]{1,0:T(8,128)(2,1)S(1)} copy-done((bf16[896,1792]{1,0:T(8,128)(2,1)S(1)}, bf16[896,1792]{1,0:T(8,128)(2,1)}, u32[]{:S(2)}) %copy-start.1) | copy-done | bytes 3211288
  13.5 0.0 copy-start.2
  13.5 0.9 copy-done.2
  14.5 0.0 copy-start.3
  14.5 0.9 copy-done.3
  15.4 3.5 %fresh.1 = (f32[64,1024]{1,0:T(8,128)S(1)}, f32[64,1024]{1,0:T(8,128)S(1)}, bf16[2,64,256]{2,1,0:T(8,128)(2,1)S(1)}, f32[64,2]{1,0:T(8,128)S(1)}, bf16[2,896,1792]{2,1,0:T(8,128)(2,1)S(1)}) custom-call(s32[1]{0:T(128)} %bitcast.core_ref, bf16[128,896]{1,0:T(8,128)(2,1)S(1)} %copy-done, bf16[128,896]{1,0:T(8,128)(2,1)S(1)} %copy-done.2, ...), custom_call_target="tpu_custom_call" | custom-call | flops 5000000000 | bytes 2000000 | tf_op jit(solution)/shard_map/fresh/pallas_call | solution.py:219
  18.9 0.0 copy-start.6
  18.9 2.7 %copy-done.6 = bf16[2,896,1792]{2,1,0:T(8,128)(2,1)} copy-done((bf16[2,896,1792]{2,1,0:T(8,128)(2,1)}, bf16[2,896,1792]{2,1,0:T(8,128)(2,1)S(1)}, u32[]{:S(2)}) %copy-start.6) | copy-done | bytes 6422552
  21.5 0.0 copy-start.4
  21.5 0.0 copy-start.5
  21.5 0.3 collective-permute-start.1
  21.8 5.2 %all-to-all-done.in_ref = bf16[8,336,128]{2,1,0:T(8,128)(2,1)S(1)} async-done(((bf16[8,336,128]{2,1,0:T(8,128)(2,1)}), bf16[8,336,128]{2,1,0:T(8,128)(2,1)S(1)}, u32[]{:S(2)}, u32[]{:S(2)}) %all-to-all-start) | async-done | bytes 688160 | tf_op jit(solution)/shard_map/all_to_all | solution.py:216
  27.0 0.0 copy-start.7
  27.0 0.0 collective-permute-done.1.fresh_ref.other_ref
  27.0 1.7 %attend.1 = bf16[16,64,128]{2,1,0:T(8,128)(2,1)S(1)} custom-call(bf16[8,336,128]{2,1,0:T(8,128)(2,1)S(1)} %all-to-all-done.in_ref, f32[64,1024]{1,0:T(8,128)S(1)} %collective-permute-done.1.fresh_ref.other_ref), custom_call_target="tpu_custom_call" | custom-call | flops 99999997952 | bytes 2000000 | tf_op jit(solution)/shard_map/attend/pallas_call | solution.py:236
  28.7 14.2 %all_to_all.20 = bf16[16,64,128]{2,1,0:T(8,128)(2,1)S(1)} all-to-all(bf16[16,64,128]{2,1,0:T(8,128)(2,1)S(1)} %attend.1), channel_id=1, replica_groups=mesh['group'=2,'patch'=8,'expert'=2] {'patch','expert'}, dimensions={0} | all-to-all | bytes 524288 | tf_op jit(solution)/shard_map/all_to_all | solution.py:245
  42.9 0.0 slice-start
  42.9 0.0 slice-start.4
  42.9 0.0 copy-done.4
  42.9 0.0 copy-done.5
  42.9 0.0 copy-done.7
  42.9 0.0 slice-start.1
  42.9 0.0 slice-start.2
  43.0 0.0 slice-start.3
  43.0 0.0 slice-start.5
  43.0 0.0 slice-start.6
  43.0 0.0 slice-start.7
  43.0 2.3 %home.1 = (f32[64,1792]{1,0:T(8,128)S(1)}, bf16[256,1792]{1,0:T(8,128)(2,1)S(1)}) custom-call(s32[1]{0:T(128)} %bitcast.core_ref, bf16[8,2,64,128]{3,2,1,0:T(8,128)(2,1)S(1)} %bitcast.14, f32[64,1024]{1,0:T(8,128)S(1)} %get-tuple-element.13.own_ref, f32[64,1024]{1,0:T(8,128)S(1)} %collective-permute-done.1.fresh_ref.other_ref, ...), custom_call_target="tpu_custom_call" | custom-call | flops 99999997952 | bytes 8000000 | tf_op jit(solution)/shard_map/home/pallas_call | solution.py:246
  45.3 26.6 %all_to_all.21 = bf16[16,16,1792]{2,1,0:T(8,128)(2,1)S(1)} all-to-all(bf16[16,16,1792]{2,1,0:T(8,128)(2,1)S(1)} %bitcast.13), channel_id=1, replica_groups=mesh['group'=2,'patch'=8,'expert'=2] {'patch','expert'}, dimensions={0} | all-to-all | bytes 1835008 | tf_op jit(solution)/shard_map/all_to_all | solution.py:369
  71.9 0.0 slice-done
  71.9 0.0 slice-done.4
  71.9 0.0 slice-done.1
  71.9 0.0 slice-done.2
  71.9 0.0 slice-done.3
  71.9 0.0 slice-done.5
  71.9 0.0 slice-done.6
  72.0 0.0 slice-done.7
  72.0 6.9 %experts.1 = bf16[256,1792]{1,0:T(8,128)(2,1)S(1)} custom-call(bf16[256,1792]{1,0:T(8,128)(2,1)S(1)} %bitcast.11, bf16[1,1792,3584]{2,1,0:T(8,128)(2,1)S(1)} %bitcast.7, bf16[1,3584,1792]{2,1,0:T(8,128)(2,1)S(1)} %bitcast.9), custom_call_target="tpu_custom_call" | custom-call | tf_op jit(solution)/shard_map/experts/pallas_call | solution.py:329
  78.9 26.7 %all_to_all.22 = bf16[16,16,1792]{2,1,0:T(8,128)(2,1)S(1)} all-to-all(bf16[16,16,1792]{2,1,0:T(8,128)(2,1)S(1)} %bitcast.12), channel_id=1, replica_groups=mesh['group'=2,'patch'=8,'expert'=2] {'patch','expert'}, dimensions={0} | all-to-all | bytes 1835008 | tf_op jit(solution)/shard_map/all_to_all | solution.py:371
  105.7 1.0 combine.1
  (2 shorter events, 0.0 us)
Async XLA Ops:
  0.0 10.7 %collective-permute-start = (bf16[896,1792]{1,0:T(8,128)(2,1)}, bf16[896,1792]{1,0:T(8,128)(2,1)}, u32[]{:S(2)}, u32[]{:S(2)}) collective-permute-start(bf16[896,1792]{1,0:T(8,128)(2,1)} %w_own_ref.1), channel_id=1, source_target_pairs={{0,1},{1,0},{2,3},{3,2},{4,5},{5,4},{6,7},{7,6},{8,9},{9,8},{10,11... | collective-permute-start | bytes 9633800 | tf_op jit(solution)/shard_map/ppermute | solution.py:215
  2.1 24.9 %all-to-all-start = ((bf16[8,336,128]{2,1,0:T(8,128)(2,1)}), bf16[8,336,128]{2,1,0:T(8,128)(2,1)S(1)}, u32[]{:S(2)}, u32[]{:S(2)}) async-start(bf16[8,336,128]{2,1,0:T(8,128)(2,1)} %pack.1), calls=%async_computation | async-start | bytes 1376256 | tf_op jit(solution)/shard_map/all_to_all | solution.py:216
  10.7 0.9 copy-start
  11.6 1.9 %copy-start.1 = (bf16[896,1792]{1,0:T(8,128)(2,1)S(1)}, bf16[896,1792]{1,0:T(8,128)(2,1)}, u32[]{:S(2)}) copy-start(bf16[896,1792]{1,0:T(8,128)(2,1)} %w_own_ref.1) | copy-start | bytes 9633796
  13.5 0.9 copy-start.2
  14.5 0.9 copy-start.3
  18.9 2.7 %copy-start.6 = (bf16[2,896,1792]{2,1,0:T(8,128)(2,1)}, bf16[2,896,1792]{2,1,0:T(8,128)(2,1)S(1)}, u32[]{:S(2)}) copy-start(bf16[2,896,1792]{2,1,0:T(8,128)(2,1)S(1)} %get-tuple-element.14.w_ref) | copy-start | bytes 19267588
  21.5 21.4 %copy-start.4 = (bf16[64,1792]{1,0:T(8,128)(2,1)S(1)}, bf16[64,1792]{1,0:T(8,128)(2,1)}, u32[]{:S(2)}) copy-start(bf16[64,1792]{1,0:T(8,128)(2,1)} %residual_ref.1) | copy-start | bytes 688132
  21.5 21.4 %copy-start.5 = (f32[2,1792]{1,0:T(2,128)S(1)}, f32[2,1792]{1,0:T(2,128)}, u32[]{:S(2)}) copy-start(f32[2,1792]{1,0:T(2,128)} %modulation_ref.1) | copy-start | bytes 43012
  21.5 5.5 %collective-permute-start.1 = (f32[64,1024]{1,0:T(8,128)S(1)}, f32[64,1024]{1,0:T(8,128)S(1)}, u32[]{:S(2)}, u32[]{:S(2)}) collective-permute-start(f32[64,1024]{1,0:T(8,128)S(1)} %get-tuple-element.12), channel_id=1, source_target_pairs={{0,1},{1,0},{2,3},{3,2},{4,5},{5,4},{6,7},{7,6},{8,9},{9,8},{10,11... | collective-permute-start | bytes 786440 | tf_op jit(solution)/shard_map/ppermute | solution.py:235
  27.0 15.9 %copy-start.7 = (bf16[2,896,1792]{2,1,0:T(8,128)(2,1)S(1)}, bf16[2,896,1792]{2,1,0:T(8,128)(2,1)}, u32[]{:S(2)}) copy-start(bf16[2,896,1792]{2,1,0:T(8,128)(2,1)} %copy-done.6) | copy-start | bytes 19267588
  42.9 29.0 %slice-start = ((s8[12845056]{0:T(1024)(128)(4,1)}), s8[4194304]{0:T(1024)(128)(4,1)S(1)}, s32[]{:S(2)}) async-start(s8[12845056]{0:T(1024)(128)(4,1)} %bitcast.6), calls=%async_computation.4 | async-start | bytes 8388608
  42.9 29.0 %slice-start.4 = ((s8[12845056]{0:T(1024)(128)(4,1)}), s8[4194304]{0:T(1024)(128)(4,1)S(1)}, s32[]{:S(2)}) async-start(s8[12845056]{0:T(1024)(128)(4,1)} %bitcast.8), calls=%async_computation.8 | async-start | bytes 8388608
  42.9 29.0 %slice-start.1 = ((s8[12845056]{0:T(1024)(128)(4,1)}), s8[4194304]{0:T(1024)(128)(4,1)S(1)}, s32[]{:S(2)}) async-start(s8[12845056]{0:T(1024)(128)(4,1)} %bitcast.6), calls=%async_computation.5 | async-start | bytes 8388608
  42.9 29.0 %slice-start.2 = ((s8[12845056]{0:T(1024)(128)(4,1)}), s8[4194304]{0:T(1024)(128)(4,1)S(1)}, s32[]{:S(2)}) async-start(s8[12845056]{0:T(1024)(128)(4,1)} %bitcast.6), calls=%async_computation.6 | async-start | bytes 8388608
  43.0 29.0 %slice-start.3 = ((s8[12845056]{0:T(1024)(128)(4,1)}), s8[262144]{0:T(1024)(128)(4,1)S(1)}, s32[]{:S(2)}) async-start(s8[12845056]{0:T(1024)(128)(4,1)} %bitcast.6), calls=%async_computation.7 | async-start | bytes 524288
  43.0 29.0 %slice-start.5 = ((s8[12845056]{0:T(1024)(128)(4,1)}), s8[4194304]{0:T(1024)(128)(4,1)S(1)}, s32[]{:S(2)}) async-start(s8[12845056]{0:T(1024)(128)(4,1)} %bitcast.8), calls=%async_computation.9 | async-start | bytes 8388608
  43.0 29.0 %slice-start.6 = ((s8[12845056]{0:T(1024)(128)(4,1)}), s8[4194304]{0:T(1024)(128)(4,1)S(1)}, s32[]{:S(2)}) async-start(s8[12845056]{0:T(1024)(128)(4,1)} %bitcast.8), calls=%async_computation.10 | async-start | bytes 8388608
  43.0 29.0 %slice-start.7 = ((s8[12845056]{0:T(1024)(128)(4,1)}), s8[262144]{0:T(1024)(128)(4,1)S(1)}, s32[]{:S(2)}) async-start(s8[12845056]{0:T(1024)(128)(4,1)} %bitcast.8), calls=%async_computation.11 | async-start | bytes 524288
